TPU v7x, 32 devices: a whole 2x2x4 slice. The times are simulated.
32 devices in a mesh: tm: 4 (over x, core), sensor: 8 (over z, y).
Axes of the slice: x: 2, y: 2, z: 4, core: 2. Of those that a mesh axis runs over, the one named last changes fastest.
Arguments:
- values: bfloat16 [65536, 256], P('sensor'), may hold values from -0.046875 to 0.046875
- blocks: int32 [65536, 2], P('sensor'), may hold values from 0 to 7, all different within a row
- noise_scale: float32 [4, 65536], P('tm', 'sensor'), may hold values from 0.5 to 2
- readings: float32 [4, 65536], P('tm', 'sensor'), may hold values from -6 to 6
- available: int32 [4, 65536], P('tm', 'sensor'), may hold values 0 or 1
- decay: float32 [4, 1024], P('tm'), may hold values from 0.7 to 1
- prior_factor: float32 [1024, 1024], replicated, may hold values from -3 to 3, as said below
- prior_target: float32 [1024], replicated, may hold values from -6 to 6
Outputs:
- factor_post: float32 [4, 1024, 1024], P('tm', 'sensor')
- estimate: float32 [4, 1024], P('tm')
Inputs may be any that keep to these rules, and one draw needn't show every extreme that they name: `prior_factor`: upper triangular; diagonal entries from 1 to 3, the other upper entries at most 3 / sqrt(1024) in size.
All inputs are finite; a program needn't handle non-finite values. No bound on the sum of `available` on one device may be relied on, other than what follows from the above.
Results may differ from a plain program's by a relative error of at most 0.0038.
Values sent between devices are 32-bit elements; how exact they have to be, the bound alone decides.
No kernel may reach another device: no remote copies, remote signals or barrier semaphores. Data moves between devices by JAX's collectives and lax.ppermute only.
A program may use at most 128 MiB of HBM per device.

v0:
```python
import jax
import jax.numpy as jnp
from jax import lax
from jax.sharding import PartitionSpec as P


def shifted(shard, axis, by):
    length = lax.axis_size(axis)
    pairs = [(i, i + by) for i in range(length) if 0 <= i + by < length]
    return lax.ppermute(shard, axis, pairs)


def expand(weighted, blocks, count):
    width = weighted.shape[1] // 2
    picked = (blocks[:, :, None] == jnp.arange(count, dtype=jnp.int32)[None, None, :]).astype(
        weighted.dtype
    )
    first = weighted[:, :width]
    second = weighted[:, width:]
    dense = picked[:, 0, :, None] * first[:, None, :] + picked[:, 1, :, None] * second[:, None, :]
    return dense.reshape(weighted.shape[0], count * width)


def measure(values, blocks, noise_row, reading_row, avail_row, count):
    factor = avail_row.astype(jnp.float32) / noise_row
    weighted = (values.astype(jnp.float32) * factor[:, None]).astype(jnp.bfloat16)
    target = (reading_row * factor).astype(jnp.bfloat16)
    dense = expand(weighted, blocks, count)
    gram_part = lax.dot_general(
        dense, dense, (((0,), (0,)), ((), ())), preferred_element_type=jnp.float32
    )
    vec_part = lax.dot_general(
        target, dense, (((0,), (0,)), ((), ())), preferred_element_type=jnp.float32
    )
    return (gram_part, vec_part)


def per_device(values, blocks, noise_scale, readings, available, decay, prior_factor, prior_target):
    width_full = prior_factor.shape[0]
    block_width = values.shape[1] // 2
    count = width_full // block_width
    sensor_count = lax.axis_size("sensor")
    share = width_full // sensor_count
    own_start = lax.axis_index("sensor") * share

    def row_part(vector):
        return lax.dynamic_slice_in_dim(vector, own_start, share, 0)

    step_index = 0
    gram_part, vec_part = measure(
        values, blocks, noise_scale[step_index], readings[step_index], available[step_index], count
    )
    gram_part, vec_part = (
        lax.psum_scatter(gram_part, "sensor", scatter_dimension=0, tiled=True),
        lax.psum_scatter(vec_part, "sensor", scatter_dimension=0, tiled=True),
    )
    grams = [gram_part]
    vectors = [vec_part]
    rate_all = jnp.ones((width_full,), jnp.float32)
    step_index = 0
    rate = decay[step_index]
    rate_rows = row_part(rate)
    rate_all = rate_all * rate
    shift_info = rate_rows[:, None] * grams[step_index] * rate[None, :]
    shift_vec = rate_rows * vectors[step_index]
    slab = lax.dynamic_slice_in_dim(prior_factor, own_start, share, 1)
    info_first = jnp.dot(
        slab.T, prior_factor, precision=lax.Precision.HIGHEST, preferred_element_type=jnp.float32
    )
    ivec_first = jnp.dot(
        prior_target, slab, precision=lax.Precision.HIGHEST, preferred_element_type=jnp.float32
    )
    time_index = lax.axis_index("tm")
    rows_all = row_part(rate_all)
    prior_info = info_first
    prior_vec = ivec_first
    for turn_index in range(lax.axis_size("tm") - 1):
        outgoing = (
            rows_all[:, None] * prior_info * rate_all[None, :] + shift_info,
            rows_all * prior_vec + shift_vec,
        )
        incoming = shifted((outgoing[0], outgoing[1]), "tm", 1)
        taking = time_index == turn_index + 1
        prior_info = jnp.where(taking, incoming[0], prior_info)
        prior_vec = jnp.where(taking, incoming[1], prior_vec)
    step_index = 0
    post = prior_info + grams[step_index]
    pvec = prior_vec + vectors[step_index]
    post_full = lax.all_gather(post, "sensor", axis=0, tiled=True)
    pvec_full = lax.all_gather(pvec, "sensor", axis=0, tiled=True)
    lower = jnp.linalg.cholesky(post_full)
    middle = lax.linalg.triangular_solve(lower, pvec_full[:, None], left_side=True, lower=True)
    solved = lax.linalg.triangular_solve(
        lower, middle, left_side=True, lower=True, transpose_a=True
    )
    factors = [lax.dynamic_slice_in_dim(lower, own_start, share, 1).T]
    estimates = [solved[:, 0]]
    return (jnp.stack(factors), jnp.stack(estimates))


def solution(mesh):
    placed = (
        P("sensor", None),
        P("sensor", None),
        P("tm", "sensor"),
        P("tm", "sensor"),
        P("tm", "sensor"),
        P("tm", None),
        P(),
        P(),
    )
    return jax.shard_map(
        per_device,
        mesh=mesh,
        in_specs=placed,
        out_specs=(P("tm", "sensor", None), P("tm", None)),
        check_vma=False,
    )
```

profile of v0, /device:TPU:0, one launch (start us, length us, event | category | flops | bytes accessed | tf_op | source)
XLA Modules:
  0.0 665.9 jit_solution(9948473029068317600)
XLA Ops:
  8.0 2.9 multiply_convert_fusion
  10.9 2.2 fusion.153
  16.0 63.5 %multiply_add_fusion = bf16[8192,8,128]{2,1,0:T(8,128)(2,1)S(1)} fusion(bf16[8192,128]{1,0:T(8,128)(2,1)} %get-tuple-element.35, bf16[8192,8]{1,0:T(8,128)(2,1)S(1)} %copy.25, bf16[8192,128]{1,0:T(8,128)(2,1)} %get-tuple-element.34, bf16[8192,8]{1,0:T(8,128)(2,1)} %copy.24), kind=kLoop, calls=%fused_computation.6 | loop fusion | flops 25165824 | bytes 21233664 | tf_op jit(solution)/shard_map/add | solution.py:20
  79.5 5.7 copy-done.1
  85.2 20.7 %fusion.2 = f32[1024,1024]{0,1:T(8,128)} fusion(bf16[1024,8,8,128]{3,2,1,0:T(8,128)(2,1)S(1)} %bitcast.382), kind=kOutput, calls=%fused_computation.4 | convolution fusion | flops 17179869184 | bytes 20971520 | tf_op jit(solution)/shard_map/dot_general | solution.py:29
  107.7 8.1 %fusion = f32[1,1024]{1,0:T(1,128)S(1)} fusion(bf16[1024,8,8,128]{3,2,1,0:T(8,128)(2,1)} %bitcast.383, f32[1,8192]{1,0:T(1,128)S(1)} %copy-done.6, f32[1,8192]{1,0:T(1,128)S(1)} %convert_divide_fusion), kind=kOutput, calls=%fused_computation.2 | convolution fusion | flops 16793600 | bytes 16846848 | tf_op jit(solution)/shard_map/dot_general | solution.py:32
  115.8 23.9 %all-reduce.1 = f32[1024]{0:T(1024)S(1)} all-reduce(f32[1024]{0:T(1024)S(1)} %bitcast.391), channel_id=3, replica_groups=mesh['tm'=4,'sensor'=8] {'sensor'}, use_global_device_ids=true, to_apply=%region_17.18.clone | all-reduce | flops 1024 | bytes 8192
  141.2 56.2 %reduce-scatter.2.cloned.1.call-done = f32[128,1024]{0,1:T(8,128)} async-done(((f32[1024,1024]{0,1:T(8,128)}), f32[128,1024]{0,1:T(8,128)}) %reduce-scatter.2.cloned.1.call-update) | async-done | bytes 524304 | tf_op jit(solution)/shard_map/reduce_scatter | solution.py:54
  197.4 9.2 %multiply_add_fusion.3 = (f32[128,1024]{0,1:T(8,128)S(1)}, f32[128,1024]{0,1:T(8,128)S(1)}) fusion(f32[128,1024]{0,1:T(8,128)} %reduce-scatter.2.cloned.1.call-done, f32[1024]{0:T(1024)S(1)} %bitcast.385, f32[128]{0:T(128)S(1)} %get-tuple-element.27, f32[1024,1024]{1,0:T(8,128)} %param.14, s32[]{:T(128)S(6)} %select_n.51), kind=kOutput, calls=%fused_computation.90 | convolution fusion | flops 1611268096 | bytes 6296068 | tf_op jit(solution)/shard_map/dot_general | solution.py:67
  210.2 8.2 %collective-permute-start.1 = (f32[128,1024]{0,1:T(8,128)S(1)}, f32[128,1024]{0,1:T(8,128)S(1)}, u32[]{:S(2)}, u32[]{:S(2)}) collective-permute-start(f32[128,1024]{0,1:T(8,128)S(1)} %get-tuple-element.30), channel_id=1, source_target_pairs={{0,8},{8,16},{16,24},{1,9},{9,17},{17,25},{2,10},{10,18},{18,26},{... | collective-permute-start | bytes 1572872 | tf_op jit(solution)/shard_map/ppermute | solution.py:10
  220.1 9.0 %collective-permute-start.2 = (f32[128,1024]{0,1:T(8,128)S(1)}, f32[128,1024]{0,1:T(8,128)S(1)}, u32[]{:S(2)}, u32[]{:S(2)}) collective-permute-start(f32[128,1024]{0,1:T(8,128)S(1)} %multiply_add_fusion.1), channel_id=1, source_target_pairs={{0,8},{8,16},{16,24},{1,9},{9,17},{17,25},{2,10},{10,18},{18,26},{... | collective-permute-start | bytes 1572872 | tf_op jit(solution)/shard_map/ppermute | solution.py:10
  231.5 9.0 %collective-permute-start.3 = (f32[128]{0:T(128)S(1)}, f32[128]{0:T(128)S(1)}, u32[]{:S(2)}, u32[]{:S(2)}) collective-permute-start(f32[128]{0:T(128)S(1)} %get-tuple-element.26), channel_id=1, source_target_pairs={{0,8},{8,16},{16,24},{1,9},{9,17},{17,25},{2,10},{10,18},{18,26},{... | collective-permute-start | bytes 1544 | tf_op jit(solution)/shard_map/ppermute | solution.py:10
  241.4 4.3 collective-permute-start.4
  246.5 4.0 collective-permute-start.5
  251.5 19.3 %all-gather = f32[8,1,128]{2,1,0:T(1,128)S(1)} all-gather(f32[1,1,128]{2,1,0:T(1,128)S(1)} %fusion.142), channel_id=1, replica_groups=mesh['tm'=4,'sensor'=8] {'sensor'}, dimensions={0}, use_global_device_ids=true | all-gather | bytes 4608 | tf_op jit(solution)/shard_map/all_gather | solution.py:90
  270.8 43.7 %all-gather.3.cloned.1.call-done = f32[1024,1024]{0,1:T(8,128)} async-done(((f32[128,1024]{0,1:T(8,128)}), f32[1024,1024]{0,1:T(8,128)}) %all-gather.3.cloned.1.call-update) | async-done | bytes 4194320 | tf_op jit(solution)/shard_map/all_gather | solution.py:89
  314.5 5.7 copy.28
  320.2 4.4 fusion.6
  326.6 11.7 %cholesky.223 = f32[128,128]{1,0:T(8,128)S(1)} custom-call(f32[128,128]{1,0:T(8,128)S(1)} %cholesky.580), custom_call_target="Cholesky" | custom-call | tf_op jit(solution)/shard_map/jit(cholesky)/cholesky | solution.py:91
  338.3 2.5 cholesky.255
  340.8 9.8 %custom-call.64 = f32[1,128,128]{1,2,0:T(8,128)S(1)} custom-call(f32[1,128,128]{2,1,0:T(8,128)S(1)} %get-tuple-element.59), custom_call_target="InvertDiagBlocksLowerTriangular" | custom-call | tf_op jit(solution)/shard_map/jit(cholesky)/cholesky | solution.py:91
  350.6 2.4 constant_dynamic-update-slice_fusion.48
  354.6 11.9 %cholesky.244 = f32[128,128]{1,0:T(8,128)S(1)} custom-call(f32[128,128]{1,0:T(8,128)S(1)} %cholesky.584), custom_call_target="Cholesky" | custom-call | tf_op jit(solution)/shard_map/jit(cholesky)/cholesky | solution.py:91
  367.1 9.8 %custom-call.65 = f32[1,128,128]{1,2,0:T(8,128)S(1)} custom-call(f32[1,128,128]{2,1,0:T(8,128)S(1)} %get-tuple-element.56), custom_call_target="InvertDiagBlocksLowerTriangular" | custom-call | tf_op jit(solution)/shard_map/jit(cholesky)/cholesky | solution.py:91
  380.2 11.7 %cholesky.468 = f32[128,128]{1,0:T(8,128)S(1)} custom-call(f32[128,128]{1,0:T(8,128)S(1)} %cholesky.589), custom_call_target="Cholesky" | custom-call | tf_op jit(solution)/shard_map/jit(cholesky)/cholesky | solution.py:91
  392.6 9.8 %custom-call.66 = f32[1,128,128]{1,2,0:T(8,128)S(1)} custom-call(f32[1,128,128]{2,1,0:T(8,128)S(1)} %get-tuple-element.53), custom_call_target="InvertDiagBlocksLowerTriangular" | custom-call | tf_op jit(solution)/shard_map/jit(cholesky)/cholesky | solution.py:91
  403.6 2.4 slice_subtract_fusion.2
  406.0 11.9 %cholesky.487 = f32[128,128]{1,0:T(8,128)S(1)} custom-call(f32[128,128]{1,0:T(8,128)S(1)} %cholesky.594), custom_call_target="Cholesky" | custom-call | tf_op jit(solution)/shard_map/jit(cholesky)/cholesky | solution.py:91
  418.5 9.8 %custom-call.67 = f32[1,128,128]{1,2,0:T(8,128)S(1)} custom-call(f32[1,128,128]{2,1,0:T(8,128)S(1)} %get-tuple-element.50), custom_call_target="InvertDiagBlocksLowerTriangular" | custom-call | tf_op jit(solution)/shard_map/jit(cholesky)/cholesky | solution.py:91
  429.4 2.3 slice_subtract_fusion.3
  431.8 11.7 %cholesky.506 = f32[128,128]{1,0:T(8,128)S(1)} custom-call(f32[128,128]{1,0:T(8,128)S(1)} %cholesky.599), custom_call_target="Cholesky" | custom-call | tf_op jit(solution)/shard_map/jit(cholesky)/cholesky | solution.py:91
  444.1 10.2 %custom-call.68 = f32[1,128,128]{1,2,0:T(8,128)S(1)} custom-call(f32[1,128,128]{2,1,0:T(8,128)S(1)} %get-tuple-element.47), custom_call_target="InvertDiagBlocksLowerTriangular" | custom-call | tf_op jit(solution)/shard_map/jit(cholesky)/cholesky | solution.py:91
  455.4 2.3 slice_subtract_fusion.4
  457.7 11.7 %cholesky.526 = f32[128,128]{1,0:T(8,128)S(1)} custom-call(f32[128,128]{1,0:T(8,128)S(1)} %cholesky.604), custom_call_target="Cholesky" | custom-call | tf_op jit(solution)/shard_map/jit(cholesky)/cholesky | solution.py:91
  470.0 9.8 %custom-call.69 = f32[1,128,128]{1,2,0:T(8,128)S(1)} custom-call(f32[1,128,128]{2,1,0:T(8,128)S(1)} %get-tuple-element.44), custom_call_target="InvertDiagBlocksLowerTriangular" | custom-call | tf_op jit(solution)/shard_map/jit(cholesky)/cholesky | solution.py:91
  482.8 11.7 %cholesky.546 = f32[128,128]{1,0:T(8,128)S(1)} custom-call(f32[128,128]{1,0:T(8,128)S(1)} %cholesky.609), custom_call_target="Cholesky" | custom-call | tf_op jit(solution)/shard_map/jit(cholesky)/cholesky | solution.py:91
  495.3 9.8 %custom-call.70 = f32[1,128,128]{1,2,0:T(8,128)S(1)} custom-call(f32[1,128,128]{2,1,0:T(8,128)S(1)} %get-tuple-element.41), custom_call_target="InvertDiagBlocksLowerTriangular" | custom-call | tf_op jit(solution)/shard_map/jit(cholesky)/cholesky | solution.py:91
  507.8 11.7 %cholesky.564 = f32[128,128]{1,0:T(8,128)S(1)} custom-call(f32[128,128]{1,0:T(8,128)S(1)} %slice_subtract_fusion.6), custom_call_target="Cholesky" | custom-call | tf_op jit(solution)/shard_map/jit(cholesky)/cholesky | solution.py:91
  529.7 4.8 fusion.7
  535.6 22.8 %while.1 = (s32[]{:T(128)}, f32[1024,1024]{1,0:T(8,128)}, s32[8,2]{0,1:T(2,128)S(1)}, f32[8,128,128]{2,1,0:T(8,128)S(1)}, s32[]{:T(128)}) while((s32[]{:T(128)}, f32[1024,1024]{1,0:T(8,128)}, s32[8,2]{0,1:T(2,128)S(1)}, f32[8,128,128]{2,1,0:T(8,128)S(1)}, s32[]{:T(128)}) %tuple.70), condition=%wide.while_cond, body=%wide.while_body.sunk | while | flops 2 | bytes 131189 | solution.py:93
  536.2 2.2 bitcast_dynamic-update-slice_fusion.2
  539.1 2.2 bitcast_dynamic-update-slice_fusion.2
  542.0 2.2 bitcast_dynamic-update-slice_fusion.2
  544.8 2.2 bitcast_dynamic-update-slice_fusion.2
  547.7 2.2 bitcast_dynamic-update-slice_fusion.2
  550.5 2.2 bitcast_dynamic-update-slice_fusion.2
  553.4 2.2 bitcast_dynamic-update-slice_fusion.2
  558.4 78.8 %custom-call.71 = f32[8,128,128]{1,2,0:T(8,128)S(1)} custom-call(f32[8,128,128]{2,1,0:T(8,128)S(1)} %get-tuple-element.9), custom_call_target="InvertDiagBlocksLowerTriangular" | custom-call | tf_op jit(solution)/shard_map/triangular_solve | solution.py:93
  (148 shorter events, 71.3 us)
Async XLA Ops:
  7.2 132.5 %copy-start = (f32[1024]{0:T(1024)S(1)}, f32[1024]{0:T(1024)}, u32[]{:S(2)}) copy-start(f32[1024]{0:T(1024)} %param.15) | copy-start | bytes 12292
  7.2 190.2 %reduce-scatter.2.cloned.1.call-start = ((), (), s32[]{:S(2)}) async-start(), calls=%async_computation.1 | async-start | bytes 4718592 | tf_op jit(solution)/shard_map/reduce_scatter | solution.py:54
  10.9 2.2 copy-start.4
  79.4 5.7 copy-start.1
  105.8 0.7 copy-start.8
  105.8 1.9 copy-start.6
  105.9 208.6 %all-gather.3.cloned.1.call-start = ((), (), s32[]{:S(2)}) async-start(), calls=%async_computation.2 | async-start | bytes 4718592 | tf_op jit(solution)/shard_map/all_gather | solution.py:89
  107.7 33.4 %copy-start.5 = (f32[1,1024]{1,0:T(1,128)S(1)}, f32[1,1024]{1,0:T(1,128)}, u32[]{:S(2)}) copy-start(f32[1,1024]{1,0:T(1,128)} %param.13) | copy-start | bytes 12292
  197.4 12.5 %copy-start.3 = (f32[128,1024]{0,1:T(8,128)S(1)}, f32[128,1024]{0,1:T(8,128)}, u32[]{:S(2)}) copy-start(f32[128,1024]{0,1:T(8,128)} %reduce-scatter.2.cloned.1.call-done) | copy-start | bytes 1572868
  206.7 3.3 collective-permute-start
  210.2 9.7 %collective-permute-start.1 = (f32[128,1024]{0,1:T(8,128)S(1)}, f32[128,1024]{0,1:T(8,128)S(1)}, u32[]{:S(2)}, u32[]{:S(2)}) collective-permute-start(f32[128,1024]{0,1:T(8,128)S(1)} %get-tuple-element.30), channel_id=1, source_target_pairs={{0,8},{8,16},{16,24},{1,9},{9,17},{17,25},{2,10},{10,18},{18,26},{... | collective-permute-start | bytes 1572872 | tf_op jit(solution)/shard_map/ppermute | solution.py:10
  220.1 10.5 %collective-permute-start.2 = (f32[128,1024]{0,1:T(8,128)S(1)}, f32[128,1024]{0,1:T(8,128)S(1)}, u32[]{:S(2)}, u32[]{:S(2)}) collective-permute-start(f32[128,1024]{0,1:T(8,128)S(1)} %multiply_add_fusion.1), channel_id=1, source_target_pairs={{0,8},{8,16},{16,24},{1,9},{9,17},{17,25},{2,10},{10,18},{18,26},{... | collective-permute-start | bytes 1572872 | tf_op jit(solution)/shard_map/ppermute | solution.py:10
  231.5 9.8 %collective-permute-start.3 = (f32[128]{0:T(128)S(1)}, f32[128]{0:T(128)S(1)}, u32[]{:S(2)}, u32[]{:S(2)}) collective-permute-start(f32[128]{0:T(128)S(1)} %get-tuple-element.26), channel_id=1, source_target_pairs={{0,8},{8,16},{16,24},{1,9},{9,17},{17,25},{2,10},{10,18},{18,26},{... | collective-permute-start | bytes 1544 | tf_op jit(solution)/shard_map/ppermute | solution.py:10
  241.4 5.1 collective-permute-start.4
  246.5 4.8 collective-permute-start.5
  324.6 1.9 copy-start.2
  658.2 0.6 copy-start.7
Sparse Core Ops, SparseCore 0:
  106.0 91.3 reduce-scatter.1
  231.6 82.7 all-gather.2
where the time goes:
time: 675 us; the launch traced here: 666 us
  other arithmetic  329 us (49%)
  waiting for transfers between devices  107 us (16%)
  matrix products  83.1 us (12%)
  local copies, waits for them, and re-layouts  46.7 us (7%)
  blocking collectives  43.2 us (6%)
  starting transfers between devices  36.4 us (5%)
  between operations  20.4 us (3%)
    another operation x30, other arithmetic, per_device(): lower = jnp.linalg.cholesky(post_full)  172 us
    another operation x3, other arithmetic, per_device(): lax.linalg.triangular_solve(lower, middle, left_side=True, lower=True, tr...  83.6 us
    add x1, other arithmetic, expand(): picked[:, 0, :, None] * first[:, None, :]  63.5 us
    reduce_scatter x1, waiting for transfers between devices, per_device(): lax.psum_scatter(gram_part, 'sensor', scatter_dimension=0, tiled=True)  56.2 us
    all_gather x1, waiting for transfers between devices, per_device(): post_full = lax.all_gather(post, 'sensor', axis=0, tiled=True)  43.7 us
    ppermute x6, starting transfers between devices, shifted(): return lax.ppermute(shard, axis, pairs)  36.3 us
    unnamed x1, blocking collectives  23.9 us
    another operation x14, matrix products, per_device(): lower = jnp.linalg.cholesky(post_full)  23.1 us
  transfers between devices with their start and end apart: 8, of which 8 were waited for; matrix products, arithmetic and copies ran while one was open for 2% of the time, Pallas kernels for 0%

commit v1 on v0

v1 whole, which is shorter than its diff:
```python
import functools

import jax
import jax.numpy as jnp
from jax import lax
from jax.experimental import pallas as pl
from jax.experimental.pallas import tpu as pltpu
from jax.sharding import PartitionSpec as P

HI = lax.Precision.HIGHEST
SUB = 8
CHUNK = 1024
BF16 = jnp.bfloat16
F32 = jnp.float32


def block_row(i, j, count):
    return i * count - i * (i - 1) // 2 + (j - i)


def packed_rows(count, width, sensors):
    return count * (count + 1) // 2 * width + SUB * sensors


def column_of(row):
    n = row.shape[1]
    return jnp.broadcast_to(row, (n, n)).T


def nt(a, b):
    return lax.dot_general(a, b, (((1,), (1,)), ((), ())), preferred_element_type=F32)


def gram_kernel(
    count, v_ref, b_ref, n_ref, r_ref, a_ref, p_ref, t_ref, out_ref, wide_ref, vec_ref, *acc_refs
):
    step = pl.program_id(0)
    width = v_ref.shape[1] // 2
    pair = 2 * width
    chunk = v_ref.shape[0]

    @pl.when(step == 0)
    def _():
        vec_ref[...] = jnp.zeros_like(vec_ref)
        for acc in acc_refs:
            acc[...] = jnp.zeros_like(acc)

    factor = a_ref[...].astype(F32) / n_ref[...]
    target = jnp.broadcast_to(r_ref[...] * factor, (16, chunk)).astype(BF16)
    rows = lax.broadcasted_iota(jnp.int32, (pair, pair), 0)
    cols = lax.broadcasted_iota(jnp.int32, (pair, pair), 1)
    eye = (rows == cols).astype(F32).astype(BF16)
    weighted = (nt(eye, v_ref[...]) * factor).astype(BF16)
    blocks = b_ref[...]
    for b in range(count):
        hit = jnp.where(blocks == b, 1.0, 0.0)
        hit0 = jnp.broadcast_to(hit[0:1], (16, chunk)).astype(BF16)
        hit1 = jnp.broadcast_to(hit[1:2], (16, chunk)).astype(BF16)
        for q in range(width // 16):
            lo = 16 * q
            wide_ref[b * width + lo : b * width + lo + 16, :] = (
                weighted[lo : lo + 16] * hit0 + weighted[width + lo : width + lo + 16] * hit1
            )
    for j, acc in enumerate(acc_refs):
        right = wide_ref[j * pair : (j + 1) * pair, :]
        acc[...] += nt(wide_ref[0 : (j + 1) * pair, :], right)
        vec_ref[:, j * pair : (j + 1) * pair] += nt(target, right)

    @pl.when(step == pl.num_programs(0) - 1)
    def _():
        prior = p_ref[...]
        vec = vec_ref[0:1, :] + jnp.dot(t_ref[...], prior, precision=HI, preferred_element_type=F32)
        base = count * (count + 1) // 2 * width
        out_ref[base:, :] = jnp.zeros((out_ref.shape[0] - base, width), F32)
        for i in range(count):
            out_ref[base + i : base + i + 1, :] = vec[:, i * width : (i + 1) * width]
        for j, acc in enumerate(acc_refs):
            total = acc[...] + lax.dot_general(
                prior[:, : (j + 1) * pair],
                prior[:, j * pair : (j + 1) * pair],
                (((0,), (0,)), ((), ())),
                precision=HI,
                preferred_element_type=F32,
            )
            for jj in (2 * j, 2 * j + 1):
                for i in range(jj + 1):
                    at = block_row(i, jj, count) * width
                    out_ref[at : at + width, :] = total[
                        i * width : (i + 1) * width, (jj % 2) * width : (jj % 2 + 1) * width
                    ]


def local_gram(values, blocks, noise, reading, avail, prior, target, count, sensors):
    rows, pair = values.shape
    width = pair // 2
    states = count * width
    total = packed_rows(count, width, sensors)
    line = pl.BlockSpec((1, CHUNK), lambda c: (0, c))
    whole = lambda shape: pl.BlockSpec(shape, lambda c: (0,) * len(shape))
    return pl.pallas_call(
        functools.partial(gram_kernel, count),
        grid=(rows // CHUNK,),
        in_specs=[
            pl.BlockSpec((CHUNK, pair), lambda c: (c, 0)),
            pl.BlockSpec((2, CHUNK), lambda c: (0, c)),
            line,
            line,
            line,
            whole(prior.shape),
            whole(target.shape),
        ],
        out_specs=whole((total, width)),
        out_shape=jax.ShapeDtypeStruct((total, width), F32),
        scratch_shapes=[pltpu.VMEM((states, CHUNK), BF16), pltpu.VMEM((16, states), F32)]
        + [pltpu.VMEM(((j + 1) * pair, pair), F32) for j in range(states // pair)],
        compiler_params=pltpu.CompilerParams(vmem_limit_bytes=48 << 20),
        cost_estimate=pl.CostEstimate(
            flops=2 * rows * states * states * 5 // 8, bytes_accessed=rows * pair * 2, transcendentals=0
        ),
        name="gram",
    )(values, blocks, noise, reading, avail, prior, target)


def frame_kernel(count, f_ref, out_ref):
    width = out_ref.shape[1]
    base = count * (count + 1) // 2 * width
    out_ref[base:, :] = jnp.zeros((out_ref.shape[0] - base, width), F32)
    parts = [f_ref[:, i * width : (i + 1) * width] for i in range(count)]
    for i in range(count):
        out_ref[base + i : base + i + 1, :] = parts[i]
        column = column_of(parts[i])
        for j in range(i, count):
            at = block_row(i, j, count) * width
            out_ref[at : at + width, :] = column * parts[j]


def frame_scale(inverse, count, width, sensors):
    total = packed_rows(count, width, sensors)
    return pl.pallas_call(
        functools.partial(frame_kernel, count),
        out_shape=jax.ShapeDtypeStruct((total, width), F32),
        cost_estimate=pl.CostEstimate(flops=total * width, bytes_accessed=total * width * 4, transcendentals=0),
        name="frames",
    )(inverse)


def spread(x, index, axis):
    return jnp.broadcast_to(lax.slice_in_dim(x, index, index + 1, axis=axis), x.shape)


def split3(x):
    a = x.astype(BF16)
    rest = x - a.astype(F32)
    b = rest.astype(BF16)
    return a, b, (rest - b.astype(F32)).astype(BF16)


def far_product(top, both):
    a, b, c = split3(both)
    left = jnp.concatenate([a, a, b, a, c, b], 0)[:, : top.shape[1]]
    right = jnp.concatenate([a, b, a, c, a, b], 0)
    return lax.dot_general(left, right, (((0,), (0,)), ((), ())), preferred_element_type=F32)


def diag_factor(block):
    size = block.shape[0]
    groups = size // SUB
    lane = lax.broadcasted_iota(jnp.int32, (SUB, size), 1)
    sub = lax.broadcasted_iota(jnp.int32, (SUB, size), 0)
    left = [block[SUB * r : SUB * (r + 1), :] for r in range(groups)]
    right = [(lane == sub + SUB * r).astype(F32) for r in range(groups)]
    tops = []
    lows = []
    for g in range(groups):
        near = min(groups, g + 2)
        cols = {r: [spread(left[r], SUB * g + k, 1) for k in range(SUB)] for r in range(g, near)}
        s = [[spread(cols[g][k], i, 0) if i >= k else None for k in range(SUB)] for i in range(SUB)]
        xs = [spread(left[g], k, 0) for k in range(SUB)]
        ys = [spread(right[g], k, 0) for k in range(SUB)]
        inv = []
        for k in range(SUB):
            inv.append(lax.rsqrt(s[k][k]))
            for i in range(k + 1, SUB):
                s[i][k] = s[i][k] * inv[k]
            for j in range(k + 1, SUB):
                for i in range(j, SUB):
                    s[i][j] = s[i][j] - s[i][k] * s[j][k]
            xs[k] = xs[k] * inv[k]
            ys[k] = ys[k] * inv[k]
            for i in range(k + 1, SUB):
                xs[i] = xs[i] - s[i][k] * xs[k]
                ys[i] = ys[i] - s[i][k] * ys[k]
        for r in range(g + 1, near):
            ls = cols[r]
            for k in range(SUB):
                ls[k] = ls[k] * inv[k]
                for j in range(k + 1, SUB):
                    ls[j] = ls[j] - s[j][k] * ls[k]
                left[r] = left[r] - ls[k] * xs[k]
                right[r] = right[r] - ls[k] * ys[k]
        top, low = xs[0], ys[0]
        for k in range(1, SUB):
            top = jnp.where(sub == k, xs[k], top)
            low = jnp.where(sub == k, ys[k], low)
        if near < groups:
            delta = far_product(top, jnp.concatenate([top, low], 1))
            for r in range(near, groups):
                left[r] = left[r] - delta[SUB * r : SUB * (r + 1), :size]
                right[r] = right[r] - delta[SUB * r : SUB * (r + 1), size:]
        tops.append(jnp.where(lane >= sub + SUB * g, top, 0.0))
        lows.append(low)
    return jnp.concatenate(tops, 0), jnp.concatenate(lows, 0)


def dot_tn(a, b):
    return lax.dot_general(a, b, (((0,), (0,)), ((), ())), precision=HI, preferred_element_type=F32)


def dot_nn(a, b):
    return jnp.dot(a, b, precision=HI, preferred_element_type=F32)


def factor_kernel(count, own_ref, x_ref, f_ref, rows_ref, est_ref, s_ref, r_ref, t_ref):
    width = x_ref.shape[1]
    share = rows_ref.shape[0]
    base = count * (count + 1) // 2 * width

    def prior_row(k):
        parts = []
        for j in range(k, count):
            at = block_row(k, j, count) * width
            parts.append(x_ref[at : at + width, :])
        parts.append(column_of(x_ref[base + k : base + k + 1, :]))
        return jnp.concatenate(parts, 1)

    s_ref[:, :] = prior_row(0)

    @pl.loop(0, count)
    def _(k):
        at = pl.multiple_of(k * width, width)
        upper, inverse = diag_factor(s_ref[:, pl.ds(at, width)])
        t_ref[pl.ds(at, width), :] = inverse
        r_ref[pl.ds(at, width), pl.ds(at, width)] = upper
        for kk in range(count):

            @pl.when(k == kk)
            def _():
                rest = (kk + 1) * width
                row = dot_nn(t_ref[kk * width : rest, :], s_ref[:, rest:])
                r_ref[kk * width : rest, rest:] = row
                if kk + 1 < count:
                    s_ref[:, rest:] = prior_row(kk + 1) - dot_tn(
                        r_ref[0:rest, rest : rest + width], r_ref[0:rest, rest:]
                    )

    states = count * width
    solved = [None] * count
    for k in reversed(range(count)):
        right = r_ref[k * width : (k + 1) * width, states:]
        if k + 1 < count:
            right = right - dot_nn(
                r_ref[k * width : (k + 1) * width, (k + 1) * width : states],
                jnp.concatenate(solved[k + 1 :], 0),
            )
        solved[k] = dot_tn(t_ref[k * width : (k + 1) * width, :], right)
    for k in range(count):
        cols = slice(k * width, (k + 1) * width)
        est_ref[:, cols] = solved[k].T[0:1, :] / f_ref[:, cols]
    first = pl.multiple_of(own_ref[0] * share, share)
    for j in range(count):
        cols = slice(j * width, (j + 1) * width)
        mine = r_ref[pl.ds(first, share), cols] * f_ref[:, cols]
        rows_ref[:, cols] = jnp.where(first < (j + 1) * width, mine, 0.0)


def factor(own, packed, frame, count, share):
    width = packed.shape[1]
    states = count * width
    vmem = pl.BlockSpec(memory_space=pltpu.VMEM)
    return pl.pallas_call(
        functools.partial(factor_kernel, count),
        in_specs=[pl.BlockSpec(memory_space=pltpu.SMEM), vmem, vmem],
        out_specs=[vmem, vmem],
        out_shape=[
            jax.ShapeDtypeStruct((share, states), F32),
            jax.ShapeDtypeStruct((1, states), F32),
        ],
        scratch_shapes=[
            pltpu.VMEM((width, states + width), F32),
            pltpu.VMEM((states, states + width), F32),
            pltpu.VMEM((states, width), F32),
        ],
        compiler_params=pltpu.CompilerParams(vmem_limit_bytes=48 << 20),
        cost_estimate=pl.CostEstimate(
            flops=4 * states**3, bytes_accessed=packed.size * 4, transcendentals=states
        ),
        name="factor",
    )(own, packed, frame)


def per_device(values, blocks, noise_scale, readings, available, decay, prior_factor, prior_target):
    states = prior_factor.shape[0]
    width = values.shape[1] // 2
    count = states // width
    sensors = lax.axis_size("sensor")
    steps = lax.axis_size("tm")
    share = states // sensors
    own = lax.axis_index("sensor")
    time = lax.axis_index("tm")

    def earlier(x, by):
        return lax.ppermute(x, "tm", [(i, i + by) for i in range(steps - by)])

    frame = jnp.ones((1, states), F32)
    for by in range(1, steps):
        frame = frame * jnp.where(time >= by, earlier(decay, by), 1.0)
    first = (time == 0).astype(F32)
    prior = lax.dynamic_slice_in_dim(prior_factor, own * share, share, 0) * first
    target = lax.dynamic_slice_in_dim(prior_target, own * share, share, 0)[None, :]
    packed = local_gram(
        values, blocks.T, noise_scale, readings, available, prior, target, count, sensors
    )
    scale = frame_scale(1.0 / frame, count, width, sensors)
    piece = packed.shape[0] // sensors
    scale = lax.dynamic_slice_in_dim(scale, own * piece, piece, 0)
    part = lax.psum_scatter(packed, "sensor", scatter_dimension=0, tiled=True) * scale
    by = 1
    while by < steps:
        part = part + earlier(part, by)
        by *= 2
    packed = lax.all_gather(part, "sensor", axis=0, tiled=True)
    rows, estimate = factor(own.astype(jnp.int32)[None], packed, frame, count, share)
    return rows[None], estimate


def solution(mesh):
    placed = (
        P("sensor", None),
        P("sensor", None),
        P("tm", "sensor"),
        P("tm", "sensor"),
        P("tm", "sensor"),
        P("tm", None),
        P(),
        P(),
    )
    return jax.shard_map(
        per_device,
        mesh=mesh,
        in_specs=placed,
        out_specs=(P("tm", "sensor", None), P("tm", None)),
        check_vma=False,
    )
```

time: 675 us -> 233 us (0.35); the launches traced: 666 us -> 232 us
  other arithmetic: 329 us -> 3.56 us
  matrix products: 83.1 us -> 0 us
  Pallas kernels: 0 us -> 70.3 us
  blocking collectives: 43.2 us -> 0 us
  local copies, waits for them, and re-layouts: 46.7 us -> 6.1 us
  starting transfers between devices: 36.4 us -> 18 us
  waiting for transfers between devices: 107 us -> 120 us
    another operation x33 -> x0, other arithmetic: 256 us -> none  [the longest x30 172 us: per_device(): lower = jnp.linalg.cholesky(post_full)]
    pallas_call x0 -> x3, Pallas kernels: none -> 70.3 us  [the longest x1 44 us: factor(): pl.pallas_call(functools.partial(factor_kernel, count), in_specs=[pl.Bloc...]
    add x7 -> x2, other arithmetic: 65 us -> 0.79 us  [per_device(): part = part + earlier(part, by)]
    unnamed x2 -> x3, waiting for transfers between devices: 0.03 us -> 60.7 us
    reduce_scatter x1 -> x0, waiting for transfers between devices: 56.2 us -> none  [per_device(): lax.psum_scatter(gram_part, 'sensor', scatter_dimension=0, tiled=True)]
    another operation x44 -> x0, matrix products: 43.7 us -> none  [the longest x14 23.1 us: per_device(): lower = jnp.linalg.cholesky(post_full)]
    dot_general x4 -> x0, matrix products: 39.4 us -> none  [the longest x1 20.7 us: measure(): lax.dot_general(dense, dense, (((0,), (0,)), ((), ())), preferred_element...]
    another operation x38 -> x0, local copies, waits for them, and re-layouts: 25.3 us -> none
  transfers between devices with their start and end apart: 8 -> 7, of which waited for: 8 -> 5; matrix products, arithmetic and copies ran while one was open for 2% -> 0% of each run, Pallas kernels for 0% -> 1%
where the time goes in v1:
time: 233 us; the launch traced here: 232 us
  waiting for transfers between devices  120 us (52%)
  Pallas kernels  70.3 us (30%)
  starting transfers between devices  18 us (8%)
  between operations  14.1 us (6%)
  local copies, waits for them, and re-layouts  6.1 us (3%)
  other arithmetic  3.56 us (2%)
    unnamed x3, waiting for transfers between devices  60.7 us
    all_gather x1, waiting for transfers between devices, per_device(): packed = lax.all_gather(part, 'sensor', axis=0, tiled=True)  52.5 us
    pallas_call x1, Pallas kernels, factor(): pl.pallas_call(functools.partial(factor_kernel, count), in_specs=[pl.Bloc...  44 us
    pallas_call x1, Pallas kernels, local_gram(): pl.pallas_call(functools.partial(gram_kernel, count), grid=(rows // CHUNK...  23.9 us
    ppermute x5, starting transfers between devices, earlier(): return lax.ppermute(x, 'tm', [(i, i + by) for i in range(steps - by)])  17.9 us
    ppermute x5, waiting for transfers between devices, earlier(): return lax.ppermute(x, 'tm', [(i, i + by) for i in range(steps - by)])  6.53 us
    unnamed x14, local copies, waits for them, and re-layouts  6.02 us
  transfers between devices with their start and end apart: 7, of which 5 were waited for; matrix products, arithmetic and copies ran while one was open for 0% of the time, Pallas kernels for 1%

profile of v1, /device:TPU:0, one launch (start us, length us, event | category | flops | bytes accessed | tf_op | source)
XLA Modules:
  0.0 231.9 jit_solution(16349425641501147424)
XLA Ops:
  7.2 0.0 copy-start
  7.2 0.0 reduce-scatter.4.cloned.1.call-start
  7.2 0.6 copy-done
  7.9 0.1 dynamic-slice_bitcast_fusion.t_ref
  7.9 1.1 dynamic-slice_multiply_fusion.p_ref
  9.0 0.0 copy-start.2
  9.0 0.8 copy-done.2
  9.9 0.0 copy-start.3
  9.9 0.8 copy-done.3
  10.6 0.0 copy-start.4
  10.6 0.8 copy-done.4
  11.4 0.0 copy-start.5
  11.4 0.8 copy-done.5
  12.1 23.9 %gram.1 = f32[4672,128]{1,0:T(8,128)} custom-call(bf16[8192,256]{1,0:T(8,128)(2,1)} %v_ref.1, s32[2,8192]{1,0:T(2,128)S(1)} %bitcast.6, f32[1,8192]{1,0:T(1,128)S(1)} %copy-done.3, f32[1,8192]{1,0:T(1,128)S(1)} %copy-done.4, s32[1,8192]{1,0:T(1,128)S(1)} %copy-done.5, f32[128,1024]{1,0:T(8,128)S(1)} %dynamic-slice_multiply_fusion.p_ref, ...), custom_call_target="tpu_custom_call" | custom-call | flops 10737418240 | bytes 4194304 | tf_op jit(solution)/shard_map/gram/pallas_call | solution.py:100
  36.1 0.0 copy-start.6
  36.1 0.0 reduce-scatter.4.cloned.1.call-update
  36.1 0.0 all-gather.2.cloned.1.call-start
  36.2 0.6 copy-done.6
  36.8 2.3 %collective-permute-start = (f32[1,1024]{1,0:T(1,128)S(1)}, f32[1,1024]{1,0:T(1,128)S(1)}, u32[]{:S(2)}, u32[]{:S(2)}) collective-permute-start(f32[1,1024]{1,0:T(1,128)S(1)} %copy-done.6), channel_id=1, source_target_pairs={{0,8},{8,16},{16,24},{1,9},{9,17},{17,25},{2,10},{10,18},{18,26},{... | collective-permute-start | bytes 12296 | tf_op jit(solution)/shard_map/ppermute | solution.py:312
  39.1 3.2 %collective-permute-start.2 = (f32[1,1024]{1,0:T(1,128)S(1)}, f32[1,1024]{1,0:T(1,128)S(1)}, u32[]{:S(2)}, u32[]{:S(2)}) collective-permute-start(f32[1,1024]{1,0:T(1,128)S(1)} %copy-done.6), channel_id=1, source_target_pairs={{0,24},{1,25},{2,26},{3,27},{4,28},{5,29},{6,30},{7,31}} | collective-permute-start | bytes 12296 | tf_op jit(solution)/shard_map/ppermute | solution.py:312
  42.3 1.9 collective-permute-start.1
  44.2 0.0 collective-permute-done
  44.2 0.0 collective-permute-done.2
  44.2 1.3 collective-permute-done.1
  45.5 0.6 broadcast_divide_fusion
  46.1 2.4 %frames.1 = f32[4672,128]{1,0:T(8,128)} custom-call(f32[1,1024]{1,0:T(1,128)} %get-tuple-element.6.f_ref), custom_call_target="tpu_custom_call" | custom-call | flops 598016 | bytes 2392064 | tf_op jit(solution)/shard_map/frames/pallas_call | solution.py:139
  48.5 60.7 %reduce-scatter.4.cloned.1.call-done = f32[584,128]{1,0:T(8,128)} async-done(((f32[4672,128]{1,0:T(8,128)}), f32[584,128]{1,0:T(8,128)}) %reduce-scatter.4.cloned.1.call-update) | async-done | bytes 299024
  109.2 1.1 dynamic-slice_multiply_fusion.1
  110.3 1.3 collective-permute-start.3
  111.6 1.2 collective-permute-done.3
  112.8 9.2 %collective-permute-start.4 = (f32[584,128]{1,0:T(8,128)S(1)}, f32[584,128]{1,0:T(8,128)S(1)}, u32[]{:S(2)}, u32[]{:S(2)}) collective-permute-start(f32[584,128]{1,0:T(8,128)S(1)} %add.17), channel_id=1, source_target_pairs={{0,16},{8,24},{1,17},{9,25},{2,18},{10,26},{3,19},{11,27},{4,20},{... | collective-permute-start | bytes 897032 | tf_op jit(solution)/shard_map/ppermute | solution.py:312
  122.0 4.1 %collective-permute-done.4 = f32[584,128]{1,0:T(8,128)S(1)} collective-permute-done((f32[584,128]{1,0:T(8,128)S(1)}, f32[584,128]{1,0:T(8,128)S(1)}, u32[]{:S(2)}, u32[]{:S(2)}) %collective-permute-start.4) | collective-permute-done | bytes 299040 | tf_op jit(solution)/shard_map/ppermute | solution.py:312
  126.1 0.7 add.18
  126.8 0.0 all-gather.2.cloned.1.call-update
  126.9 52.5 %all-gather.2.cloned.1.call-done.x_ref = f32[4672,128]{1,0:T(8,128)} async-done(((f32[584,128]{1,0:T(8,128)}), f32[4672,128]{1,0:T(8,128)}) %all-gather.2.cloned.1.call-update) | async-done | bytes 2392080 | tf_op jit(solution)/shard_map/all_gather | solution.py:331
  179.4 0.0 copy-start.1
  179.4 1.7 copy-done.1
  181.1 44.0 %factor.1 = (f32[128,1024]{1,0:T(8,128)}, f32[1,1024]{1,0:T(1,128)}) custom-call(s32[1]{0:T(128)} %bitcast.own_ref, f32[4672,128]{1,0:T(8,128)S(1)} %copy-done.1, f32[1,1024]{1,0:T(1,128)S(1)} %get-tuple-element.7.f_ref), custom_call_target="tpu_custom_call" | custom-call | flops 4294967296 | bytes 2392064 | tf_op jit(solution)/shard_map/factor/pallas_call | solution.py:280
  (1 shorter events, 0.0 us)
Async XLA Ops:
  7.2 0.7 copy-start
  7.2 102.0 %reduce-scatter.4.cloned.1.call-start = ((), (), s32[]{:S(2)}) async-start(), calls=%async_computation.2 | async-start | bytes 2691072
  9.0 0.8 copy-start.2
  9.9 0.8 copy-start.3
  10.6 0.8 copy-start.4
  11.4 0.8 copy-start.5
  36.1 0.7 copy-start.6
  36.1 143.3 %all-gather.2.cloned.1.call-start = ((), (), s32[]{:S(2)}) async-start(), calls=%async_computation.1 | async-start | bytes 2691072 | tf_op jit(solution)/shard_map/all_gather | solution.py:331
  36.8 7.4 %collective-permute-start = (f32[1,1024]{1,0:T(1,128)S(1)}, f32[1,1024]{1,0:T(1,128)S(1)}, u32[]{:S(2)}, u32[]{:S(2)}) collective-permute-start(f32[1,1024]{1,0:T(1,128)S(1)} %copy-done.6), channel_id=1, source_target_pairs={{0,8},{8,16},{16,24},{1,9},{9,17},{17,25},{2,10},{10,18},{18,26},{... | collective-permute-start | bytes 12296 | tf_op jit(solution)/shard_map/ppermute | solution.py:312
  39.1 5.1 %collective-permute-start.2 = (f32[1,1024]{1,0:T(1,128)S(1)}, f32[1,1024]{1,0:T(1,128)S(1)}, u32[]{:S(2)}, u32[]{:S(2)}) collective-permute-start(f32[1,1024]{1,0:T(1,128)S(1)} %copy-done.6), channel_id=1, source_target_pairs={{0,24},{1,25},{2,26},{3,27},{4,28},{5,29},{6,30},{7,31}} | collective-permute-start | bytes 12296 | tf_op jit(solution)/shard_map/ppermute | solution.py:312
  42.3 3.2 %collective-permute-start.1 = (f32[1,1024]{1,0:T(1,128)S(1)}, f32[1,1024]{1,0:T(1,128)S(1)}, u32[]{:S(2)}, u32[]{:S(2)}) collective-permute-start(f32[1,1024]{1,0:T(1,128)S(1)} %copy-done.6), channel_id=1, source_target_pairs={{0,16},{8,24},{1,17},{9,25},{2,18},{10,26},{3,19},{11,27},{4,20},{... | collective-permute-start | bytes 12296 | tf_op jit(solution)/shard_map/ppermute | solution.py:312
  110.3 2.5 %collective-permute-start.3 = (f32[584,128]{1,0:T(8,128)S(1)}, f32[584,128]{1,0:T(8,128)S(1)}, u32[]{:S(2)}, u32[]{:S(2)}) collective-permute-start(f32[584,128]{1,0:T(8,128)S(1)} %dynamic-slice_multiply_fusion.1), channel_id=1, source_target_pairs={{0,8},{8,16},{16,24},{1,9},{9,17},{17,25},{2,10},{10,18},{18,26},{... | collective-permute-start | bytes 897032 | tf_op jit(solution)/shard_map/ppermute | solution.py:312
  112.8 13.3 %collective-permute-start.4 = (f32[584,128]{1,0:T(8,128)S(1)}, f32[584,128]{1,0:T(8,128)S(1)}, u32[]{:S(2)}, u32[]{:S(2)}) collective-permute-start(f32[584,128]{1,0:T(8,128)S(1)} %add.17), channel_id=1, source_target_pairs={{0,16},{8,24},{1,17},{9,25},{2,18},{10,26},{3,19},{11,27},{4,20},{... | collective-permute-start | bytes 897032 | tf_op jit(solution)/shard_map/ppermute | solution.py:312
  179.4 1.7 copy-start.1
Sparse Core Ops, SparseCore 0:
  36.2 72.9 reduce-scatter.3
  127.0 52.3 all-gather.1

commit v2 on v1

v2 whole, which is shorter than its diff:
```python
import functools

import jax
import jax.numpy as jnp
from jax import lax
from jax.experimental import pallas as pl
from jax.experimental.pallas import tpu as pltpu
from jax.sharding import PartitionSpec as P

HI = lax.Precision.HIGHEST
SUB = 8
CHUNK = 2048
VMEM_BYTES = 60 << 20
CUTS = (2, 4)
CUT_PLACES = (0,) + CUTS
FAR = 2
FACTOR_FLOPS = 5 * 10**9
BF16 = jnp.bfloat16
F32 = jnp.float32


def upper_blocks(lo, hi, count):
    return [(i, j) for i in range(lo, hi) for j in range(i, count)]


def column_of(row):
    n = row.shape[1]
    return jnp.broadcast_to(row, (n, n)).T


def nt(a, b):
    return lax.dot_general(a, b, (((1,), (1,)), ((), ())), preferred_element_type=F32)


def dot_tn(a, b):
    return lax.dot_general(a, b, (((0,), (0,)), ((), ())), precision=HI, preferred_element_type=F32)


def dot_nn(a, b):
    return jnp.dot(a, b, precision=HI, preferred_element_type=F32)


def tiles(lo, hi, count):
    spans = [(j, min(j + 2, count)) for j in range(lo, count, 2)]
    return [(first, end, min(end, hi)) for first, end in spans]


def gram_kernel(
    count, spans, place_ref, v_ref, b_ref, n_ref, r_ref, a_ref, p_ref, t_ref, *refs
):
    out_refs = refs[: 2 * len(spans)]
    packed_refs = refs[2 * len(spans) : 3 * len(spans)]
    wide_ref, *acc_refs = refs[3 * len(spans) :]
    lo, hi = spans[0][0], spans[-1][1]
    step = pl.program_id(0)
    width = v_ref.shape[1] // 2
    pair = 2 * width
    chunk = v_ref.shape[0]
    top = 16 if lo == 0 else 0

    @pl.when(step == 0)
    def _():
        for acc in acc_refs:
            acc[...] = jnp.zeros_like(acc)

    factor = a_ref[...].astype(F32) / n_ref[...]
    if top:
        wide_ref[0:top, :] = jnp.broadcast_to(r_ref[...] * factor, (top, chunk)).astype(BF16)
    rows = lax.broadcasted_iota(jnp.int32, (pair, pair), 0)
    cols = lax.broadcasted_iota(jnp.int32, (pair, pair), 1)
    eye = (rows == cols).astype(F32).astype(BF16)
    weighted = (nt(eye, v_ref[...]) * factor).astype(BF16)
    blocks = b_ref[...]
    for b in range(lo, count):
        hit = jnp.where(blocks == b, 1.0, 0.0)
        hit0 = jnp.broadcast_to(hit[0:1], (16, chunk)).astype(BF16)
        hit1 = jnp.broadcast_to(hit[1:2], (16, chunk)).astype(BF16)
        for q in range(0, width, 16):
            at = top + (b - lo) * width + q
            wide_ref[at : at + 16, :] = (
                weighted[q : q + 16] * hit0 + weighted[width + q : width + q + 16] * hit1
            )
    columns = tiles(lo, hi, count)
    for (first, end, stop), acc in zip(columns, acc_refs):
        acc[...] += nt(
            wide_ref[0 : top + (stop - lo) * width, :],
            wide_ref[top + (first - lo) * width : top + (end - lo) * width, :],
        )

    @pl.when(step == pl.num_programs(0) - 1)
    def _():
        prior = p_ref[...] * place_ref[1].astype(F32)
        totals = [
            acc[top:, :]
            + dot_tn(prior[:, lo * width : stop * width], prior[:, first * width : end * width])
            for (first, end, stop), acc in zip(columns, acc_refs)
        ]
        for n, (start, past) in enumerate(spans):
            kept = upper_blocks(start, past, count)
            packed_ref = packed_refs[n]
            for m, (i, j) in enumerate(kept):
                tile = (j - lo) // 2
                across = j - columns[tile][0]
                packed_ref[m * width : (m + 1) * width, :] = totals[tile][
                    (i - lo) * width : (i - lo + 1) * width, across * width : (across + 1) * width
                ]
            if start == 0:
                base = len(kept) * width
                packed_ref[base:, :] = jnp.zeros((packed_ref.shape[0] - base, width), F32)
                vec = jnp.concatenate([acc[0:1, :] for acc in acc_refs], 1) + dot_nn(t_ref[0], prior)
                for i in range(count):
                    packed_ref[base + i : base + i + 1, :] = vec[:, i * width : (i + 1) * width]
            half = packed_ref.shape[0] // 2
            upper = place_ref[2 + n]
            out_refs[2 * n][...] = packed_ref[pl.ds(pl.multiple_of(upper * half, SUB), half), :]
            out_refs[2 * n + 1][...] = packed_ref[
                pl.ds(pl.multiple_of((1 - upper) * half, SUB), half), :
            ]


def packed_rows(lo, hi, count, width, sensors):
    return len(upper_blocks(lo, hi, count)) * width + (SUB * sensors if lo == 0 else 0)


def local_gram(spans, place, values, blocks, noise, reading, avail, prior, target, count, sensors):
    rows, pair = values.shape
    width = pair // 2
    lo, hi = spans[0][0], spans[-1][1]
    share = prior.shape[0] // sensors
    totals = [packed_rows(first, past, count, width, sensors) for first, past in spans]
    top = 16 if lo == 0 else 0
    chunk = min(CHUNK, rows)
    line = pl.BlockSpec((1, chunk), lambda c, place: (0, c))
    halves = [total // 2 for total in totals for _ in range(2)]
    return pl.pallas_call(
        functools.partial(gram_kernel, count, spans),
        grid_spec=pltpu.PrefetchScalarGridSpec(
            num_scalar_prefetch=1,
            grid=(rows // chunk,),
            in_specs=[
                pl.BlockSpec((chunk, pair), lambda c, place: (c, 0)),
                pl.BlockSpec((2, chunk), lambda c, place: (0, c)),
                line,
                line,
                line,
                pl.BlockSpec((share, prior.shape[1]), lambda c, place: (place[0], 0)),
                pl.BlockSpec((1, 1, share), lambda c, place: (place[0], 0, 0)),
            ],
            out_specs=[pl.BlockSpec((half, width), lambda c, place: (0, 0)) for half in halves],
            scratch_shapes=[pltpu.VMEM((total, width), F32) for total in totals]
            + [pltpu.VMEM((top + (count - lo) * width, chunk), BF16)]
            + [
                pltpu.VMEM((top + (stop - lo) * width, (end - first) * width), F32)
                for first, end, stop in tiles(lo, hi, count)
            ],
        ),
        out_shape=[jax.ShapeDtypeStruct((half, width), F32) for half in halves],
        compiler_params=pltpu.CompilerParams(vmem_limit_bytes=VMEM_BYTES),
        cost_estimate=pl.CostEstimate(
            flops=2 * rows * width * sum(totals), bytes_accessed=rows * pair * 2, transcendentals=0
        ),
        name="gram",
    )(place, values, blocks, noise, reading, avail, prior, target.reshape(sensors, 1, share))


def frame_kernel(count, spans, f_ref, *out_refs):
    width = out_refs[0].shape[1]
    parts = [f_ref[:, i * width : (i + 1) * width] for i in range(count)]
    for (lo, hi), out_ref in zip(spans, out_refs):
        kept = upper_blocks(lo, hi, count)
        for n, (i, j) in enumerate(kept):
            out_ref[n * width : (n + 1) * width, :] = column_of(parts[i]) * parts[j]
        base = len(kept) * width
        if lo == 0:
            out_ref[base:, :] = jnp.zeros((out_ref.shape[0] - base, width), F32)
            for i in range(count):
                out_ref[base + i : base + i + 1, :] = parts[i]


def frame_scales(inverse, spans, count, width, sensors):
    shapes = [(packed_rows(lo, hi, count, width, sensors), width) for lo, hi in spans]
    size = sum(rows * width for rows, width in shapes)
    return pl.pallas_call(
        functools.partial(frame_kernel, count, spans),
        out_shape=[jax.ShapeDtypeStruct(shape, F32) for shape in shapes],
        cost_estimate=pl.CostEstimate(flops=size, bytes_accessed=size * 4, transcendentals=0),
        name="frames",
    )(inverse)


def spread(x, index, axis):
    return jnp.broadcast_to(lax.slice_in_dim(x, index, index + 1, axis=axis), x.shape)


def split3(x):
    a = x.astype(BF16)
    rest = x - a.astype(F32)
    b = rest.astype(BF16)
    return a, b, (rest - b.astype(F32)).astype(BF16)


def far_product(top, both):
    a, b, c = split3(both)
    left = jnp.concatenate([a, a, b, a, c, b], 0)[:, : top.shape[1]]
    right = jnp.concatenate([a, b, a, c, a, b], 0)
    return lax.dot_general(left, right, (((0,), (0,)), ((), ())), preferred_element_type=F32)


def diag_factor(block):
    size = block.shape[0]
    groups = size // SUB
    lane = lax.broadcasted_iota(jnp.int32, (SUB, size), 1)
    sub = lax.broadcasted_iota(jnp.int32, (SUB, size), 0)
    left = [block[SUB * r : SUB * (r + 1), :] for r in range(groups)]
    right = [(lane == sub + SUB * r).astype(F32) for r in range(groups)]
    tops = []
    lows = []
    for g in range(groups):
        near = min(groups, g + 1 + FAR)
        cols = {r: [spread(left[r], SUB * g + k, 1) for k in range(SUB)] for r in range(g, near)}
        s = [[spread(cols[g][k], i, 0) if i >= k else None for k in range(SUB)] for i in range(SUB)]
        xs = [spread(left[g], k, 0) for k in range(SUB)]
        ys = [spread(right[g], k, 0) for k in range(SUB)]
        inv = []
        for k in range(SUB):
            inv.append(lax.rsqrt(s[k][k]))
            for i in range(k + 1, SUB):
                s[i][k] = s[i][k] * inv[k]
            for j in range(k + 1, SUB):
                for i in range(j, SUB):
                    s[i][j] = s[i][j] - s[i][k] * s[j][k]
            xs[k] = xs[k] * inv[k]
            ys[k] = ys[k] * inv[k]
            for i in range(k + 1, SUB):
                xs[i] = xs[i] - s[i][k] * xs[k]
                ys[i] = ys[i] - s[i][k] * ys[k]
        for r in range(g + 1, near):
            ls = cols[r]
            for k in range(SUB):
                ls[k] = ls[k] * inv[k]
                for j in range(k + 1, SUB):
                    ls[j] = ls[j] - s[j][k] * ls[k]
                left[r] = left[r] - ls[k] * xs[k]
                right[r] = right[r] - ls[k] * ys[k]
        top, low = xs[0], ys[0]
        for k in range(1, SUB):
            top = jnp.where(sub == k, xs[k], top)
            low = jnp.where(sub == k, ys[k], low)
        if near < groups:
            delta = far_product(top, jnp.concatenate([top, low], 1))
            for r in range(near, groups):
                left[r] = left[r] - delta[SUB * r : SUB * (r + 1), :size]
                right[r] = right[r] - delta[SUB * r : SUB * (r + 1), size:]
        tops.append(jnp.where(lane >= sub + SUB * g, top, 0.0))
        lows.append(low)
    return jnp.concatenate(tops, 0), jnp.concatenate(lows, 0)


def run_panels(count, lo, hi, row_of, s_ref, r_ref, t_ref):
    width = t_ref.shape[1]
    start = lo * width

    s_ref[...] = row_of(lo)

    @pl.loop(0, hi - lo)
    def _(k):
        at = pl.multiple_of(k * width, width)
        upper, inverse = diag_factor(s_ref[:, pl.ds(at, width)])
        t_ref[pl.ds(at, width), :] = inverse
        r_ref[pl.ds(at, width), pl.ds(at, width)] = upper
        for kk in range(hi - lo):

            @pl.when(k == kk)
            def _():
                rest = (kk + 1) * width
                r_ref[kk * width : rest, rest:] = dot_nn(t_ref[kk * width : rest, :], s_ref[:, rest:])
                if lo + kk + 1 < hi:
                    s_ref[:, rest:] = row_of(lo + kk + 1) - dot_tn(
                        r_ref[0:rest, rest : rest + width], r_ref[0:rest, rest:]
                    )


def stage_kernel(count, lo, hi, place_ref, own_ref, other_ref, *refs):
    refs = list(refs)
    before = lo > 0
    last = hi == count
    carry_ref = refs.pop(0) if before else None
    if last:
        frame_ref = refs.pop(0)
        earlier = [(refs.pop(0), refs.pop(0)) for _ in range((len(refs) - 6) // 2)]
        rows_ref, est_ref, r_ref, t_ref = refs[:4]
    else:
        r_ref, t_ref, left_ref = refs[:3]
    x_ref, s_ref = refs[-2:]
    width = x_ref.shape[1]
    states = count * width
    kept = upper_blocks(lo, hi, count)
    half = own_ref.shape[0]
    upper = place_ref[1 + CUT_PLACES.index(lo)]
    x_ref[pl.ds(pl.multiple_of(upper * half, SUB), half), :] = own_ref[...]
    x_ref[pl.ds(pl.multiple_of((1 - upper) * half, SUB), half), :] = other_ref[...]

    def taken_before(k):
        return carry_ref[(k - lo) * width : (k - lo + 1) * width, (k - lo) * width :]

    def vec_column(k):
        base = len(kept) * width
        return column_of(x_ref[base + k : base + k + 1, :])

    def row_of(k):
        parts = [x_ref[pl.ds(kept.index((k, j)) * width, width), :] for j in range(k, count)]
        if before:
            parts.append(jnp.zeros((width, width), F32))
            return jnp.concatenate(parts, 1) + taken_before(k)
        return jnp.concatenate(parts + [vec_column(k)], 1)

    run_panels(count, lo, hi, row_of, s_ref, r_ref, t_ref)
    if not last:
        for k in range(hi, count):
            at = (k - lo) * width
            taken = dot_tn(r_ref[:, at : at + width], r_ref[:, at:])
            rows = slice((k - hi) * width, (k - hi + 1) * width)
            if before:
                left_ref[rows, (k - hi) * width :] = taken_before(k) - taken
            else:
                end = states - k * width
                left_ref[rows, (k - hi) * width : states - hi * width] = -taken[:, :end]
                left_ref[rows, states - hi * width :] = vec_column(k) - taken[:, end:]
        return

    owners = []
    groups = []
    for r, t in earlier + [(r_ref, t_ref)]:
        groups.append((r, t, len(owners)))
        owners += [groups[-1]] * (t.shape[0] // width)
    solved = [None] * count
    for k in reversed(range(count)):
        r, t, first = owners[k]
        mine = slice((k - first) * width, (k - first + 1) * width)
        right = r[mine, states - first * width :]
        if k + 1 < count:
            right = right - dot_nn(
                r[mine, (k + 1 - first) * width : states - first * width],
                jnp.concatenate(solved[k + 1 :], 0),
            )
        solved[k] = dot_tn(t[mine, :], right)
    for k in range(count):
        cols = slice(k * width, (k + 1) * width)
        est_ref[:, cols] = solved[k].T[0:1, :] / frame_ref[:, cols]
    share = rows_ref.shape[0]
    mine = place_ref[0] * share
    for r, t, first in groups:
        inside = jnp.logical_and(mine >= first * width, mine < first * width + t.shape[0])

        @pl.when(inside)
        def _(r=r, first=first):
            at = pl.multiple_of(mine - first * width, SUB)
            if first:
                rows_ref[:, : first * width] = jnp.zeros((share, first * width), F32)
            for j in range(first, count):
                cols = slice(j * width, (j + 1) * width)
                row = r[pl.ds(at, share), (j - first) * width : (j - first + 1) * width]
                rows_ref[:, cols] = jnp.where(mine < (j + 1) * width, row * frame_ref[:, cols], 0.0)


def factor_stage(span, place, halves, carry, earlier, frame, count, share):
    lo, hi = span
    width = halves[0].shape[1]
    states = count * width
    rest = states - lo * width
    rows = (hi - lo) * width
    last = hi == count
    vmem = pl.BlockSpec(memory_space=pltpu.VMEM)
    operands = list(halves)
    if lo:
        operands.append(carry)
    parts = [(rows, rest + width), (rows, width)]
    if last:
        operands += [frame] + [x for pair in earlier for x in pair]
        outs = [(share, states), (1, states)]
    else:
        outs = parts + [(states - hi * width, states - hi * width + width)]
    scratch = (parts if last else []) + [(2 * halves[0].shape[0], width), (width, rest + width)]
    return pl.pallas_call(
        functools.partial(stage_kernel, count, lo, hi),
        in_specs=[pl.BlockSpec(memory_space=pltpu.SMEM)] + [vmem] * len(operands),
        out_specs=[vmem] * len(outs),
        out_shape=[jax.ShapeDtypeStruct(shape, F32) for shape in outs],
        scratch_shapes=[pltpu.VMEM(shape, F32) for shape in scratch],
        compiler_params=pltpu.CompilerParams(vmem_limit_bytes=VMEM_BYTES),
        cost_estimate=pl.CostEstimate(
            flops=(hi - lo) * FACTOR_FLOPS, bytes_accessed=8 * halves[0].size, transcendentals=rows
        ),
        name="factor",
    )(place, *operands)


def exchange(x, axis, mask):
    return lax.ppermute(x, axis, [(i, i ^ mask) for i in range(lax.axis_size(axis))])


def after(x, other):
    return lax.optimization_barrier((x, other))[0]


def is_upper(axis, bit):
    return ((lax.axis_index(axis) & bit) != 0).astype(jnp.int32)


def halve(x, axis, bit):
    half = x.shape[0] // 2
    upper = is_upper(axis, bit)
    return (
        lax.dynamic_slice_in_dim(x, upper * half, half, 0),
        lax.dynamic_slice_in_dim(x, (1 - upper) * half, half, 0),
    )


def per_device(values, blocks, noise_scale, readings, available, decay, prior_factor, prior_target):
    states = prior_factor.shape[0]
    width = values.shape[1] // 2
    count = states // width
    sensors = lax.axis_size("sensor")
    steps = lax.axis_size("tm")
    share = states // sensors
    own = lax.axis_index("sensor").astype(jnp.int32)
    time = lax.axis_index("tm")
    bits = [1 << n for n in range(sensors.bit_length() - 1)]
    turned = [bits[1], bits[0]] + bits[2:]
    spans = [(0, CUTS[0]), (CUTS[0], CUTS[1]), (CUTS[1], count)]
    orders = [bits, turned, bits]
    uppers = [is_upper("sensor", order[0]) for order in orders]
    begins = (time == 0).astype(jnp.int32)

    def earlier(x, by):
        return lax.ppermute(x, "tm", [(i, i + by) for i in range(steps - by)])

    rest = (values, blocks.T, noise_scale, readings, available, prior_factor, prior_target)
    halves = list(local_gram(spans[:1], jnp.stack([own, begins, uppers[0]]), *rest, count, sensors))
    place = jnp.stack([own, begins] + uppers[1:])
    place, halves[1] = lax.optimization_barrier((place, halves[1]))
    halves += local_gram(spans[1:], place, *rest, count, sensors)
    decay = after(decay, halves[-1])

    frame = jnp.ones((1, states), F32)
    for by in range(1, steps):
        frame = frame * jnp.where(time >= by, earlier(decay, by), 1.0)
    scales = frame_scales(1.0 / frame, spans, count, width, sensors)

    places = jnp.stack([own] + uppers)
    parts = []

    def stage(step):
        moved = [step(n, part) for n, part in enumerate(parts)]
        for n, (other, combine) in enumerate(moved):
            if n:
                other = after(other, parts[n - 1])
            parts[n] = combine(other)

    def sum_first(n, part):
        return exchange(halves[2 * n + 1], "sensor", orders[n][0]), lambda other: part + other

    def sum_at(level):
        def step(n, part):
            stays, leaves = halve(part, "sensor", orders[n][level])
            return exchange(leaves, "sensor", orders[n][level]), lambda other: stays + other

        return step

    def add_earlier(by):
        return lambda n, part: (earlier(part, by), lambda other: part + other)

    def gather_at(level):
        def step(n, part):
            bit = orders[n][level]

            def combine(other):
                return jnp.where(
                    is_upper("sensor", bit) == 1,
                    jnp.concatenate([other, part], 0),
                    jnp.concatenate([part, other], 0),
                )

            return exchange(part, "sensor", bit), combine

        return step

    parts = halves[0::2]
    stage(sum_first)
    for level in range(1, len(bits)):
        stage(sum_at(level))
    for n, (order, scale) in enumerate(zip(orders, scales)):
        for bit in order:
            scale = halve(scale, "sensor", bit)[0]
        parts[n] = parts[n] * scale
    by = 1
    while by < steps:
        stage(add_earlier(by))
        by *= 2
    for level in reversed(range(1, len(bits))):
        stage(gather_at(level))
    stage(lambda n, part: (exchange(part, "sensor", orders[n][0]), lambda other: (part, other)))
    done = []
    carry = None
    for span, pieces in zip(spans[:-1], parts):
        upper, inverses, carry = factor_stage(span, places, pieces, carry, [], frame, count, share)
        done.append((upper, inverses))
    rows, estimate = factor_stage(spans[-1], places, parts[-1], carry, done, frame, count, share)
    return rows[None], estimate


def solution(mesh):
    placed = (
        P("sensor", None),
        P("sensor", None),
        P("tm", "sensor"),
        P("tm", "sensor"),
        P("tm", "sensor"),
        P("tm", None),
        P(),
        P(),
    )
    return jax.shard_map(
        per_device,
        mesh=mesh,
        in_specs=placed,
        out_specs=(P("tm", "sensor", None), P("tm", None)),
        check_vma=False,
    )
```

time: 233 us -> 166 us (0.71)
  waiting for transfers between devices: 120 us -> 28.7 us
  starting transfers between devices: 18 us -> 50 us
  between operations: 14.1 us -> 1.05 us
  Pallas kernels: 70.3 us -> 78.9 us
  local copies, waits for them, and re-layouts: 6.1 us -> 0.14 us
  other arithmetic: 3.56 us -> 6.69 us
    unnamed x3 -> x0, waiting for transfers between devices: 60.7 us -> none
    all_gather x1 -> x0, waiting for transfers between devices: 52.5 us -> none  [per_device(): packed = lax.all_gather(part, 'sensor', axis=0, tiled=True)]
    ppermute x0 -> x18, starting transfers between devices: none -> 30.7 us  [exchange(): lax.ppermute(x, axis, [(i, i ^ mask) for i in range(lax.axis_size(axis))])]
    ppermute x0 -> x18, waiting for transfers between devices: none -> 27.8 us  [exchange(): lax.ppermute(x, axis, [(i, i ^ mask) for i in range(lax.axis_size(axis))])]
    pallas_call x3 -> x6, Pallas kernels: 70.3 us -> 78.9 us  [the longest x3 52.1 us: factor_stage(): pl.pallas_call(functools.partial(stage_kernel, count, lo, hi), in_specs=[...]
    unnamed x14 -> x18, local copies, waits for them, and re-layouts: 6.02 us -> 0.04 us
    ppermute x5 -> x9, waiting for transfers between devices: 6.53 us -> 0.92 us  [earlier(): return lax.ppermute(x, 'tm', [(i, i + by) for i in range(steps - by)])]
    ppermute x5 -> x9, starting transfers between devices: 17.9 us -> 19.3 us  [earlier(): return lax.ppermute(x, 'tm', [(i, i + by) for i in range(steps - by)])]
  transfers between devices with their start and end apart: 7 -> 27, of which waited for: 5 -> 11; matrix products, arithmetic and copies ran while one was open for 0% -> 3% of each run, Pallas kernels for 1% -> 10%
where the time goes in v2:
time: 166 us; the launch traced here: 165 us
  Pallas kernels  78.9 us (48%)
  starting transfers between devices  50 us (30%)
  waiting for transfers between devices  28.7 us (17%)
  other arithmetic  6.69 us (4%)
    pallas_call x3, Pallas kernels, factor_stage(): pl.pallas_call(functools.partial(stage_kernel, count, lo, hi), in_specs=[...  52.1 us
    ppermute x18, starting transfers between devices, exchange(): lax.ppermute(x, axis, [(i, i ^ mask) for i in range(lax.axis_size(axis))])  30.7 us
    ppermute x18, waiting for transfers between devices, exchange(): lax.ppermute(x, axis, [(i, i ^ mask) for i in range(lax.axis_size(axis))])  27.8 us
    pallas_call x2, Pallas kernels, local_gram(): pl.pallas_call(functools.partial(gram_kernel, count, spans), grid_spec=pl...  24.5 us
    ppermute x9, starting transfers between devices, earlier(): return lax.ppermute(x, 'tm', [(i, i + by) for i in range(steps - by)])  19.3 us
  transfers between devices with their start and end apart: 27, of which 11 were waited for; matrix products, arithmetic and copies ran while one was open for 3% of the time, Pallas kernels for 10%

profile of v2, /device:TPU:0, one launch (start us, length us, event | category | flops | bytes accessed | tf_op | source)
XLA Modules:
  0.0 165.5 jit_solution(7210052740952528856)
XLA Ops:
  0.6 0.6 pad_add_fusion.place_ref
  1.3 0.6 add_add_fusion.1.place_ref
  1.9 11.1 %gram.2 = (f32[992,128]{1,0:T(8,128)}, f32[992,128]{1,0:T(8,128)}) custom-call(s32[3]{0:T(128)} %pad_add_fusion.place_ref, bf16[8192,256]{1,0:T(8,128)(2,1)} %v_ref.3, s32[2,8192]{1,0:T(2,128)} %bitcast.7, f32[1,8192]{1,0:T(1,128)} %n_ref.3, f32[1,8192]{1,0:T(1,128)} %r_ref.3, s32[1,8192]{1,0:T(1,128)} %a_ref.3, f32[1024,1024]{1,0:T(8,128)} %p_ref.3, ...), custom_call_target="tpu_custom_call" | custom-call | flops 4160749568 | bytes 4194304 | tf_op jit(solution)/shard_map/gram/pallas_call | solution.py:135
  13.0 3.0 %collective-permute-start.2 = (f32[992,128]{1,0:T(8,128)}, f32[992,128]{1,0:T(8,128)S(1)}, u32[]{:S(2)}, u32[]{:S(2)}) collective-permute-start(f32[992,128]{1,0:T(8,128)} %get-tuple-element.45), channel_id=1, source_target_pairs={{0,1},{1,0},{2,3},{3,2},{4,5},{5,4},{6,7},{7,6},{8,9},{9,8},{10,11... | collective-permute-start | bytes 1523720 | tf_op jit(solution)/shard_map/ppermute | solution.py:399
  16.0 13.5 %gram.3 = (f32[704,128]{1,0:T(8,128)}, f32[704,128]{1,0:T(8,128)}, f32[640,128]{1,0:T(8,128)}, f32[640,128]{1,0:T(8,128)}) custom-call(s32[4]{0:T(128)} %add_add_fusion.1.place_ref, bf16[8192,256]{1,0:T(8,128)(2,1)} %v_ref.3, s32[2,8192]{1,0:T(2,128)} %bitcast.8, f32[1,8192]{1,0:T(1,128)} %n_ref.3, f32[1,8192]{1,0:T(1,128)} %r_ref.3, s32[1,8192]{1,0:T(1,128)} %a_ref.3, ...), custom_call_target="tpu_custom_call" | custom-call | flops 5637144576 | bytes 4194304 | tf_op jit(solution)/shard_map/gram/pallas_call | solution.py:135
  29.5 1.7 collective-permute-start.1
  31.1 2.2 %collective-permute-start.11 = (f32[1,1024]{1,0:T(1,128)S(1)}, f32[1,1024]{1,0:T(1,128)S(1)}, u32[]{:S(2)}, u32[]{:S(2)}) collective-permute-start(f32[1,1024]{1,0:T(1,128)S(1)} %copy-done.8), channel_id=1, source_target_pairs={{0,24},{1,25},{2,26},{3,27},{4,28},{5,29},{6,30},{7,31}} | collective-permute-start | bytes 12296 | tf_op jit(solution)/shard_map/ppermute | solution.py:436
  33.3 1.8 %collective-permute-start.10 = (f32[1,1024]{1,0:T(1,128)S(1)}, f32[1,1024]{1,0:T(1,128)S(1)}, u32[]{:S(2)}, u32[]{:S(2)}) collective-permute-start(f32[1,1024]{1,0:T(1,128)S(1)} %copy-done.8), channel_id=1, source_target_pairs={{0,16},{8,24},{1,17},{9,25},{2,18},{10,26},{3,19},{11,27},{4,20},{... | collective-permute-start | bytes 12296 | tf_op jit(solution)/shard_map/ppermute | solution.py:436
  35.1 1.5 collective-permute-start.9
  36.8 0.6 collective-permute-start
  37.5 0.5 collective-permute-start.5
  38.0 0.6 broadcast_divide_fusion
  38.6 2.3 %frames.1 = (f32[1984,128]{1,0:T(8,128)}, f32[1408,128]{1,0:T(8,128)}, f32[1280,128]{1,0:T(8,128)}) custom-call(f32[1,1024]{1,0:T(1,128)} %get-tuple-element.78.f_ref), custom_call_target="tpu_custom_call" | custom-call | flops 598016 | bytes 2392064 | tf_op jit(solution)/shard_map/frames/pallas_call | solution.py:183
  40.9 1.0 add.91
  41.9 4.7 %collective-permute-done = f32[640,128]{1,0:T(8,128)S(1)} collective-permute-done((f32[640,128]{1,0:T(8,128)}, f32[640,128]{1,0:T(8,128)S(1)}, u32[]{:S(2)}, u32[]{:S(2)}) %collective-permute-start) | collective-permute-done | bytes 327712 | tf_op jit(solution)/shard_map/ppermute | solution.py:399
  46.7 0.5 collective-permute-start.3
  47.3 0.6 collective-permute-start.4
  47.9 2.7 %collective-permute-start.8 = (f32[248,128]{1,0:T(8,128)S(1)}, f32[248,128]{1,0:T(8,128)S(1)}, u32[]{:S(2)}, u32[]{:S(2)}) collective-permute-start(f32[248,128]{1,0:T(8,128)S(1)} %constant_dynamic-slice_fusion), channel_id=1, source_target_pairs={{0,4},{1,5},{2,6},{3,7},{4,0},{5,1},{6,2},{7,3},{8,12},{9,13},{10,... | collective-permute-start | bytes 380936 | tf_op jit(solution)/shard_map/ppermute | solution.py:399
  50.6 2.2 %collective-permute-done.4 = f32[352,128]{1,0:T(8,128)S(1)} collective-permute-done((f32[352,128]{1,0:T(8,128)S(1)}, f32[352,128]{1,0:T(8,128)S(1)}, u32[]{:S(2)}, u32[]{:S(2)}) %collective-permute-start.4) | collective-permute-done | bytes 180256 | tf_op jit(solution)/shard_map/ppermute | solution.py:399
  52.9 1.6 collective-permute-done.3
  54.4 1.7 %collective-permute-start.7 = (f32[176,128]{1,0:T(8,128)S(1)}, f32[176,128]{1,0:T(8,128)S(1)}, u32[]{:S(2)}, u32[]{:S(2)}) collective-permute-start(f32[176,128]{1,0:T(8,128)S(1)} %constant_dynamic-slice_fusion.1), channel_id=1, source_target_pairs={{0,4},{1,5},{2,6},{3,7},{4,0},{5,1},{6,2},{7,3},{8,12},{9,13},{10,... | collective-permute-start | bytes 270344 | tf_op jit(solution)/shard_map/ppermute | solution.py:399
  56.1 1.0 dynamic-slice_multiply_fusion
  57.1 3.5 %collective-permute-done.7 = f32[176,128]{1,0:T(8,128)S(1)} collective-permute-done((f32[176,128]{1,0:T(8,128)S(1)}, f32[176,128]{1,0:T(8,128)S(1)}, u32[]{:S(2)}, u32[]{:S(2)}) %collective-permute-start.7) | collective-permute-done | bytes 90144 | tf_op jit(solution)/shard_map/ppermute | solution.py:399
  60.6 1.3 collective-permute-start.14
  61.9 0.9 dynamic-slice_multiply_fusion.1
  62.9 1.8 %collective-permute-start.13 = (f32[176,128]{1,0:T(8,128)S(1)}, f32[176,128]{1,0:T(8,128)S(1)}, u32[]{:S(2)}, u32[]{:S(2)}) collective-permute-start(f32[176,128]{1,0:T(8,128)S(1)} %dynamic-slice_multiply_fusion.1), channel_id=1, source_target_pairs={{0,8},{8,16},{16,24},{1,9},{9,17},{17,25},{2,10},{10,18},{18,26},{... | collective-permute-start | bytes 270344 | tf_op jit(solution)/shard_map/ppermute | solution.py:436
  64.7 3.3 %collective-permute-start.17 = (f32[248,128]{1,0:T(8,128)S(1)}, f32[248,128]{1,0:T(8,128)S(1)}, u32[]{:S(2)}, u32[]{:S(2)}) collective-permute-start(f32[248,128]{1,0:T(8,128)S(1)} %add.105), channel_id=1, source_target_pairs={{0,16},{8,24},{1,17},{9,25},{2,18},{10,26},{3,19},{11,27},{4,20},{... | collective-permute-start | bytes 380936 | tf_op jit(solution)/shard_map/ppermute | solution.py:436
  68.4 5.1 %collective-permute-done.6 = f32[160,128]{1,0:T(8,128)S(1)} collective-permute-done((f32[160,128]{1,0:T(8,128)S(1)}, f32[160,128]{1,0:T(8,128)S(1)}, u32[]{:S(2)}, u32[]{:S(2)}) %collective-permute-start.6) | collective-permute-done | bytes 81952 | tf_op jit(solution)/shard_map/ppermute | solution.py:399
  73.5 1.3 collective-permute-start.16
  75.1 0.9 dynamic-slice_multiply_fusion.2
  76.0 1.3 collective-permute-start.12
  77.4 0.9 collective-permute-done.12
  78.3 4.8 %collective-permute-start.15 = (f32[160,128]{1,0:T(8,128)S(1)}, f32[160,128]{1,0:T(8,128)S(1)}, u32[]{:S(2)}, u32[]{:S(2)}) collective-permute-start(f32[160,128]{1,0:T(8,128)S(1)} %add.107), channel_id=1, source_target_pairs={{0,16},{8,24},{1,17},{9,25},{2,18},{10,26},{3,19},{11,27},{4,20},{... | collective-permute-start | bytes 245768 | tf_op jit(solution)/shard_map/ppermute | solution.py:436
  83.1 2.7 %collective-permute-start.19 = (f32[176,128]{1,0:T(8,128)S(1)}, f32[176,128]{1,0:T(8,128)S(1)}, u32[]{:S(2)}, u32[]{:S(2)}) collective-permute-start(f32[176,128]{1,0:T(8,128)S(1)} %add.109), channel_id=1, source_target_pairs={{0,4},{1,5},{2,6},{3,7},{4,0},{5,1},{6,2},{7,3},{8,12},{9,13},{10,... | collective-permute-start | bytes 270344 | tf_op jit(solution)/shard_map/ppermute | solution.py:399
  86.0 2.6 %collective-permute-start.18 = (f32[160,128]{1,0:T(8,128)S(1)}, f32[160,128]{1,0:T(8,128)S(1)}, u32[]{:S(2)}, u32[]{:S(2)}) collective-permute-start(f32[160,128]{1,0:T(8,128)S(1)} %add.110), channel_id=1, source_target_pairs={{0,4},{1,5},{2,6},{3,7},{4,0},{5,1},{6,2},{7,3},{8,12},{9,13},{10,... | collective-permute-start | bytes 245768 | tf_op jit(solution)/shard_map/ppermute | solution.py:399
  88.7 3.2 %collective-permute-start.22 = (f32[352,128]{1,0:T(8,128)S(1)}, f32[352,128]{1,0:T(8,128)S(1)}, u32[]{:S(2)}, u32[]{:S(2)}) collective-permute-start(f32[352,128]{1,0:T(8,128)S(1)} %maximum_select_fusion.4), channel_id=1, source_target_pairs={{0,1},{1,0},{2,3},{3,2},{4,5},{5,4},{6,7},{7,6},{8,9},{9,8},{10,11... | collective-permute-start | bytes 540680 | tf_op jit(solution)/shard_map/ppermute | solution.py:399
  91.9 0.8 collective-permute-done.18
  92.7 3.4 %collective-permute-start.21 = (f32[320,128]{1,0:T(8,128)S(1)}, f32[320,128]{1,0:T(8,128)S(1)}, u32[]{:S(2)}, u32[]{:S(2)}) collective-permute-start(f32[320,128]{1,0:T(8,128)S(1)} %maximum_select_fusion.5), channel_id=1, source_target_pairs={{0,2},{1,3},{2,0},{3,1},{4,6},{5,7},{6,4},{7,5},{8,10},{9,11},{10,... | collective-permute-start | bytes 491528 | tf_op jit(solution)/shard_map/ppermute | solution.py:399
  96.2 4.0 %collective-permute-start.26 = (f32[992,128]{1,0:T(8,128)S(1)}, f32[992,128]{1,0:T(8,128)S(1)}, u32[]{:S(2)}, u32[]{:S(2)}) collective-permute-start(f32[992,128]{1,0:T(8,128)S(1)} %maximum_select_fusion.own_ref), channel_id=1, source_target_pairs={{0,1},{1,0},{2,3},{3,2},{4,5},{5,4},{6,7},{7,6},{8,9},{9,8},{10,11... | collective-permute-start | bytes 1523720 | tf_op jit(solution)/shard_map/ppermute | solution.py:399
  100.6 0.6 collective-permute-done.21
  101.2 2.3 %collective-permute-start.24 = (f32[640,128]{1,0:T(8,128)S(1)}, f32[640,128]{1,0:T(8,128)S(1)}, u32[]{:S(2)}, u32[]{:S(2)}) collective-permute-start(f32[640,128]{1,0:T(8,128)S(1)} %maximum_select_fusion.2.own_ref), channel_id=1, source_target_pairs={{0,1},{1,0},{2,3},{3,2},{4,5},{5,4},{6,7},{7,6},{8,9},{9,8},{10,11... | collective-permute-start | bytes 983048 | tf_op jit(solution)/shard_map/ppermute | solution.py:399
  103.5 0.7 add_add_fusion.place_ref
  104.1 3.6 %collective-permute-done.25.other_ref = f32[704,128]{1,0:T(8,128)S(1)} collective-permute-done((f32[704,128]{1,0:T(8,128)S(1)}, f32[704,128]{1,0:T(8,128)S(1)}, u32[]{:S(2)}, u32[]{:S(2)}) %collective-permute-start.25) | collective-permute-done | bytes 360480 | tf_op jit(solution)/shard_map/ppermute | solution.py:399
  107.7 2.2 %collective-permute-done.26.other_ref = f32[992,128]{1,0:T(8,128)S(1)} collective-permute-done((f32[992,128]{1,0:T(8,128)S(1)}, f32[992,128]{1,0:T(8,128)S(1)}, u32[]{:S(2)}, u32[]{:S(2)}) %collective-permute-start.26) | collective-permute-done | bytes 507936 | tf_op jit(solution)/shard_map/ppermute | solution.py:399
  109.9 3.5 %collective-permute-done.24.other_ref = f32[640,128]{1,0:T(8,128)S(1)} collective-permute-done((f32[640,128]{1,0:T(8,128)S(1)}, f32[640,128]{1,0:T(8,128)S(1)}, u32[]{:S(2)}, u32[]{:S(2)}) %collective-permute-start.24) | collective-permute-done | bytes 327712 | tf_op jit(solution)/shard_map/ppermute | solution.py:399
  113.4 14.0 %factor.3 = (f32[256,1152]{1,0:T(8,128)}, f32[256,128]{1,0:T(8,128)}, f32[768,896]{1,0:T(8,128)}) custom-call(s32[4]{0:T(128)} %add_add_fusion.place_ref, f32[992,128]{1,0:T(8,128)} %copy-done.1, f32[992,128]{1,0:T(8,128)} %copy-done.5), custom_call_target="tpu_custom_call" | custom-call | flops 10000000000 | bytes 1015808 | tf_op jit(solution)/shard_map/factor/pallas_call | solution.py:384
  127.4 13.0 %factor.4 = (f32[256,896]{1,0:T(8,128)}, f32[256,128]{1,0:T(8,128)}, f32[512,640]{1,0:T(8,128)}) custom-call(s32[4]{0:T(128)} %add_add_fusion.place_ref, f32[704,128]{1,0:T(8,128)} %copy-done.2, f32[704,128]{1,0:T(8,128)} %copy-done.6, f32[768,896]{1,0:T(8,128)} %get-tuple-element.66.refs_0_), custom_call_target="tpu_custom_call" | custom-call | flops 10000000000 | bytes 720896 | tf_op jit(solution)/shard_map/factor/pallas_call | solution.py:384
  140.4 25.1 %factor.5 = (f32[128,1024]{1,0:T(8,128)}, f32[1,1024]{1,0:T(1,128)}) custom-call(s32[4]{0:T(128)} %add_add_fusion.place_ref, f32[640,128]{1,0:T(8,128)} %copy-done.3, f32[640,128]{1,0:T(8,128)} %copy-done.7, f32[512,640]{1,0:T(8,128)} %get-tuple-element.67.refs_0_, f32[1,1024]{1,0:T(1,128)} %get-tuple-element.79.refs_1_, ...), custom_call_target="tpu_custom_call" | custom-call | flops 20000000000 | bytes 655360 | tf_op jit(solution)/shard_map/factor/pallas_call | solution.py:384
  (61 shorter events, 1.8 us)
Async XLA Ops:
  13.0 18.2 %copy-start.8 = (f32[1,1024]{1,0:T(1,128)S(1)}, f32[1,1024]{1,0:T(1,128)}, u32[]{:S(2)}) copy-start(f32[1,1024]{1,0:T(1,128)} %param.13) | copy-start | bytes 12292
  13.0 24.4 %copy-start = (f32[992,128]{1,0:T(8,128)S(1)}, f32[992,128]{1,0:T(8,128)}, u32[]{:S(2)}) copy-start(f32[992,128]{1,0:T(8,128)} %get-tuple-element.44) | copy-start | bytes 1523716
  13.0 23.8 %collective-permute-start.2 = (f32[992,128]{1,0:T(8,128)}, f32[992,128]{1,0:T(8,128)S(1)}, u32[]{:S(2)}, u32[]{:S(2)}) collective-permute-start(f32[992,128]{1,0:T(8,128)} %get-tuple-element.45), channel_id=1, source_target_pairs={{0,1},{1,0},{2,3},{3,2},{4,5},{5,4},{6,7},{7,6},{8,9},{9,8},{10,11... | collective-permute-start | bytes 1523720 | tf_op jit(solution)/shard_map/ppermute | solution.py:399
  29.5 17.2 %copy-start.4 = (f32[640,128]{1,0:T(8,128)S(1)}, f32[640,128]{1,0:T(8,128)}, u32[]{:S(2)}) copy-start(f32[640,128]{1,0:T(8,128)} %get-tuple-element.40) | copy-start | bytes 983044
  29.5 11.4 %collective-permute-start.1 = (f32[704,128]{1,0:T(8,128)}, f32[704,128]{1,0:T(8,128)S(1)}, u32[]{:S(2)}, u32[]{:S(2)}) collective-permute-start(f32[704,128]{1,0:T(8,128)} %get-tuple-element.43), channel_id=1, source_target_pairs={{0,2},{1,3},{2,0},{3,1},{4,6},{5,7},{6,4},{7,5},{8,10},{9,11},{10,... | collective-permute-start | bytes 1081352 | tf_op jit(solution)/shard_map/ppermute | solution.py:399
  31.1 6.4 %collective-permute-start.11 = (f32[1,1024]{1,0:T(1,128)S(1)}, f32[1,1024]{1,0:T(1,128)S(1)}, u32[]{:S(2)}, u32[]{:S(2)}) collective-permute-start(f32[1,1024]{1,0:T(1,128)S(1)} %copy-done.8), channel_id=1, source_target_pairs={{0,24},{1,25},{2,26},{3,27},{4,28},{5,29},{6,30},{7,31}} | collective-permute-start | bytes 12296 | tf_op jit(solution)/shard_map/ppermute | solution.py:436
  33.3 4.6 %collective-permute-start.10 = (f32[1,1024]{1,0:T(1,128)S(1)}, f32[1,1024]{1,0:T(1,128)S(1)}, u32[]{:S(2)}, u32[]{:S(2)}) collective-permute-start(f32[1,1024]{1,0:T(1,128)S(1)} %copy-done.8), channel_id=1, source_target_pairs={{0,16},{8,24},{1,17},{9,25},{2,18},{10,26},{3,19},{11,27},{4,20},{... | collective-permute-start | bytes 12296 | tf_op jit(solution)/shard_map/ppermute | solution.py:436
  35.1 2.9 %collective-permute-start.9 = (f32[1,1024]{1,0:T(1,128)S(1)}, f32[1,1024]{1,0:T(1,128)S(1)}, u32[]{:S(2)}, u32[]{:S(2)}) collective-permute-start(f32[1,1024]{1,0:T(1,128)S(1)} %copy-done.8), channel_id=1, source_target_pairs={{0,8},{8,16},{16,24},{1,9},{9,17},{17,25},{2,10},{10,18},{18,26},{... | collective-permute-start | bytes 12296 | tf_op jit(solution)/shard_map/ppermute | solution.py:436
  36.8 9.9 %collective-permute-start = (f32[640,128]{1,0:T(8,128)}, f32[640,128]{1,0:T(8,128)S(1)}, u32[]{:S(2)}, u32[]{:S(2)}) collective-permute-start(f32[640,128]{1,0:T(8,128)} %get-tuple-element.41), channel_id=1, source_target_pairs={{0,1},{1,0},{2,3},{3,2},{4,5},{5,4},{6,7},{7,6},{8,9},{9,8},{10,11... | collective-permute-start | bytes 983048 | tf_op jit(solution)/shard_map/ppermute | solution.py:399
  37.5 10.4 %collective-permute-start.5 = (f32[496,128]{1,0:T(8,128)S(1)}, f32[496,128]{1,0:T(8,128)S(1)}, u32[]{:S(2)}, u32[]{:S(2)}) collective-permute-start(f32[496,128]{1,0:T(8,128)S(1)} %constant_dynamic-slice_fusion.3), channel_id=1, source_target_pairs={{0,2},{1,3},{2,0},{3,1},{4,6},{5,7},{6,4},{7,5},{8,10},{9,11},{10,... | collective-permute-start | bytes 761864 | tf_op jit(solution)/shard_map/ppermute | solution.py:399
  46.7 7.7 %collective-permute-start.3 = (f32[320,128]{1,0:T(8,128)S(1)}, f32[320,128]{1,0:T(8,128)S(1)}, u32[]{:S(2)}, u32[]{:S(2)}) collective-permute-start(f32[320,128]{1,0:T(8,128)S(1)} %constant_dynamic-slice_fusion.5), channel_id=1, source_target_pairs={{0,2},{1,3},{2,0},{3,1},{4,6},{5,7},{6,4},{7,5},{8,10},{9,11},{10,... | collective-permute-start | bytes 491528 | tf_op jit(solution)/shard_map/ppermute | solution.py:399
  47.3 5.6 %collective-permute-start.4 = (f32[352,128]{1,0:T(8,128)S(1)}, f32[352,128]{1,0:T(8,128)S(1)}, u32[]{:S(2)}, u32[]{:S(2)}) collective-permute-start(f32[352,128]{1,0:T(8,128)S(1)} %constant_dynamic-slice_fusion.4), channel_id=1, source_target_pairs={{0,1},{1,0},{2,3},{3,2},{4,5},{5,4},{6,7},{7,6},{8,9},{9,8},{10,11... | collective-permute-start | bytes 540680 | tf_op jit(solution)/shard_map/ppermute | solution.py:399
  47.9 8.2 %collective-permute-start.8 = (f32[248,128]{1,0:T(8,128)S(1)}, f32[248,128]{1,0:T(8,128)S(1)}, u32[]{:S(2)}, u32[]{:S(2)}) collective-permute-start(f32[248,128]{1,0:T(8,128)S(1)} %constant_dynamic-slice_fusion), channel_id=1, source_target_pairs={{0,4},{1,5},{2,6},{3,7},{4,0},{5,1},{6,2},{7,3},{8,12},{9,13},{10,... | collective-permute-start | bytes 380936 | tf_op jit(solution)/shard_map/ppermute | solution.py:399
  54.4 6.2 %collective-permute-start.7 = (f32[176,128]{1,0:T(8,128)S(1)}, f32[176,128]{1,0:T(8,128)S(1)}, u32[]{:S(2)}, u32[]{:S(2)}) collective-permute-start(f32[176,128]{1,0:T(8,128)S(1)} %constant_dynamic-slice_fusion.1), channel_id=1, source_target_pairs={{0,4},{1,5},{2,6},{3,7},{4,0},{5,1},{6,2},{7,3},{8,12},{9,13},{10,... | collective-permute-start | bytes 270344 | tf_op jit(solution)/shard_map/ppermute | solution.py:399
  60.6 4.0 %collective-permute-start.14 = (f32[248,128]{1,0:T(8,128)S(1)}, f32[248,128]{1,0:T(8,128)S(1)}, u32[]{:S(2)}, u32[]{:S(2)}) collective-permute-start(f32[248,128]{1,0:T(8,128)S(1)} %dynamic-slice_multiply_fusion), channel_id=1, source_target_pairs={{0,8},{8,16},{16,24},{1,9},{9,17},{17,25},{2,10},{10,18},{18,26},{... | collective-permute-start | bytes 380936 | tf_op jit(solution)/shard_map/ppermute | solution.py:436
  62.9 10.6 %collective-permute-start.13 = (f32[176,128]{1,0:T(8,128)S(1)}, f32[176,128]{1,0:T(8,128)S(1)}, u32[]{:S(2)}, u32[]{:S(2)}) collective-permute-start(f32[176,128]{1,0:T(8,128)S(1)} %dynamic-slice_multiply_fusion.1), channel_id=1, source_target_pairs={{0,8},{8,16},{16,24},{1,9},{9,17},{17,25},{2,10},{10,18},{18,26},{... | collective-permute-start | bytes 270344 | tf_op jit(solution)/shard_map/ppermute | solution.py:436
  64.7 10.1 %collective-permute-start.17 = (f32[248,128]{1,0:T(8,128)S(1)}, f32[248,128]{1,0:T(8,128)S(1)}, u32[]{:S(2)}, u32[]{:S(2)}) collective-permute-start(f32[248,128]{1,0:T(8,128)S(1)} %add.105), channel_id=1, source_target_pairs={{0,16},{8,24},{1,17},{9,25},{2,18},{10,26},{3,19},{11,27},{4,20},{... | collective-permute-start | bytes 380936 | tf_op jit(solution)/shard_map/ppermute | solution.py:436
  68.0 5.5 %collective-permute-start.6 = (f32[160,128]{1,0:T(8,128)S(1)}, f32[160,128]{1,0:T(8,128)S(1)}, u32[]{:S(2)}, u32[]{:S(2)}) collective-permute-start(f32[160,128]{1,0:T(8,128)S(1)} %constant_dynamic-slice_fusion.2), channel_id=1, source_target_pairs={{0,4},{1,5},{2,6},{3,7},{4,0},{5,1},{6,2},{7,3},{8,12},{9,13},{10,... | collective-permute-start | bytes 245768 | tf_op jit(solution)/shard_map/ppermute | solution.py:399
  73.5 9.7 %collective-permute-start.16 = (f32[176,128]{1,0:T(8,128)S(1)}, f32[176,128]{1,0:T(8,128)S(1)}, u32[]{:S(2)}, u32[]{:S(2)}) collective-permute-start(f32[176,128]{1,0:T(8,128)S(1)} %add.106), channel_id=1, source_target_pairs={{0,16},{8,24},{1,17},{9,25},{2,18},{10,26},{3,19},{11,27},{4,20},{... | collective-permute-start | bytes 270344 | tf_op jit(solution)/shard_map/ppermute | solution.py:436
  74.8 11.1 %collective-permute-start.20 = (f32[248,128]{1,0:T(8,128)S(1)}, f32[248,128]{1,0:T(8,128)S(1)}, u32[]{:S(2)}, u32[]{:S(2)}) collective-permute-start(f32[248,128]{1,0:T(8,128)S(1)} %add.108), channel_id=1, source_target_pairs={{0,4},{1,5},{2,6},{3,7},{4,0},{5,1},{6,2},{7,3},{8,12},{9,13},{10,... | collective-permute-start | bytes 380936 | tf_op jit(solution)/shard_map/ppermute | solution.py:399
  76.0 2.2 %collective-permute-start.12 = (f32[160,128]{1,0:T(8,128)S(1)}, f32[160,128]{1,0:T(8,128)S(1)}, u32[]{:S(2)}, u32[]{:S(2)}) collective-permute-start(f32[160,128]{1,0:T(8,128)S(1)} %dynamic-slice_multiply_fusion.2), channel_id=1, source_target_pairs={{0,8},{8,16},{16,24},{1,9},{9,17},{17,25},{2,10},{10,18},{18,26},{... | collective-permute-start | bytes 245768 | tf_op jit(solution)/shard_map/ppermute | solution.py:436
  78.3 7.7 %collective-permute-start.15 = (f32[160,128]{1,0:T(8,128)S(1)}, f32[160,128]{1,0:T(8,128)S(1)}, u32[]{:S(2)}, u32[]{:S(2)}) collective-permute-start(f32[160,128]{1,0:T(8,128)S(1)} %add.107), channel_id=1, source_target_pairs={{0,16},{8,24},{1,17},{9,25},{2,18},{10,26},{3,19},{11,27},{4,20},{... | collective-permute-start | bytes 245768 | tf_op jit(solution)/shard_map/ppermute | solution.py:436
  83.1 5.6 %collective-permute-start.19 = (f32[176,128]{1,0:T(8,128)S(1)}, f32[176,128]{1,0:T(8,128)S(1)}, u32[]{:S(2)}, u32[]{:S(2)}) collective-permute-start(f32[176,128]{1,0:T(8,128)S(1)} %add.109), channel_id=1, source_target_pairs={{0,4},{1,5},{2,6},{3,7},{4,0},{5,1},{6,2},{7,3},{8,12},{9,13},{10,... | collective-permute-start | bytes 270344 | tf_op jit(solution)/shard_map/ppermute | solution.py:399
  85.9 10.2 %collective-permute-start.23 = (f32[496,128]{1,0:T(8,128)S(1)}, f32[496,128]{1,0:T(8,128)S(1)}, u32[]{:S(2)}, u32[]{:S(2)}) collective-permute-start(f32[496,128]{1,0:T(8,128)S(1)} %maximum_select_fusion.3), channel_id=1, source_target_pairs={{0,2},{1,3},{2,0},{3,1},{4,6},{5,7},{6,4},{7,5},{8,10},{9,11},{10,... | collective-permute-start | bytes 761864 | tf_op jit(solution)/shard_map/ppermute | solution.py:399
  86.0 6.7 %collective-permute-start.18 = (f32[160,128]{1,0:T(8,128)S(1)}, f32[160,128]{1,0:T(8,128)S(1)}, u32[]{:S(2)}, u32[]{:S(2)}) collective-permute-start(f32[160,128]{1,0:T(8,128)S(1)} %add.110), channel_id=1, source_target_pairs={{0,4},{1,5},{2,6},{3,7},{4,0},{5,1},{6,2},{7,3},{8,12},{9,13},{10,... | collective-permute-start | bytes 245768 | tf_op jit(solution)/shard_map/ppermute | solution.py:399
  88.7 11.5 %collective-permute-start.22 = (f32[352,128]{1,0:T(8,128)S(1)}, f32[352,128]{1,0:T(8,128)S(1)}, u32[]{:S(2)}, u32[]{:S(2)}) collective-permute-start(f32[352,128]{1,0:T(8,128)S(1)} %maximum_select_fusion.4), channel_id=1, source_target_pairs={{0,1},{1,0},{2,3},{3,2},{4,5},{5,4},{6,7},{7,6},{8,9},{9,8},{10,11... | collective-permute-start | bytes 540680 | tf_op jit(solution)/shard_map/ppermute | solution.py:399
  92.7 8.4 %collective-permute-start.21 = (f32[320,128]{1,0:T(8,128)S(1)}, f32[320,128]{1,0:T(8,128)S(1)}, u32[]{:S(2)}, u32[]{:S(2)}) collective-permute-start(f32[320,128]{1,0:T(8,128)S(1)} %maximum_select_fusion.5), channel_id=1, source_target_pairs={{0,2},{1,3},{2,0},{3,1},{4,6},{5,7},{6,4},{7,5},{8,10},{9,11},{10,... | collective-permute-start | bytes 491528 | tf_op jit(solution)/shard_map/ppermute | solution.py:399
  96.2 17.2 %copy-start.1 = (f32[992,128]{1,0:T(8,128)}, f32[992,128]{1,0:T(8,128)S(1)}, u32[]{:S(2)}) copy-start(f32[992,128]{1,0:T(8,128)S(1)} %maximum_select_fusion.own_ref) | copy-start | bytes 1523716
  96.2 13.7 %collective-permute-start.26 = (f32[992,128]{1,0:T(8,128)S(1)}, f32[992,128]{1,0:T(8,128)S(1)}, u32[]{:S(2)}, u32[]{:S(2)}) collective-permute-start(f32[992,128]{1,0:T(8,128)S(1)} %maximum_select_fusion.own_ref), channel_id=1, source_target_pairs={{0,1},{1,0},{2,3},{3,2},{4,5},{5,4},{6,7},{7,6},{8,9},{9,8},{10,11... | collective-permute-start | bytes 1523720 | tf_op jit(solution)/shard_map/ppermute | solution.py:399
  100.2 27.2 %copy-start.2 = (f32[704,128]{1,0:T(8,128)}, f32[704,128]{1,0:T(8,128)S(1)}, u32[]{:S(2)}) copy-start(f32[704,128]{1,0:T(8,128)S(1)} %maximum_select_fusion.1.own_ref) | copy-start | bytes 1081348
  100.2 7.5 %collective-permute-start.25 = (f32[704,128]{1,0:T(8,128)S(1)}, f32[704,128]{1,0:T(8,128)S(1)}, u32[]{:S(2)}, u32[]{:S(2)}) collective-permute-start(f32[704,128]{1,0:T(8,128)S(1)} %maximum_select_fusion.1.own_ref), channel_id=1, source_target_pairs={{0,2},{1,3},{2,0},{3,1},{4,6},{5,7},{6,4},{7,5},{8,10},{9,11},{10,... | collective-permute-start | bytes 1081352 | tf_op jit(solution)/shard_map/ppermute | solution.py:399
  101.2 26.3 %copy-start.3 = (f32[640,128]{1,0:T(8,128)}, f32[640,128]{1,0:T(8,128)S(1)}, u32[]{:S(2)}) copy-start(f32[640,128]{1,0:T(8,128)S(1)} %maximum_select_fusion.2.own_ref) | copy-start | bytes 983044
  101.2 12.2 %collective-permute-start.24 = (f32[640,128]{1,0:T(8,128)S(1)}, f32[640,128]{1,0:T(8,128)S(1)}, u32[]{:S(2)}, u32[]{:S(2)}) collective-permute-start(f32[640,128]{1,0:T(8,128)S(1)} %maximum_select_fusion.2.own_ref), channel_id=1, source_target_pairs={{0,1},{1,0},{2,3},{3,2},{4,5},{5,4},{6,7},{7,6},{8,9},{9,8},{10,11... | collective-permute-start | bytes 983048 | tf_op jit(solution)/shard_map/ppermute | solution.py:399
  107.7 19.7 %copy-start.6 = (f32[704,128]{1,0:T(8,128)}, f32[704,128]{1,0:T(8,128)S(1)}, u32[]{:S(2)}) copy-start(f32[704,128]{1,0:T(8,128)S(1)} %collective-permute-done.25.other_ref) | copy-start | bytes 1081348
  109.9 3.5 %copy-start.5 = (f32[992,128]{1,0:T(8,128)}, f32[992,128]{1,0:T(8,128)S(1)}, u32[]{:S(2)}) copy-start(f32[992,128]{1,0:T(8,128)S(1)} %collective-permute-done.26.other_ref) | copy-start | bytes 1523716
  113.4 14.0 %copy-start.7 = (f32[640,128]{1,0:T(8,128)}, f32[640,128]{1,0:T(8,128)S(1)}, u32[]{:S(2)}) copy-start(f32[640,128]{1,0:T(8,128)S(1)} %collective-permute-done.24.other_ref) | copy-start | bytes 983044

commit v3 on v2

--- a/solution.py
+++ b/solution.py
@@ -11,9 +11,11 @@
 SUB = 8
 CHUNK = 2048
 VMEM_BYTES = 60 << 20
-CUTS = (2, 4)
+CUTS = (2,)
 CUT_PLACES = (0,) + CUTS
-FAR = 2
+FAR = 3
+TIED = ()
+TURNED = (1,)
 FACTOR_FLOPS = 5 * 10**9
 BF16 = jnp.bfloat16
 F32 = jnp.float32
@@ -46,7 +48,7 @@
 
 
 def gram_kernel(
-    count, spans, place_ref, v_ref, b_ref, n_ref, r_ref, a_ref, p_ref, t_ref, *refs
+    count, spans, number, place_ref, v_ref, b_ref, n_ref, r_ref, a_ref, p_ref, t_ref, *refs
 ):
     out_refs = refs[: 2 * len(spans)]
     packed_refs = refs[2 * len(spans) : 3 * len(spans)]
@@ -111,7 +113,7 @@
                 for i in range(count):
                     packed_ref[base + i : base + i + 1, :] = vec[:, i * width : (i + 1) * width]
             half = packed_ref.shape[0] // 2
-            upper = place_ref[2 + n]
+            upper = place_ref[2 + number + n]
             out_refs[2 * n][...] = packed_ref[pl.ds(pl.multiple_of(upper * half, SUB), half), :]
             out_refs[2 * n + 1][...] = packed_ref[
                 pl.ds(pl.multiple_of((1 - upper) * half, SUB), half), :
@@ -122,7 +124,7 @@
     return len(upper_blocks(lo, hi, count)) * width + (SUB * sensors if lo == 0 else 0)
 
 
-def local_gram(spans, place, values, blocks, noise, reading, avail, prior, target, count, sensors):
+def local_gram(spans, number, place, values, blocks, noise, reading, avail, prior, target, count, sensors):
     rows, pair = values.shape
     width = pair // 2
     lo, hi = spans[0][0], spans[-1][1]
@@ -133,7 +135,7 @@
     line = pl.BlockSpec((1, chunk), lambda c, place: (0, c))
     halves = [total // 2 for total in totals for _ in range(2)]
     return pl.pallas_call(
-        functools.partial(gram_kernel, count, spans),
+        functools.partial(gram_kernel, count, spans, number),
         grid_spec=pltpu.PrefetchScalarGridSpec(
             num_scalar_prefetch=1,
             grid=(rows // chunk,),
@@ -163,29 +165,38 @@
     )(place, values, blocks, noise, reading, avail, prior, target.reshape(sensors, 1, share))
 
 
-def frame_kernel(count, spans, f_ref, *out_refs):
+def decay_kernel(count, spans, place_ref, f_ref, *refs):
+    out_refs, packed_refs = refs[: len(spans)], refs[len(spans) :]
     width = out_refs[0].shape[1]
     parts = [f_ref[:, i * width : (i + 1) * width] for i in range(count)]
-    for (lo, hi), out_ref in zip(spans, out_refs):
+    for n, (lo, hi) in enumerate(spans):
+        packed_ref, out_ref = packed_refs[n], out_refs[n]
         kept = upper_blocks(lo, hi, count)
-        for n, (i, j) in enumerate(kept):
-            out_ref[n * width : (n + 1) * width, :] = column_of(parts[i]) * parts[j]
+        for m, (i, j) in enumerate(kept):
+            packed_ref[m * width : (m + 1) * width, :] = column_of(parts[i]) * parts[j]
         base = len(kept) * width
         if lo == 0:
-            out_ref[base:, :] = jnp.zeros((out_ref.shape[0] - base, width), F32)
+            packed_ref[base:, :] = jnp.zeros((packed_ref.shape[0] - base, width), F32)
             for i in range(count):
-                out_ref[base + i : base + i + 1, :] = parts[i]
-
-
-def frame_scales(inverse, spans, count, width, sensors):
-    shapes = [(packed_rows(lo, hi, count, width, sensors), width) for lo, hi in spans]
-    size = sum(rows * width for rows, width in shapes)
+                packed_ref[base + i : base + i + 1, :] = parts[i]
+        at = pl.multiple_of(place_ref[2 + len(spans) + n], SUB)
+        out_ref[...] = packed_ref[pl.ds(at, out_ref.shape[0]), :]
+
+
+def decay_pieces(place, decay, spans, count, width, sensors):
+    totals = [packed_rows(lo, hi, count, width, sensors) for lo, hi in spans]
+    vmem = pl.BlockSpec(memory_space=pltpu.VMEM)
+    size = sum(totals) * width
     return pl.pallas_call(
-        functools.partial(frame_kernel, count, spans),
-        out_shape=[jax.ShapeDtypeStruct(shape, F32) for shape in shapes],
-        cost_estimate=pl.CostEstimate(flops=size, bytes_accessed=size * 4, transcendentals=0),
-        name="frames",
-    )(inverse)
+        functools.partial(decay_kernel, count, spans),
+        in_specs=[pl.BlockSpec(memory_space=pltpu.SMEM), vmem],
+        out_specs=[vmem] * len(spans),
+        out_shape=[jax.ShapeDtypeStruct((total // sensors, width), F32) for total in totals],
+        scratch_shapes=[pltpu.VMEM((total, width), F32) for total in totals],
+        cost_estimate=pl.CostEstimate(flops=size, bytes_accessed=size, transcendentals=0),
+        compiler_params=pltpu.CompilerParams(vmem_limit_bytes=VMEM_BYTES),
+        name="decays",
+    )(place, decay)
 
 
 def spread(x, index, axis):
@@ -218,34 +229,32 @@
     for g in range(groups):
         near = min(groups, g + 1 + FAR)
         cols = {r: [spread(left[r], SUB * g + k, 1) for k in range(SUB)] for r in range(g, near)}
-        s = [[spread(cols[g][k], i, 0) if i >= k else None for k in range(SUB)] for i in range(SUB)]
-        xs = [spread(left[g], k, 0) for k in range(SUB)]
-        ys = [spread(right[g], k, 0) for k in range(SUB)]
-        inv = []
+        mine, top, low = cols[g], left[g], right[g]
+        inv, xs, ys = [], [], []
+        below = [[None] * SUB for _ in range(SUB)]
         for k in range(SUB):
-            inv.append(lax.rsqrt(s[k][k]))
+            inv.append(spread(lax.rsqrt(mine[k]), k, 0))
+            mine[k] = mine[k] * inv[k]
             for i in range(k + 1, SUB):
-                s[i][k] = s[i][k] * inv[k]
-            for j in range(k + 1, SUB):
-                for i in range(j, SUB):
-                    s[i][j] = s[i][j] - s[i][k] * s[j][k]
-            xs[k] = xs[k] * inv[k]
-            ys[k] = ys[k] * inv[k]
-            for i in range(k + 1, SUB):
-                xs[i] = xs[i] - s[i][k] * xs[k]
-                ys[i] = ys[i] - s[i][k] * ys[k]
+                below[i][k] = spread(mine[k], i, 0)
+                mine[i] = mine[i] - mine[k] * below[i][k]
+            xs.append(spread(top, k, 0) * inv[k])
+            ys.append(spread(low, k, 0) * inv[k])
+            under = jnp.where(sub > k, mine[k], 0.0)
+            top = top - under * xs[k]
+            low = low - under * ys[k]
         for r in range(g + 1, near):
             ls = cols[r]
             for k in range(SUB):
                 ls[k] = ls[k] * inv[k]
                 for j in range(k + 1, SUB):
-                    ls[j] = ls[j] - s[j][k] * ls[k]
+                    ls[j] = ls[j] - below[j][k] * ls[k]
                 left[r] = left[r] - ls[k] * xs[k]
                 right[r] = right[r] - ls[k] * ys[k]
-        top, low = xs[0], ys[0]
+        scale = inv[0]
         for k in range(1, SUB):
-            top = jnp.where(sub == k, xs[k], top)
-            low = jnp.where(sub == k, ys[k], low)
+            scale = jnp.where(sub == k, inv[k], scale)
+        top, low = top * scale, low * scale
         if near < groups:
             delta = far_product(top, jnp.concatenate([top, low], 1))
             for r in range(near, groups):
@@ -286,7 +295,6 @@
     last = hi == count
     carry_ref = refs.pop(0) if before else None
     if last:
-        frame_ref = refs.pop(0)
         earlier = [(refs.pop(0), refs.pop(0)) for _ in range((len(refs) - 6) // 2)]
         rows_ref, est_ref, r_ref, t_ref = refs[:4]
     else:
@@ -296,7 +304,7 @@
     states = count * width
     kept = upper_blocks(lo, hi, count)
     half = own_ref.shape[0]
-    upper = place_ref[1 + CUT_PLACES.index(lo)]
+    upper = place_ref[2 + CUT_PLACES.index(lo)]
     x_ref[pl.ds(pl.multiple_of(upper * half, SUB), half), :] = own_ref[...]
     x_ref[pl.ds(pl.multiple_of((1 - upper) * half, SUB), half), :] = other_ref[...]
 
@@ -333,20 +341,18 @@
     for r, t in earlier + [(r_ref, t_ref)]:
         groups.append((r, t, len(owners)))
         owners += [groups[-1]] * (t.shape[0] // width)
-    solved = [None] * count
+    taken = [jnp.zeros((width, width), F32)] * count
     for k in reversed(range(count)):
         r, t, first = owners[k]
         mine = slice((k - first) * width, (k - first + 1) * width)
-        right = r[mine, states - first * width :]
-        if k + 1 < count:
-            right = right - dot_nn(
-                r[mine, (k + 1 - first) * width : states - first * width],
-                jnp.concatenate(solved[k + 1 :], 0),
-            )
-        solved[k] = dot_tn(t[mine, :], right)
-    for k in range(count):
+        right = r[mine, states - first * width :] - jnp.sum(taken[k], axis=1, keepdims=True)
+        solved = jnp.sum(t[mine, :] * right, axis=0, keepdims=True)
         cols = slice(k * width, (k + 1) * width)
-        est_ref[:, cols] = solved[k].T[0:1, :] / frame_ref[:, cols]
+        est_ref[:, cols] = solved
+        for i in range(k):
+            r, t, first = owners[i]
+            rows = slice((i - first) * width, (i - first + 1) * width)
+            taken[i] = taken[i] + r[rows, (k - first) * width : (k - first + 1) * width] * solved
     share = rows_ref.shape[0]
     mine = place_ref[0] * share
     for r, t, first in groups:
@@ -360,10 +366,10 @@
             for j in range(first, count):
                 cols = slice(j * width, (j + 1) * width)
                 row = r[pl.ds(at, share), (j - first) * width : (j - first + 1) * width]
-                rows_ref[:, cols] = jnp.where(mine < (j + 1) * width, row * frame_ref[:, cols], 0.0)
-
-
-def factor_stage(span, place, halves, carry, earlier, frame, count, share):
+                rows_ref[:, cols] = jnp.where(mine < (j + 1) * width, row, 0.0)
+
+
+def factor_stage(span, place, halves, carry, earlier, count, share):
     lo, hi = span
     width = halves[0].shape[1]
     states = count * width
@@ -376,7 +382,7 @@
         operands.append(carry)
     parts = [(rows, rest + width), (rows, width)]
     if last:
-        operands += [frame] + [x for pair in earlier for x in pair]
+        operands += [x for pair in earlier for x in pair]
         outs = [(share, states), (1, states)]
     else:
         outs = parts + [(states - hi * width, states - hi * width + width)]
@@ -427,8 +433,8 @@
     time = lax.axis_index("tm")
     bits = [1 << n for n in range(sensors.bit_length() - 1)]
     turned = [bits[1], bits[0]] + bits[2:]
-    spans = [(0, CUTS[0]), (CUTS[0], CUTS[1]), (CUTS[1], count)]
-    orders = [bits, turned, bits]
+    spans = list(zip((0,) + CUTS, CUTS + (count,)))
+    orders = [turned if n in TURNED else bits for n in range(len(spans))]
     uppers = [is_upper("sensor", order[0]) for order in orders]
     begins = (time == 0).astype(jnp.int32)
 
@@ -436,24 +442,25 @@
         return lax.ppermute(x, "tm", [(i, i + by) for i in range(steps - by)])
 
     rest = (values, blocks.T, noise_scale, readings, available, prior_factor, prior_target)
-    halves = list(local_gram(spans[:1], jnp.stack([own, begins, uppers[0]]), *rest, count, sensors))
-    place = jnp.stack([own, begins] + uppers[1:])
-    place, halves[1] = lax.optimization_barrier((place, halves[1]))
-    halves += local_gram(spans[1:], place, *rest, count, sensors)
+    sizes = [packed_rows(lo, hi, count, width, sensors) for lo, hi in spans]
+    offsets = [
+        sum(is_upper("sensor", bit) * (size >> (n + 1)) for n, bit in enumerate(order))
+        for size, order in zip(sizes, orders)
+    ]
+    place = jnp.stack([own, begins] + uppers + offsets)
+    halves = list(local_gram(spans[:1], 0, place, *rest, count, sensors))
+    later, halves[1] = lax.optimization_barrier((place, halves[1]))
+    halves += local_gram(spans[1:], 1, later, *rest, count, sensors)
+    own_decay = decay_pieces(place, decay, spans, count, width, sensors)
     decay = after(decay, halves[-1])
-
-    frame = jnp.ones((1, states), F32)
-    for by in range(1, steps):
-        frame = frame * jnp.where(time >= by, earlier(decay, by), 1.0)
-    scales = frame_scales(1.0 / frame, spans, count, width, sensors)
-
-    places = jnp.stack([own] + uppers)
+    shifted = {gap: earlier(decay, gap) for gap in range(1, steps // 2)}
+
     parts = []
 
     def stage(step):
         moved = [step(n, part) for n, part in enumerate(parts)]
         for n, (other, combine) in enumerate(moved):
-            if n:
+            if n and n in TIED:
                 other = after(other, parts[n - 1])
             parts[n] = combine(other)
 
@@ -468,7 +475,18 @@
         return step
 
     def add_earlier(by):
-        return lambda n, part: (earlier(part, by), lambda other: part + other)
+        between = 1.0
+        for gap in range(1, by):
+            between = between * shifted[gap]
+        decays = decay_pieces(place, between, spans, count, width, sensors) if by > 1 else None
+
+        def step(n, part):
+            other = earlier(part * own_decay[n], by)
+            if by > 1:
+                other = other * decays[n]
+            return other, lambda other: part + other
+
+        return step
 
     def gather_at(level):
         def step(n, part):
@@ -487,12 +505,11 @@
 
     parts = halves[0::2]
     stage(sum_first)
-    for level in range(1, len(bits)):
+
+    stage(sum_at(1))
+
+    for level in range(2, len(bits)):
         stage(sum_at(level))
-    for n, (order, scale) in enumerate(zip(orders, scales)):
-        for bit in order:
-            scale = halve(scale, "sensor", bit)[0]
-        parts[n] = parts[n] * scale
     by = 1
     while by < steps:
         stage(add_earlier(by))
@@ -503,9 +520,9 @@
     done = []
     carry = None
     for span, pieces in zip(spans[:-1], parts):
-        upper, inverses, carry = factor_stage(span, places, pieces, carry, [], frame, count, share)
+        upper, inverses, carry = factor_stage(span, place, pieces, carry, [], count, share)
         done.append((upper, inverses))
-    rows, estimate = factor_stage(spans[-1], places, parts[-1], carry, done, frame, count, share)
+    rows, estimate = factor_stage(spans[-1], place, parts[-1], carry, done, count, share)
     return rows[None], estimate
 
 

time: 166 us -> 152 us (0.916)
  starting transfers between devices: 50 us -> 25.7 us
  waiting for transfers between devices: 28.7 us -> 52.3 us
  Pallas kernels: 78.9 us -> 68.2 us
  other arithmetic: 6.69 us -> 1.7 us
  local copies, waits for them, and re-layouts: 0.14 us -> 2.99 us
    ppermute x18 -> x12, waiting for transfers between devices: 27.8 us -> 49.5 us  [exchange(): lax.ppermute(x, axis, [(i, i ^ mask) for i in range(lax.axis_size(axis))])]
    ppermute x18 -> x12, starting transfers between devices: 30.7 us -> 13.1 us  [exchange(): lax.ppermute(x, axis, [(i, i ^ mask) for i in range(lax.axis_size(axis))])]
    pallas_call x3 -> x2, Pallas kernels: 52.1 us -> 40.3 us  [factor_stage(): pl.pallas_call(functools.partial(stage_kernel, count, lo, hi), in_specs=[...]
    ppermute x9 -> x5, starting transfers between devices: 19.3 us -> 12.6 us  [earlier(): return lax.ppermute(x, 'tm', [(i, i + by) for i in range(steps - by)])]
    mul x3 -> x4, other arithmetic: 2.78 us -> 0.17 us  [step(): other = earlier(part * own_decay[n], by)]
    unnamed x18 -> x22, local copies, waits for them, and re-layouts: 0.04 us -> 2.27 us
    another operation x3 -> x0, other arithmetic: 1.88 us -> none  [the longest x1 0.65 us: per_device(): places = jnp.stack([own] + uppers)]
    ppermute x9 -> x5, waiting for transfers between devices: 0.92 us -> 2.79 us  [earlier(): return lax.ppermute(x, 'tm', [(i, i + by) for i in range(steps - by)])]
  transfers between devices with their start and end apart: 27 -> 17, of which waited for: 11 -> 12; matrix products, arithmetic and copies ran while one was open for 3% -> 1% of each run, Pallas kernels for 10% -> 19%
where the time goes in v3:
time: 152 us
  Pallas kernels  68.2 us (45%)
  waiting for transfers between devices  52.3 us (34%)
  starting transfers between devices  25.7 us (17%)
  local copies, waits for them, and re-layouts  2.99 us (2%)
  other arithmetic  1.7 us (1%)
    ppermute x12, waiting for transfers between devices, exchange(): lax.ppermute(x, axis, [(i, i ^ mask) for i in range(lax.axis_size(axis))])  49.5 us
    pallas_call x2, Pallas kernels, factor_stage(): pl.pallas_call(functools.partial(stage_kernel, count, lo, hi), in_specs=[...  40.3 us
    pallas_call x2, Pallas kernels, local_gram(): pl.pallas_call(functools.partial(gram_kernel, count, spans, number), grid...  24.6 us
    ppermute x12, starting transfers between devices, exchange(): lax.ppermute(x, axis, [(i, i ^ mask) for i in range(lax.axis_size(axis))])  13.1 us
    ppermute x5, starting transfers between devices, earlier(): return lax.ppermute(x, 'tm', [(i, i + by) for i in range(steps - by)])  12.6 us
    pallas_call x2, Pallas kernels, decay_pieces(): pl.pallas_call(functools.partial(decay_kernel, count, spans), in_specs=[p...  3.33 us
  transfers between devices with their start and end apart: 17, of which 12 were waited for; matrix products, arithmetic and copies ran while one was open for 1% of the time, Pallas kernels for 19%

profile of v3, /device:TPU:0, one launch (start us, length us, event | category | flops | bytes accessed | tf_op | source)
XLA Modules:
  0.0 151.7 jit_solution(14163354247297798712)
XLA Ops:
  0.7 0.6 stack.31.place_ref
  1.3 11.1 %gram.2 = (f32[992,128]{1,0:T(8,128)}, f32[992,128]{1,0:T(8,128)}) custom-call(s32[6]{0:T(128)} %stack.31.place_ref, bf16[8192,256]{1,0:T(8,128)(2,1)} %v_ref.3, s32[2,8192]{1,0:T(2,128)} %bitcast.9, f32[1,8192]{1,0:T(1,128)} %n_ref.3, f32[1,8192]{1,0:T(1,128)} %r_ref.3, s32[1,8192]{1,0:T(1,128)} %a_ref.3, f32[1024,1024]{1,0:T(8,128)} %p_ref.3, ...), custom_call_target="tpu_custom_call" | custom-call | flops 4160749568 | bytes 4194304 | tf_op jit(solution)/shard_map/gram/pallas_call | solution.py:137
  12.4 3.0 %collective-permute-start.9 = (f32[992,128]{1,0:T(8,128)}, f32[992,128]{1,0:T(8,128)S(1)}, u32[]{:S(2)}, u32[]{:S(2)}) collective-permute-start(f32[992,128]{1,0:T(8,128)} %get-tuple-element.26), channel_id=1, source_target_pairs={{0,1},{1,0},{2,3},{3,2},{4,5},{5,4},{6,7},{7,6},{8,9},{9,8},{10,11... | collective-permute-start | bytes 1523720 | tf_op jit(solution)/shard_map/ppermute | solution.py:405
  15.4 13.5 %gram.3 = (f32[1344,128]{1,0:T(8,128)}, f32[1344,128]{1,0:T(8,128)}) custom-call(s32[6]{0:T(128)} %stack.31.place_ref, bf16[8192,256]{1,0:T(8,128)(2,1)} %v_ref.3, s32[2,8192]{1,0:T(2,128)} %bitcast.10, f32[1,8192]{1,0:T(1,128)} %n_ref.3, f32[1,8192]{1,0:T(1,128)} %r_ref.3, s32[1,8192]{1,0:T(1,128)} %a_ref.3, f32[1024,1024]{1,0:T(8,128)} %p_ref.3, ...), custom_call_target="tpu_custom_call" | custom-call | flops 5637144576 | bytes 4194304 | tf_op jit(solution)/shard_map/gram/pallas_call | solution.py:137
  28.9 1.6 %collective-permute-start = (f32[1344,128]{1,0:T(8,128)}, f32[1344,128]{1,0:T(8,128)S(1)}, u32[]{:S(2)}, u32[]{:S(2)}) collective-permute-start(f32[1344,128]{1,0:T(8,128)} %get-tuple-element.21), channel_id=1, source_target_pairs={{0,2},{1,3},{2,0},{3,1},{4,6},{5,7},{6,4},{7,5},{8,10},{9,11},{10,... | collective-permute-start | bytes 2064392 | tf_op jit(solution)/shard_map/ppermute | solution.py:405
  30.5 0.0 collective-permute-done.9
  30.5 0.1 add.69
  30.6 0.5 collective-permute-start.10
  31.1 1.3 collective-permute-start.5
  32.4 1.7 %decays.2 = (f32[248,128]{1,0:T(8,128)}, f32[336,128]{1,0:T(8,128)}) custom-call(s32[6]{0:T(128)} %stack.31.place_ref, f32[1,1024]{1,0:T(1,128)} %f_ref.1), custom_call_target="tpu_custom_call" | custom-call | flops 598016 | bytes 598016 | tf_op jit(solution)/shard_map/decays/pallas_call | solution.py:190
  34.0 0.0 collective-permute-done.5.f_ref
  34.1 0.0 copy-start.8
  34.1 0.6 copy-done.8
  34.7 1.7 %decays.3 = (f32[248,128]{1,0:T(8,128)}, f32[336,128]{1,0:T(8,128)}) custom-call(s32[6]{0:T(128)} %stack.31.place_ref, f32[1,1024]{1,0:T(1,128)} %copy-done.8), custom_call_target="tpu_custom_call" | custom-call | flops 598016 | bytes 598016 | tf_op jit(solution)/shard_map/decays/pallas_call | solution.py:190
  36.3 11.1 %collective-permute-done = f32[1344,128]{1,0:T(8,128)S(1)} collective-permute-done((f32[1344,128]{1,0:T(8,128)}, f32[1344,128]{1,0:T(8,128)S(1)}, u32[]{:S(2)}, u32[]{:S(2)}) %collective-permute-start) | collective-permute-done | bytes 688160 | tf_op jit(solution)/shard_map/ppermute | solution.py:405
  47.5 1.2 add.62
  48.7 0.2 collective-permute-start.1
  48.9 2.5 %collective-permute-done.10 = f32[496,128]{1,0:T(8,128)S(1)} collective-permute-done((f32[496,128]{1,0:T(8,128)S(1)}, f32[496,128]{1,0:T(8,128)S(1)}, u32[]{:S(2)}, u32[]{:S(2)}) %collective-permute-start.10) | collective-permute-done | bytes 253984 | tf_op jit(solution)/shard_map/ppermute | solution.py:405
  51.5 2.7 %collective-permute-start.11 = (f32[248,128]{1,0:T(8,128)S(1)}, f32[248,128]{1,0:T(8,128)S(1)}, u32[]{:S(2)}, u32[]{:S(2)}) collective-permute-start(f32[248,128]{1,0:T(8,128)S(1)} %constant_dynamic-slice_fusion), channel_id=1, source_target_pairs={{0,4},{1,5},{2,6},{3,7},{4,0},{5,1},{6,2},{7,3},{8,12},{9,13},{10,... | collective-permute-start | bytes 380936 | tf_op jit(solution)/shard_map/ppermute | solution.py:405
  54.1 1.9 %collective-permute-done.1 = f32[672,128]{1,0:T(8,128)S(1)} collective-permute-done((f32[672,128]{1,0:T(8,128)S(1)}, f32[672,128]{1,0:T(8,128)S(1)}, u32[]{:S(2)}, u32[]{:S(2)}) %collective-permute-start.1) | collective-permute-done | bytes 344096 | tf_op jit(solution)/shard_map/ppermute | solution.py:405
  56.1 2.7 %collective-permute-start.2 = (f32[336,128]{1,0:T(8,128)S(1)}, f32[336,128]{1,0:T(8,128)S(1)}, u32[]{:S(2)}, u32[]{:S(2)}) collective-permute-start(f32[336,128]{1,0:T(8,128)S(1)} %constant_dynamic-slice_fusion.2), channel_id=1, source_target_pairs={{0,4},{1,5},{2,6},{3,7},{4,0},{5,1},{6,2},{7,3},{8,12},{9,13},{10,... | collective-permute-start | bytes 516104 | tf_op jit(solution)/shard_map/ppermute | solution.py:405
  58.8 5.2 %collective-permute-done.11 = f32[248,128]{1,0:T(8,128)S(1)} collective-permute-done((f32[248,128]{1,0:T(8,128)S(1)}, f32[248,128]{1,0:T(8,128)S(1)}, u32[]{:S(2)}, u32[]{:S(2)}) %collective-permute-start.11) | collective-permute-done | bytes 127008 | tf_op jit(solution)/shard_map/ppermute | solution.py:405
  64.0 1.3 collective-permute-start.12
  65.4 1.2 collective-permute-done.2
  66.5 3.0 %collective-permute-start.3 = (f32[336,128]{1,0:T(8,128)S(1)}, f32[336,128]{1,0:T(8,128)S(1)}, u32[]{:S(2)}, u32[]{:S(2)}) collective-permute-start(f32[336,128]{1,0:T(8,128)S(1)} %fusion.1), channel_id=1, source_target_pairs={{0,8},{8,16},{16,24},{1,9},{9,17},{17,25},{2,10},{10,18},{18,26},{... | collective-permute-start | bytes 516104 | tf_op jit(solution)/shard_map/ppermute | solution.py:442
  69.5 0.0 collective-permute-done.12
  69.6 4.1 %collective-permute-start.13 = (f32[248,128]{1,0:T(8,128)S(1)}, f32[248,128]{1,0:T(8,128)S(1)}, u32[]{:S(2)}, u32[]{:S(2)}) collective-permute-start(f32[248,128]{1,0:T(8,128)S(1)} %get-tuple-element.34), channel_id=1, source_target_pairs={{0,16},{8,24},{1,17},{9,25},{2,18},{10,26},{3,19},{11,27},{4,20},{... | collective-permute-start | bytes 380936 | tf_op jit(solution)/shard_map/ppermute | solution.py:442
  73.7 0.0 collective-permute-done.3
  73.7 0.1 fusion.6
  73.8 2.9 %collective-permute-start.4 = (f32[336,128]{1,0:T(8,128)S(1)}, f32[336,128]{1,0:T(8,128)S(1)}, u32[]{:S(2)}, u32[]{:S(2)}) collective-permute-start(f32[336,128]{1,0:T(8,128)S(1)} %get-tuple-element.36), channel_id=1, source_target_pairs={{0,16},{8,24},{1,17},{9,25},{2,18},{10,26},{3,19},{11,27},{4,20},{... | collective-permute-start | bytes 516104 | tf_op jit(solution)/shard_map/ppermute | solution.py:442
  76.7 0.6 collective-permute-done.13
  77.4 0.1 collective-permute-start.14
  77.4 2.2 %collective-permute-done.4 = f32[336,128]{1,0:T(8,128)S(1)} collective-permute-done((f32[336,128]{1,0:T(8,128)S(1)}, f32[336,128]{1,0:T(8,128)S(1)}, u32[]{:S(2)}, u32[]{:S(2)}) %collective-permute-start.4) | collective-permute-done | bytes 172064 | tf_op jit(solution)/shard_map/ppermute | solution.py:442
  79.7 0.8 collective-permute-start.6
  80.5 8.7 %collective-permute-done.14 = f32[248,128]{1,0:T(8,128)S(1)} collective-permute-done((f32[248,128]{1,0:T(8,128)S(1)}, f32[248,128]{1,0:T(8,128)S(1)}, u32[]{:S(2)}, u32[]{:S(2)}) %collective-permute-start.14) | collective-permute-done | bytes 127008 | tf_op jit(solution)/shard_map/ppermute | solution.py:405
  89.2 0.1 collective-permute-start.15
  89.3 1.7 %collective-permute-done.6 = f32[336,128]{1,0:T(8,128)S(1)} collective-permute-done((f32[336,128]{1,0:T(8,128)S(1)}, f32[336,128]{1,0:T(8,128)S(1)}, u32[]{:S(2)}, u32[]{:S(2)}) %collective-permute-start.6) | collective-permute-done | bytes 172064 | tf_op jit(solution)/shard_map/ppermute | solution.py:405
  91.0 0.6 collective-permute-start.7
  91.6 3.9 %collective-permute-done.15 = f32[496,128]{1,0:T(8,128)S(1)} collective-permute-done((f32[496,128]{1,0:T(8,128)S(1)}, f32[496,128]{1,0:T(8,128)S(1)}, u32[]{:S(2)}, u32[]{:S(2)}) %collective-permute-start.15) | collective-permute-done | bytes 253984 | tf_op jit(solution)/shard_map/ppermute | solution.py:405
  95.6 0.0 copy-start.2
  95.6 0.6 collective-permute-start.16
  96.2 5.9 %collective-permute-done.7 = f32[672,128]{1,0:T(8,128)S(1)} collective-permute-done((f32[672,128]{1,0:T(8,128)S(1)}, f32[672,128]{1,0:T(8,128)S(1)}, u32[]{:S(2)}, u32[]{:S(2)}) %collective-permute-start.7) | collective-permute-done | bytes 344096 | tf_op jit(solution)/shard_map/ppermute | solution.py:405
  102.2 0.3 collective-permute-start.8
  102.5 7.2 %collective-permute-done.16.other_ref = f32[992,128]{1,0:T(8,128)S(1)} collective-permute-done((f32[992,128]{1,0:T(8,128)S(1)}, f32[992,128]{1,0:T(8,128)S(1)}, u32[]{:S(2)}, u32[]{:S(2)}) %collective-permute-start.16) | collective-permute-done | bytes 507936 | tf_op jit(solution)/shard_map/ppermute | solution.py:405
  109.8 0.8 copy-done.10
  110.5 12.8 %factor.2 = (f32[256,1152]{1,0:T(8,128)}, f32[256,128]{1,0:T(8,128)}, f32[768,896]{1,0:T(8,128)}) custom-call(s32[6]{0:T(128)} %stack.31.place_ref, f32[992,128]{1,0:T(8,128)} %copy-done.2, f32[992,128]{1,0:T(8,128)} %copy-done.10), custom_call_target="tpu_custom_call" | custom-call | flops 10000000000 | bytes 1015808 | tf_op jit(solution)/shard_map/factor/pallas_call | solution.py:390
  123.3 0.9 copy-done.9
  124.2 27.5 %factor.3 = (f32[128,1024]{1,0:T(8,128)}, f32[1,1024]{1,0:T(1,128)}) custom-call(s32[6]{0:T(128)} %stack.31.place_ref, f32[1344,128]{1,0:T(8,128)} %copy-done.1, f32[1344,128]{1,0:T(8,128)} %copy-done.9, f32[768,896]{1,0:T(8,128)} %get-tuple-element.29.refs_0_, f32[256,1152]{1,0:T(8,128)} %get-tuple-element.30.refs_1_, f32[256,128]{1,0:T(8,128)} %get-tuple-element.31.refs_2_), custom_call_target="tpu_custom_call" | custom-call | flops 30000001024 | bytes 1376256 | tf_op jit(solution)/shard_map/factor/pallas_call | solution.py:390
  (33 shorter events, 0.5 us)
Async XLA Ops:
  12.4 18.1 %copy-start.3 = (f32[992,128]{1,0:T(8,128)S(1)}, f32[992,128]{1,0:T(8,128)}, u32[]{:S(2)}) copy-start(f32[992,128]{1,0:T(8,128)} %get-tuple-element.25) | copy-start | bytes 1523716
  12.4 18.7 %copy-start.7 = (f32[1,1024]{1,0:T(1,128)S(1)}, f32[1,1024]{1,0:T(1,128)}, u32[]{:S(2)}) copy-start(f32[1,1024]{1,0:T(1,128)} %f_ref.1) | copy-start | bytes 12292
  12.4 18.1 %collective-permute-start.9 = (f32[992,128]{1,0:T(8,128)}, f32[992,128]{1,0:T(8,128)S(1)}, u32[]{:S(2)}, u32[]{:S(2)}) collective-permute-start(f32[992,128]{1,0:T(8,128)} %get-tuple-element.26), channel_id=1, source_target_pairs={{0,1},{1,0},{2,3},{3,2},{4,5},{5,4},{6,7},{7,6},{8,9},{9,8},{10,11... | collective-permute-start | bytes 1523720 | tf_op jit(solution)/shard_map/ppermute | solution.py:405
  28.9 18.6 %collective-permute-start = (f32[1344,128]{1,0:T(8,128)}, f32[1344,128]{1,0:T(8,128)S(1)}, u32[]{:S(2)}, u32[]{:S(2)}) collective-permute-start(f32[1344,128]{1,0:T(8,128)} %get-tuple-element.21), channel_id=1, source_target_pairs={{0,2},{1,3},{2,0},{3,1},{4,6},{5,7},{6,4},{7,5},{8,10},{9,11},{10,... | collective-permute-start | bytes 2064392 | tf_op jit(solution)/shard_map/ppermute | solution.py:405
  30.6 20.9 %collective-permute-start.10 = (f32[496,128]{1,0:T(8,128)S(1)}, f32[496,128]{1,0:T(8,128)S(1)}, u32[]{:S(2)}, u32[]{:S(2)}) collective-permute-start(f32[496,128]{1,0:T(8,128)S(1)} %constant_dynamic-slice_fusion.1), channel_id=1, source_target_pairs={{0,2},{1,3},{2,0},{3,1},{4,6},{5,7},{6,4},{7,5},{8,10},{9,11},{10,... | collective-permute-start | bytes 761864 | tf_op jit(solution)/shard_map/ppermute | solution.py:405
  31.1 3.0 %collective-permute-start.5 = (f32[1,1024]{1,0:T(1,128)S(1)}, f32[1,1024]{1,0:T(1,128)S(1)}, u32[]{:S(2)}, u32[]{:S(2)}) collective-permute-start(f32[1,1024]{1,0:T(1,128)S(1)} %copy-done.7), channel_id=1, source_target_pairs={{0,8},{8,16},{16,24},{1,9},{9,17},{17,25},{2,10},{10,18},{18,26},{... | collective-permute-start | bytes 12296 | tf_op jit(solution)/shard_map/ppermute | solution.py:442
  34.0 30.0 %copy-start.4 = (f32[248,128]{1,0:T(8,128)S(1)}, f32[248,128]{1,0:T(8,128)}, u32[]{:S(2)}) copy-start(f32[248,128]{1,0:T(8,128)} %get-tuple-element.27) | copy-start | bytes 380932
  34.0 32.5 %copy-start = (f32[336,128]{1,0:T(8,128)S(1)}, f32[336,128]{1,0:T(8,128)}, u32[]{:S(2)}) copy-start(f32[336,128]{1,0:T(8,128)} %get-tuple-element.22) | copy-start | bytes 516100
  34.1 0.6 copy-start.8
  36.3 41.0 %copy-start.6 = (f32[248,128]{1,0:T(8,128)S(1)}, f32[248,128]{1,0:T(8,128)}, u32[]{:S(2)}) copy-start(f32[248,128]{1,0:T(8,128)} %get-tuple-element.28) | copy-start | bytes 380932
  47.5 32.2 %copy-start.5 = (f32[336,128]{1,0:T(8,128)S(1)}, f32[336,128]{1,0:T(8,128)}, u32[]{:S(2)}) copy-start(f32[336,128]{1,0:T(8,128)} %get-tuple-element.24) | copy-start | bytes 516100
  48.7 7.3 %collective-permute-start.1 = (f32[672,128]{1,0:T(8,128)S(1)}, f32[672,128]{1,0:T(8,128)S(1)}, u32[]{:S(2)}, u32[]{:S(2)}) collective-permute-start(f32[672,128]{1,0:T(8,128)S(1)} %constant_dynamic-slice_fusion.3), channel_id=1, source_target_pairs={{0,1},{1,0},{2,3},{3,2},{4,5},{5,4},{6,7},{7,6},{8,9},{9,8},{10,11... | collective-permute-start | bytes 1032200 | tf_op jit(solution)/shard_map/ppermute | solution.py:405
  51.5 12.5 %collective-permute-start.11 = (f32[248,128]{1,0:T(8,128)S(1)}, f32[248,128]{1,0:T(8,128)S(1)}, u32[]{:S(2)}, u32[]{:S(2)}) collective-permute-start(f32[248,128]{1,0:T(8,128)S(1)} %constant_dynamic-slice_fusion), channel_id=1, source_target_pairs={{0,4},{1,5},{2,6},{3,7},{4,0},{5,1},{6,2},{7,3},{8,12},{9,13},{10,... | collective-permute-start | bytes 380936 | tf_op jit(solution)/shard_map/ppermute | solution.py:405
  56.1 10.4 %collective-permute-start.2 = (f32[336,128]{1,0:T(8,128)S(1)}, f32[336,128]{1,0:T(8,128)S(1)}, u32[]{:S(2)}, u32[]{:S(2)}) collective-permute-start(f32[336,128]{1,0:T(8,128)S(1)} %constant_dynamic-slice_fusion.2), channel_id=1, source_target_pairs={{0,4},{1,5},{2,6},{3,7},{4,0},{5,1},{6,2},{7,3},{8,12},{9,13},{10,... | collective-permute-start | bytes 516104 | tf_op jit(solution)/shard_map/ppermute | solution.py:405
  64.0 5.5 %collective-permute-start.12 = (f32[248,128]{1,0:T(8,128)S(1)}, f32[248,128]{1,0:T(8,128)S(1)}, u32[]{:S(2)}, u32[]{:S(2)}) collective-permute-start(f32[248,128]{1,0:T(8,128)S(1)} %fusion.3), channel_id=1, source_target_pairs={{0,8},{8,16},{16,24},{1,9},{9,17},{17,25},{2,10},{10,18},{18,26},{... | collective-permute-start | bytes 380936 | tf_op jit(solution)/shard_map/ppermute | solution.py:442
  66.5 7.2 %collective-permute-start.3 = (f32[336,128]{1,0:T(8,128)S(1)}, f32[336,128]{1,0:T(8,128)S(1)}, u32[]{:S(2)}, u32[]{:S(2)}) collective-permute-start(f32[336,128]{1,0:T(8,128)S(1)} %fusion.1), channel_id=1, source_target_pairs={{0,8},{8,16},{16,24},{1,9},{9,17},{17,25},{2,10},{10,18},{18,26},{... | collective-permute-start | bytes 516104 | tf_op jit(solution)/shard_map/ppermute | solution.py:442
  69.6 7.7 %collective-permute-start.13 = (f32[248,128]{1,0:T(8,128)S(1)}, f32[248,128]{1,0:T(8,128)S(1)}, u32[]{:S(2)}, u32[]{:S(2)}) collective-permute-start(f32[248,128]{1,0:T(8,128)S(1)} %get-tuple-element.34), channel_id=1, source_target_pairs={{0,16},{8,24},{1,17},{9,25},{2,18},{10,26},{3,19},{11,27},{4,20},{... | collective-permute-start | bytes 380936 | tf_op jit(solution)/shard_map/ppermute | solution.py:442
  73.8 5.8 %collective-permute-start.4 = (f32[336,128]{1,0:T(8,128)S(1)}, f32[336,128]{1,0:T(8,128)S(1)}, u32[]{:S(2)}, u32[]{:S(2)}) collective-permute-start(f32[336,128]{1,0:T(8,128)S(1)} %get-tuple-element.36), channel_id=1, source_target_pairs={{0,16},{8,24},{1,17},{9,25},{2,18},{10,26},{3,19},{11,27},{4,20},{... | collective-permute-start | bytes 516104 | tf_op jit(solution)/shard_map/ppermute | solution.py:442
  77.4 11.8 %collective-permute-start.14 = (f32[248,128]{1,0:T(8,128)S(1)}, f32[248,128]{1,0:T(8,128)S(1)}, u32[]{:S(2)}, u32[]{:S(2)}) collective-permute-start(f32[248,128]{1,0:T(8,128)S(1)} %multiply_add_fusion.1), channel_id=1, source_target_pairs={{0,4},{1,5},{2,6},{3,7},{4,0},{5,1},{6,2},{7,3},{8,12},{9,13},{10,... | collective-permute-start | bytes 380936 | tf_op jit(solution)/shard_map/ppermute | solution.py:405
  79.7 11.3 %collective-permute-start.6 = (f32[336,128]{1,0:T(8,128)S(1)}, f32[336,128]{1,0:T(8,128)S(1)}, u32[]{:S(2)}, u32[]{:S(2)}) collective-permute-start(f32[336,128]{1,0:T(8,128)S(1)} %multiply_add_fusion), channel_id=1, source_target_pairs={{0,4},{1,5},{2,6},{3,7},{4,0},{5,1},{6,2},{7,3},{8,12},{9,13},{10,... | collective-permute-start | bytes 516104 | tf_op jit(solution)/shard_map/ppermute | solution.py:405
  89.2 6.3 %collective-permute-start.15 = (f32[496,128]{1,0:T(8,128)S(1)}, f32[496,128]{1,0:T(8,128)S(1)}, u32[]{:S(2)}, u32[]{:S(2)}) collective-permute-start(f32[496,128]{1,0:T(8,128)S(1)} %maximum_select_fusion.3), channel_id=1, source_target_pairs={{0,2},{1,3},{2,0},{3,1},{4,6},{5,7},{6,4},{7,5},{8,10},{9,11},{10,... | collective-permute-start | bytes 761864 | tf_op jit(solution)/shard_map/ppermute | solution.py:405
  91.0 11.1 %collective-permute-start.7 = (f32[672,128]{1,0:T(8,128)S(1)}, f32[672,128]{1,0:T(8,128)S(1)}, u32[]{:S(2)}, u32[]{:S(2)}) collective-permute-start(f32[672,128]{1,0:T(8,128)S(1)} %maximum_select_fusion.2), channel_id=1, source_target_pairs={{0,1},{1,0},{2,3},{3,2},{4,5},{5,4},{6,7},{7,6},{8,9},{9,8},{10,11... | collective-permute-start | bytes 1032200 | tf_op jit(solution)/shard_map/ppermute | solution.py:405
  95.6 14.2 %copy-start.2 = (f32[992,128]{1,0:T(8,128)}, f32[992,128]{1,0:T(8,128)S(1)}, u32[]{:S(2)}) copy-start(f32[992,128]{1,0:T(8,128)S(1)} %maximum_select_fusion.1.own_ref) | copy-start | bytes 1523716
  95.6 14.1 %collective-permute-start.16 = (f32[992,128]{1,0:T(8,128)S(1)}, f32[992,128]{1,0:T(8,128)S(1)}, u32[]{:S(2)}, u32[]{:S(2)}) collective-permute-start(f32[992,128]{1,0:T(8,128)S(1)} %maximum_select_fusion.1.own_ref), channel_id=1, source_target_pairs={{0,1},{1,0},{2,3},{3,2},{4,5},{5,4},{6,7},{7,6},{8,9},{9,8},{10,11... | collective-permute-start | bytes 1523720 | tf_op jit(solution)/shard_map/ppermute | solution.py:405
  102.2 21.2 %copy-start.1 = (f32[1344,128]{1,0:T(8,128)}, f32[1344,128]{1,0:T(8,128)S(1)}, u32[]{:S(2)}) copy-start(f32[1344,128]{1,0:T(8,128)S(1)} %maximum_select_fusion.own_ref) | copy-start | bytes 2064388
  102.2 21.2 %collective-permute-start.8 = (f32[1344,128]{1,0:T(8,128)S(1)}, f32[1344,128]{1,0:T(8,128)S(1)}, u32[]{:S(2)}, u32[]{:S(2)}) collective-permute-start(f32[1344,128]{1,0:T(8,128)S(1)} %maximum_select_fusion.own_ref), channel_id=1, source_target_pairs={{0,2},{1,3},{2,0},{3,1},{4,6},{5,7},{6,4},{7,5},{8,10},{9,11},{10,... | collective-permute-start | bytes 2064392 | tf_op jit(solution)/shard_map/ppermute | solution.py:405
  109.8 0.8 copy-start.10
  123.3 0.9 copy-start.9

commit v4 on v3

--- a/solution.py
+++ b/solution.py
@@ -11,10 +11,10 @@
 SUB = 8
 CHUNK = 2048
 VMEM_BYTES = 60 << 20
+FACTOR_VMEM_BYTES = 24 << 20
 CUTS = (2,)
 CUT_PLACES = (0,) + CUTS
 FAR = 3
-TIED = ()
 TURNED = (1,)
 FACTOR_FLOPS = 5 * 10**9
 BF16 = jnp.bfloat16
@@ -34,12 +34,27 @@
     return lax.dot_general(a, b, (((1,), (1,)), ((), ())), preferred_element_type=F32)
 
 
+def split3(x):
+    a = x.astype(BF16)
+    rest = x - a.astype(F32)
+    b = rest.astype(BF16)
+    return a, b, (rest - b.astype(F32)).astype(BF16)
+
+
+def exact_dot(left, right, axis):
+    a, b, c = split3(left)
+    left = jnp.concatenate([a, a, b, a, c, b], axis)
+    a, b, c = split3(right)
+    right = jnp.concatenate([a, b, a, c, a, b], 0)
+    return lax.dot_general(left, right, (((axis,), (0,)), ((), ())), preferred_element_type=F32)
+
+
 def dot_tn(a, b):
-    return lax.dot_general(a, b, (((0,), (0,)), ((), ())), precision=HI, preferred_element_type=F32)
+    return exact_dot(a, b, 0)
 
 
 def dot_nn(a, b):
-    return jnp.dot(a, b, precision=HI, preferred_element_type=F32)
+    return exact_dot(a, b, 1)
 
 
 def tiles(lo, hi, count):
@@ -109,7 +124,9 @@
             if start == 0:
                 base = len(kept) * width
                 packed_ref[base:, :] = jnp.zeros((packed_ref.shape[0] - base, width), F32)
-                vec = jnp.concatenate([acc[0:1, :] for acc in acc_refs], 1) + dot_nn(t_ref[0], prior)
+                vec = jnp.concatenate([acc[0:1, :] for acc in acc_refs], 1) + jnp.dot(
+                    t_ref[0], prior, precision=HI, preferred_element_type=F32
+                )
                 for i in range(count):
                     packed_ref[base + i : base + i + 1, :] = vec[:, i * width : (i + 1) * width]
             half = packed_ref.shape[0] // 2
@@ -201,13 +218,6 @@
 
 def spread(x, index, axis):
     return jnp.broadcast_to(lax.slice_in_dim(x, index, index + 1, axis=axis), x.shape)
-
-
-def split3(x):
-    a = x.astype(BF16)
-    rest = x - a.astype(F32)
-    b = rest.astype(BF16)
-    return a, b, (rest - b.astype(F32)).astype(BF16)
 
 
 def far_product(top, both):
@@ -265,28 +275,28 @@
     return jnp.concatenate(tops, 0), jnp.concatenate(lows, 0)
 
 
-def run_panels(count, lo, hi, row_of, s_ref, r_ref, t_ref):
+def run_panels(lo, hi, row_of, r_ref, t_ref):
     width = t_ref.shape[1]
     start = lo * width
 
-    s_ref[...] = row_of(lo)
-
-    @pl.loop(0, hi - lo)
-    def _(k):
-        at = pl.multiple_of(k * width, width)
-        upper, inverse = diag_factor(s_ref[:, pl.ds(at, width)])
-        t_ref[pl.ds(at, width), :] = inverse
-        r_ref[pl.ds(at, width), pl.ds(at, width)] = upper
-        for kk in range(hi - lo):
-
-            @pl.when(k == kk)
-            def _():
-                rest = (kk + 1) * width
-                r_ref[kk * width : rest, rest:] = dot_nn(t_ref[kk * width : rest, :], s_ref[:, rest:])
-                if lo + kk + 1 < hi:
-                    s_ref[:, rest:] = row_of(lo + kk + 1) - dot_tn(
-                        r_ref[0:rest, rest : rest + width], r_ref[0:rest, rest:]
-                    )
+    row = row_of(lo)
+    for k in range(hi - lo):
+        at, end = k * width, (k + 1) * width
+        upper, inverse = diag_factor(row[:, :width])
+        t_ref[at:end, :] = inverse
+        r_ref[at:end, at:end] = upper
+        if lo + k + 1 < hi:
+            near = dot_nn(inverse, row[:, width : 2 * width])
+            r_ref[at:end, end : end + width] = near
+            following = row_of(lo + k + 1)
+            if k:
+                following = following - dot_tn(r_ref[0:at, end : end + width], r_ref[0:at, end:])
+            block = following[:, :width] - dot_tn(near, near)
+            far = dot_nn(inverse, row[:, 2 * width :])
+            r_ref[at:end, end + width :] = far
+            row = jnp.concatenate([block, following[:, width:] - dot_tn(near, far)], 1)
+        else:
+            r_ref[at:end, end:] = dot_nn(inverse, row[:, width:])
 
 
 def stage_kernel(count, lo, hi, place_ref, own_ref, other_ref, *refs):
@@ -295,11 +305,11 @@
     last = hi == count
     carry_ref = refs.pop(0) if before else None
     if last:
-        earlier = [(refs.pop(0), refs.pop(0)) for _ in range((len(refs) - 6) // 2)]
+        earlier = [(refs.pop(0), refs.pop(0)) for _ in range((len(refs) - 5) // 2)]
         rows_ref, est_ref, r_ref, t_ref = refs[:4]
     else:
         r_ref, t_ref, left_ref = refs[:3]
-    x_ref, s_ref = refs[-2:]
+    x_ref = refs[-1]
     width = x_ref.shape[1]
     states = count * width
     kept = upper_blocks(lo, hi, count)
@@ -322,7 +332,7 @@
             return jnp.concatenate(parts, 1) + taken_before(k)
         return jnp.concatenate(parts + [vec_column(k)], 1)
 
-    run_panels(count, lo, hi, row_of, s_ref, r_ref, t_ref)
+    run_panels(lo, hi, row_of, r_ref, t_ref)
     if not last:
         for k in range(hi, count):
             at = (k - lo) * width
@@ -386,14 +396,14 @@
         outs = [(share, states), (1, states)]
     else:
         outs = parts + [(states - hi * width, states - hi * width + width)]
-    scratch = (parts if last else []) + [(2 * halves[0].shape[0], width), (width, rest + width)]
+    scratch = (parts if last else []) + [(2 * halves[0].shape[0], width)]
     return pl.pallas_call(
         functools.partial(stage_kernel, count, lo, hi),
         in_specs=[pl.BlockSpec(memory_space=pltpu.SMEM)] + [vmem] * len(operands),
         out_specs=[vmem] * len(outs),
         out_shape=[jax.ShapeDtypeStruct(shape, F32) for shape in outs],
         scratch_shapes=[pltpu.VMEM(shape, F32) for shape in scratch],
-        compiler_params=pltpu.CompilerParams(vmem_limit_bytes=VMEM_BYTES),
+        compiler_params=pltpu.CompilerParams(vmem_limit_bytes=FACTOR_VMEM_BYTES),
         cost_estimate=pl.CostEstimate(
             flops=(hi - lo) * FACTOR_FLOPS, bytes_accessed=8 * halves[0].size, transcendentals=rows
         ),
@@ -460,8 +470,6 @@
     def stage(step):
         moved = [step(n, part) for n, part in enumerate(parts)]
         for n, (other, combine) in enumerate(moved):
-            if n and n in TIED:
-                other = after(other, parts[n - 1])
             parts[n] = combine(other)
 
     def sum_first(n, part):

time: 152 us -> 142 us (0.934)
  Pallas kernels: 68.2 us -> 60 us
  local copies, waits for them, and re-layouts: 2.99 us -> 1.38 us
    pallas_call x2, Pallas kernels: 40.3 us -> 33.1 us  [factor_stage(): pl.pallas_call(functools.partial(stage_kernel, count, lo, hi), in_specs=[...]
    unnamed x22 -> x16, local copies, waits for them, and re-layouts: 2.27 us -> 0.61 us
  transfers between devices with their start and end apart: 17 -> 17, of which waited for: 12 -> 12; matrix products, arithmetic and copies ran while one was open for 1% -> 1% of each run, Pallas kernels for 19% -> 18%
where the time goes in v4:
time: 142 us
  Pallas kernels  60 us (42%)
  waiting for transfers between devices  52.1 us (37%)
  starting transfers between devices  25.8 us (18%)
  other arithmetic  1.67 us (1%)
    ppermute x12, waiting for transfers between devices, exchange(): lax.ppermute(x, axis, [(i, i ^ mask) for i in range(lax.axis_size(axis))])  49.5 us
    pallas_call x2, Pallas kernels, factor_stage(): pl.pallas_call(functools.partial(stage_kernel, count, lo, hi), in_specs=[...  33.1 us
    pallas_call x2, Pallas kernels, local_gram(): pl.pallas_call(functools.partial(gram_kernel, count, spans, number), grid...  23.5 us
    ppermute x12, starting transfers between devices, exchange(): lax.ppermute(x, axis, [(i, i ^ mask) for i in range(lax.axis_size(axis))])  13 us
    ppermute x5, starting transfers between devices, earlier(): return lax.ppermute(x, 'tm', [(i, i + by) for i in range(steps - by)])  12.8 us
    pallas_call x2, Pallas kernels, decay_pieces(): pl.pallas_call(functools.partial(decay_kernel, count, spans), in_specs=[p...  3.35 us
  transfers between devices with their start and end apart: 17, of which 12 were waited for; matrix products, arithmetic and copies ran while one was open for 1% of the time, Pallas kernels for 18%

profile of v4, /device:TPU:0, one launch (start us, length us, event | category | flops | bytes accessed | tf_op | source)
XLA Modules:
  0.0 141.9 jit_solution(14054321395342590139)
XLA Ops:
  0.7 0.7 stack.31.place_ref
  1.3 10.7 %gram.2 = (f32[992,128]{1,0:T(8,128)}, f32[992,128]{1,0:T(8,128)}) custom-call(s32[6]{0:T(128)} %stack.31.place_ref, bf16[8192,256]{1,0:T(8,128)(2,1)} %v_ref.3, s32[2,8192]{1,0:T(2,128)} %bitcast.9, f32[1,8192]{1,0:T(1,128)} %n_ref.3, f32[1,8192]{1,0:T(1,128)} %r_ref.3, s32[1,8192]{1,0:T(1,128)} %a_ref.3, f32[1024,1024]{1,0:T(8,128)} %p_ref.3, ...), custom_call_target="tpu_custom_call" | custom-call | flops 4160749568 | bytes 4194304 | tf_op jit(solution)/shard_map/gram/pallas_call | solution.py:154
  12.0 3.0 %collective-permute-start.9 = (f32[992,128]{1,0:T(8,128)}, f32[992,128]{1,0:T(8,128)S(1)}, u32[]{:S(2)}, u32[]{:S(2)}) collective-permute-start(f32[992,128]{1,0:T(8,128)} %get-tuple-element.26), channel_id=1, source_target_pairs={{0,1},{1,0},{2,3},{3,2},{4,5},{5,4},{6,7},{7,6},{8,9},{9,8},{10,11... | collective-permute-start | bytes 1523720 | tf_op jit(solution)/shard_map/ppermute | solution.py:415
  15.1 12.8 %gram.3 = (f32[1344,128]{1,0:T(8,128)}, f32[1344,128]{1,0:T(8,128)}) custom-call(s32[6]{0:T(128)} %stack.31.place_ref, bf16[8192,256]{1,0:T(8,128)(2,1)} %v_ref.3, s32[2,8192]{1,0:T(2,128)} %bitcast.10, f32[1,8192]{1,0:T(1,128)} %n_ref.3, f32[1,8192]{1,0:T(1,128)} %r_ref.3, s32[1,8192]{1,0:T(1,128)} %a_ref.3, f32[1024,1024]{1,0:T(8,128)} %p_ref.3, ...), custom_call_target="tpu_custom_call" | custom-call | flops 5637144576 | bytes 4194304 | tf_op jit(solution)/shard_map/gram/pallas_call | solution.py:154
  27.9 1.6 %collective-permute-start = (f32[1344,128]{1,0:T(8,128)}, f32[1344,128]{1,0:T(8,128)S(1)}, u32[]{:S(2)}, u32[]{:S(2)}) collective-permute-start(f32[1344,128]{1,0:T(8,128)} %get-tuple-element.21), channel_id=1, source_target_pairs={{0,2},{1,3},{2,0},{3,1},{4,6},{5,7},{6,4},{7,5},{8,10},{9,11},{10,... | collective-permute-start | bytes 2064392 | tf_op jit(solution)/shard_map/ppermute | solution.py:415
  29.5 0.0 collective-permute-done.9
  29.5 0.0 copy-done.2
  29.5 0.1 add.69
  29.6 0.5 collective-permute-start.10
  30.1 1.3 collective-permute-start.5
  31.4 1.7 %decays.2 = (f32[248,128]{1,0:T(8,128)}, f32[336,128]{1,0:T(8,128)}) custom-call(s32[6]{0:T(128)} %stack.31.place_ref, f32[1,1024]{1,0:T(1,128)} %f_ref.1), custom_call_target="tpu_custom_call" | custom-call | flops 598016 | bytes 598016 | tf_op jit(solution)/shard_map/decays/pallas_call | solution.py:207
  33.1 0.0 collective-permute-done.5.f_ref
  33.1 0.0 copy-start.7
  33.1 0.6 copy-done.7
  33.7 1.7 %decays.3 = (f32[248,128]{1,0:T(8,128)}, f32[336,128]{1,0:T(8,128)}) custom-call(s32[6]{0:T(128)} %stack.31.place_ref, f32[1,1024]{1,0:T(1,128)} %copy-done.7), custom_call_target="tpu_custom_call" | custom-call | flops 598016 | bytes 598016 | tf_op jit(solution)/shard_map/decays/pallas_call | solution.py:207
  35.4 11.1 %collective-permute-done = f32[1344,128]{1,0:T(8,128)S(1)} collective-permute-done((f32[1344,128]{1,0:T(8,128)}, f32[1344,128]{1,0:T(8,128)S(1)}, u32[]{:S(2)}, u32[]{:S(2)}) %collective-permute-start) | collective-permute-done | bytes 688160 | tf_op jit(solution)/shard_map/ppermute | solution.py:415
  46.5 1.2 add.62
  47.7 0.2 collective-permute-start.1
  47.9 2.5 %collective-permute-done.10 = f32[496,128]{1,0:T(8,128)S(1)} collective-permute-done((f32[496,128]{1,0:T(8,128)S(1)}, f32[496,128]{1,0:T(8,128)S(1)}, u32[]{:S(2)}, u32[]{:S(2)}) %collective-permute-start.10) | collective-permute-done | bytes 253984 | tf_op jit(solution)/shard_map/ppermute | solution.py:415
  50.5 2.7 %collective-permute-start.11 = (f32[248,128]{1,0:T(8,128)S(1)}, f32[248,128]{1,0:T(8,128)S(1)}, u32[]{:S(2)}, u32[]{:S(2)}) collective-permute-start(f32[248,128]{1,0:T(8,128)S(1)} %constant_dynamic-slice_fusion), channel_id=1, source_target_pairs={{0,4},{1,5},{2,6},{3,7},{4,0},{5,1},{6,2},{7,3},{8,12},{9,13},{10,... | collective-permute-start | bytes 380936 | tf_op jit(solution)/shard_map/ppermute | solution.py:415
  53.2 1.9 %collective-permute-done.1 = f32[672,128]{1,0:T(8,128)S(1)} collective-permute-done((f32[672,128]{1,0:T(8,128)S(1)}, f32[672,128]{1,0:T(8,128)S(1)}, u32[]{:S(2)}, u32[]{:S(2)}) %collective-permute-start.1) | collective-permute-done | bytes 344096 | tf_op jit(solution)/shard_map/ppermute | solution.py:415
  55.1 0.0 copy-start
  55.1 2.7 %collective-permute-start.2 = (f32[336,128]{1,0:T(8,128)S(1)}, f32[336,128]{1,0:T(8,128)S(1)}, u32[]{:S(2)}, u32[]{:S(2)}) collective-permute-start(f32[336,128]{1,0:T(8,128)S(1)} %constant_dynamic-slice_fusion.2), channel_id=1, source_target_pairs={{0,4},{1,5},{2,6},{3,7},{4,0},{5,1},{6,2},{7,3},{8,12},{9,13},{10,... | collective-permute-start | bytes 516104 | tf_op jit(solution)/shard_map/ppermute | solution.py:415
  57.8 5.3 %collective-permute-done.11 = f32[248,128]{1,0:T(8,128)S(1)} collective-permute-done((f32[248,128]{1,0:T(8,128)S(1)}, f32[248,128]{1,0:T(8,128)S(1)}, u32[]{:S(2)}, u32[]{:S(2)}) %collective-permute-start.11) | collective-permute-done | bytes 127008 | tf_op jit(solution)/shard_map/ppermute | solution.py:415
  63.1 1.3 collective-permute-start.12
  64.4 1.1 collective-permute-done.2
  65.6 3.0 %collective-permute-start.3 = (f32[336,128]{1,0:T(8,128)S(1)}, f32[336,128]{1,0:T(8,128)S(1)}, u32[]{:S(2)}, u32[]{:S(2)}) collective-permute-start(f32[336,128]{1,0:T(8,128)S(1)} %fusion.1), channel_id=1, source_target_pairs={{0,8},{8,16},{16,24},{1,9},{9,17},{17,25},{2,10},{10,18},{18,26},{... | collective-permute-start | bytes 516104 | tf_op jit(solution)/shard_map/ppermute | solution.py:452
  68.6 0.0 collective-permute-done.12
  68.6 4.1 %collective-permute-start.13 = (f32[248,128]{1,0:T(8,128)S(1)}, f32[248,128]{1,0:T(8,128)S(1)}, u32[]{:S(2)}, u32[]{:S(2)}) collective-permute-start(f32[248,128]{1,0:T(8,128)S(1)} %get-tuple-element.34), channel_id=1, source_target_pairs={{0,16},{8,24},{1,17},{9,25},{2,18},{10,26},{3,19},{11,27},{4,20},{... | collective-permute-start | bytes 380936 | tf_op jit(solution)/shard_map/ppermute | solution.py:452
  72.7 0.0 collective-permute-done.3
  72.8 0.1 fusion.6
  72.8 3.1 %collective-permute-start.4 = (f32[336,128]{1,0:T(8,128)S(1)}, f32[336,128]{1,0:T(8,128)S(1)}, u32[]{:S(2)}, u32[]{:S(2)}) collective-permute-start(f32[336,128]{1,0:T(8,128)S(1)} %get-tuple-element.36), channel_id=1, source_target_pairs={{0,16},{8,24},{1,17},{9,25},{2,18},{10,26},{3,19},{11,27},{4,20},{... | collective-permute-start | bytes 516104 | tf_op jit(solution)/shard_map/ppermute | solution.py:452
  75.9 0.4 collective-permute-done.13
  76.4 0.1 collective-permute-start.14
  76.5 2.2 %collective-permute-done.4 = f32[336,128]{1,0:T(8,128)S(1)} collective-permute-done((f32[336,128]{1,0:T(8,128)S(1)}, f32[336,128]{1,0:T(8,128)S(1)}, u32[]{:S(2)}, u32[]{:S(2)}) %collective-permute-start.4) | collective-permute-done | bytes 172064 | tf_op jit(solution)/shard_map/ppermute | solution.py:452
  78.7 0.8 collective-permute-start.6
  79.5 8.7 %collective-permute-done.14 = f32[248,128]{1,0:T(8,128)S(1)} collective-permute-done((f32[248,128]{1,0:T(8,128)S(1)}, f32[248,128]{1,0:T(8,128)S(1)}, u32[]{:S(2)}, u32[]{:S(2)}) %collective-permute-start.14) | collective-permute-done | bytes 127008 | tf_op jit(solution)/shard_map/ppermute | solution.py:415
  88.2 0.1 collective-permute-start.15
  88.3 1.7 %collective-permute-done.6 = f32[336,128]{1,0:T(8,128)S(1)} collective-permute-done((f32[336,128]{1,0:T(8,128)S(1)}, f32[336,128]{1,0:T(8,128)S(1)}, u32[]{:S(2)}, u32[]{:S(2)}) %collective-permute-start.6) | collective-permute-done | bytes 172064 | tf_op jit(solution)/shard_map/ppermute | solution.py:415
  90.1 0.6 collective-permute-start.7
  90.6 3.9 %collective-permute-done.15 = f32[496,128]{1,0:T(8,128)S(1)} collective-permute-done((f32[496,128]{1,0:T(8,128)S(1)}, f32[496,128]{1,0:T(8,128)S(1)}, u32[]{:S(2)}, u32[]{:S(2)}) %collective-permute-start.15) | collective-permute-done | bytes 253984 | tf_op jit(solution)/shard_map/ppermute | solution.py:415
  94.6 0.6 collective-permute-start.16
  95.2 5.9 %collective-permute-done.7 = f32[672,128]{1,0:T(8,128)S(1)} collective-permute-done((f32[672,128]{1,0:T(8,128)S(1)}, f32[672,128]{1,0:T(8,128)S(1)}, u32[]{:S(2)}, u32[]{:S(2)}) %collective-permute-start.7) | collective-permute-done | bytes 344096 | tf_op jit(solution)/shard_map/ppermute | solution.py:415
  101.2 0.3 collective-permute-start.8
  101.5 7.2 %collective-permute-done.16.other_ref = f32[992,128]{1,0:T(8,128)S(1)} collective-permute-done((f32[992,128]{1,0:T(8,128)S(1)}, f32[992,128]{1,0:T(8,128)S(1)}, u32[]{:S(2)}, u32[]{:S(2)}) %collective-permute-start.16) | collective-permute-done | bytes 507936 | tf_op jit(solution)/shard_map/ppermute | solution.py:415
  108.8 9.4 %factor.2 = (f32[256,1152]{1,0:T(8,128)S(1)}, f32[256,128]{1,0:T(8,128)S(1)}, f32[768,896]{1,0:T(8,128)S(1)}) custom-call(s32[6]{0:T(128)S(1)} %copy-done, f32[992,128]{1,0:T(8,128)S(1)} %maximum_select_fusion.1.own_ref, f32[992,128]{1,0:T(8,128)S(1)} %collective-permute-done.16.other_ref), custom_call_target="tpu_custom_call" | custom-call | flops 10000000000 | bytes 1015808 | tf_op jit(solution)/shard_map/factor/pallas_call | solution.py:400
  118.2 0.0 collective-permute-done.8.other_ref
  118.2 23.7 %factor.3 = (f32[128,1024]{1,0:T(8,128)}, f32[1,1024]{1,0:T(1,128)}) custom-call(s32[6]{0:T(128)S(1)} %copy-done, f32[1344,128]{1,0:T(8,128)S(1)} %maximum_select_fusion.own_ref, f32[1344,128]{1,0:T(8,128)S(1)} %collective-permute-done.8.other_ref, f32[768,896]{1,0:T(8,128)S(1)} %get-tuple-element.29.refs_0_, f32[256,1152]{1,0:T(8,128)S(1)} %get-tuple-element.30.refs_1_, ...), custom_call_target="tpu_custom_call" | custom-call | flops 30000001024 | bytes 1376256 | tf_op jit(solution)/shard_map/factor/pallas_call | solution.py:400
  (27 shorter events, 0.5 us)
Async XLA Ops:
  12.0 17.5 %copy-start.2 = (f32[992,128]{1,0:T(8,128)S(1)}, f32[992,128]{1,0:T(8,128)}, u32[]{:S(2)}) copy-start(f32[992,128]{1,0:T(8,128)} %get-tuple-element.25) | copy-start | bytes 1523716
  12.0 18.1 %copy-start.6 = (f32[1,1024]{1,0:T(1,128)S(1)}, f32[1,1024]{1,0:T(1,128)}, u32[]{:S(2)}) copy-start(f32[1,1024]{1,0:T(1,128)} %f_ref.1) | copy-start | bytes 12292
  12.0 17.4 %collective-permute-start.9 = (f32[992,128]{1,0:T(8,128)}, f32[992,128]{1,0:T(8,128)S(1)}, u32[]{:S(2)}, u32[]{:S(2)}) collective-permute-start(f32[992,128]{1,0:T(8,128)} %get-tuple-element.26), channel_id=1, source_target_pairs={{0,1},{1,0},{2,3},{3,2},{4,5},{5,4},{6,7},{7,6},{8,9},{9,8},{10,11... | collective-permute-start | bytes 1523720 | tf_op jit(solution)/shard_map/ppermute | solution.py:415
  27.9 18.6 %collective-permute-start = (f32[1344,128]{1,0:T(8,128)}, f32[1344,128]{1,0:T(8,128)S(1)}, u32[]{:S(2)}, u32[]{:S(2)}) collective-permute-start(f32[1344,128]{1,0:T(8,128)} %get-tuple-element.21), channel_id=1, source_target_pairs={{0,2},{1,3},{2,0},{3,1},{4,6},{5,7},{6,4},{7,5},{8,10},{9,11},{10,... | collective-permute-start | bytes 2064392 | tf_op jit(solution)/shard_map/ppermute | solution.py:415
  29.6 20.9 %collective-permute-start.10 = (f32[496,128]{1,0:T(8,128)S(1)}, f32[496,128]{1,0:T(8,128)S(1)}, u32[]{:S(2)}, u32[]{:S(2)}) collective-permute-start(f32[496,128]{1,0:T(8,128)S(1)} %constant_dynamic-slice_fusion.1), channel_id=1, source_target_pairs={{0,2},{1,3},{2,0},{3,1},{4,6},{5,7},{6,4},{7,5},{8,10},{9,11},{10,... | collective-permute-start | bytes 761864 | tf_op jit(solution)/shard_map/ppermute | solution.py:415
  30.1 3.0 %collective-permute-start.5 = (f32[1,1024]{1,0:T(1,128)S(1)}, f32[1,1024]{1,0:T(1,128)S(1)}, u32[]{:S(2)}, u32[]{:S(2)}) collective-permute-start(f32[1,1024]{1,0:T(1,128)S(1)} %copy-done.6), channel_id=1, source_target_pairs={{0,8},{8,16},{16,24},{1,9},{9,17},{17,25},{2,10},{10,18},{18,26},{... | collective-permute-start | bytes 12296 | tf_op jit(solution)/shard_map/ppermute | solution.py:452
  33.1 30.0 %copy-start.3 = (f32[248,128]{1,0:T(8,128)S(1)}, f32[248,128]{1,0:T(8,128)}, u32[]{:S(2)}) copy-start(f32[248,128]{1,0:T(8,128)} %get-tuple-element.27) | copy-start | bytes 380932
  33.1 32.5 %copy-start.1 = (f32[336,128]{1,0:T(8,128)S(1)}, f32[336,128]{1,0:T(8,128)}, u32[]{:S(2)}) copy-start(f32[336,128]{1,0:T(8,128)} %get-tuple-element.22) | copy-start | bytes 516100
  33.1 0.6 copy-start.7
  35.4 41.0 %copy-start.5 = (f32[248,128]{1,0:T(8,128)S(1)}, f32[248,128]{1,0:T(8,128)}, u32[]{:S(2)}) copy-start(f32[248,128]{1,0:T(8,128)} %get-tuple-element.28) | copy-start | bytes 380932
  46.5 32.2 %copy-start.4 = (f32[336,128]{1,0:T(8,128)S(1)}, f32[336,128]{1,0:T(8,128)}, u32[]{:S(2)}) copy-start(f32[336,128]{1,0:T(8,128)} %get-tuple-element.24) | copy-start | bytes 516100
  47.7 7.3 %collective-permute-start.1 = (f32[672,128]{1,0:T(8,128)S(1)}, f32[672,128]{1,0:T(8,128)S(1)}, u32[]{:S(2)}, u32[]{:S(2)}) collective-permute-start(f32[672,128]{1,0:T(8,128)S(1)} %constant_dynamic-slice_fusion.3), channel_id=1, source_target_pairs={{0,1},{1,0},{2,3},{3,2},{4,5},{5,4},{6,7},{7,6},{8,9},{9,8},{10,11... | collective-permute-start | bytes 1032200 | tf_op jit(solution)/shard_map/ppermute | solution.py:415
  50.5 12.6 %collective-permute-start.11 = (f32[248,128]{1,0:T(8,128)S(1)}, f32[248,128]{1,0:T(8,128)S(1)}, u32[]{:S(2)}, u32[]{:S(2)}) collective-permute-start(f32[248,128]{1,0:T(8,128)S(1)} %constant_dynamic-slice_fusion), channel_id=1, source_target_pairs={{0,4},{1,5},{2,6},{3,7},{4,0},{5,1},{6,2},{7,3},{8,12},{9,13},{10,... | collective-permute-start | bytes 380936 | tf_op jit(solution)/shard_map/ppermute | solution.py:415
  55.1 53.7 %copy-start = (s32[6]{0:T(128)S(1)}, s32[6]{0:T(128)}, u32[]{:S(2)}) copy-start(s32[6]{0:T(128)} %stack.31.place_ref) | copy-start | bytes 76
  55.1 10.4 %collective-permute-start.2 = (f32[336,128]{1,0:T(8,128)S(1)}, f32[336,128]{1,0:T(8,128)S(1)}, u32[]{:S(2)}, u32[]{:S(2)}) collective-permute-start(f32[336,128]{1,0:T(8,128)S(1)} %constant_dynamic-slice_fusion.2), channel_id=1, source_target_pairs={{0,4},{1,5},{2,6},{3,7},{4,0},{5,1},{6,2},{7,3},{8,12},{9,13},{10,... | collective-permute-start | bytes 516104 | tf_op jit(solution)/shard_map/ppermute | solution.py:415
  63.1 5.4 %collective-permute-start.12 = (f32[248,128]{1,0:T(8,128)S(1)}, f32[248,128]{1,0:T(8,128)S(1)}, u32[]{:S(2)}, u32[]{:S(2)}) collective-permute-start(f32[248,128]{1,0:T(8,128)S(1)} %fusion.3), channel_id=1, source_target_pairs={{0,8},{8,16},{16,24},{1,9},{9,17},{17,25},{2,10},{10,18},{18,26},{... | collective-permute-start | bytes 380936 | tf_op jit(solution)/shard_map/ppermute | solution.py:452
  65.6 7.2 %collective-permute-start.3 = (f32[336,128]{1,0:T(8,128)S(1)}, f32[336,128]{1,0:T(8,128)S(1)}, u32[]{:S(2)}, u32[]{:S(2)}) collective-permute-start(f32[336,128]{1,0:T(8,128)S(1)} %fusion.1), channel_id=1, source_target_pairs={{0,8},{8,16},{16,24},{1,9},{9,17},{17,25},{2,10},{10,18},{18,26},{... | collective-permute-start | bytes 516104 | tf_op jit(solution)/shard_map/ppermute | solution.py:452
  68.6 7.7 %collective-permute-start.13 = (f32[248,128]{1,0:T(8,128)S(1)}, f32[248,128]{1,0:T(8,128)S(1)}, u32[]{:S(2)}, u32[]{:S(2)}) collective-permute-start(f32[248,128]{1,0:T(8,128)S(1)} %get-tuple-element.34), channel_id=1, source_target_pairs={{0,16},{8,24},{1,17},{9,25},{2,18},{10,26},{3,19},{11,27},{4,20},{... | collective-permute-start | bytes 380936 | tf_op jit(solution)/shard_map/ppermute | solution.py:452
  72.8 5.8 %collective-permute-start.4 = (f32[336,128]{1,0:T(8,128)S(1)}, f32[336,128]{1,0:T(8,128)S(1)}, u32[]{:S(2)}, u32[]{:S(2)}) collective-permute-start(f32[336,128]{1,0:T(8,128)S(1)} %get-tuple-element.36), channel_id=1, source_target_pairs={{0,16},{8,24},{1,17},{9,25},{2,18},{10,26},{3,19},{11,27},{4,20},{... | collective-permute-start | bytes 516104 | tf_op jit(solution)/shard_map/ppermute | solution.py:452
  76.4 11.8 %collective-permute-start.14 = (f32[248,128]{1,0:T(8,128)S(1)}, f32[248,128]{1,0:T(8,128)S(1)}, u32[]{:S(2)}, u32[]{:S(2)}) collective-permute-start(f32[248,128]{1,0:T(8,128)S(1)} %multiply_add_fusion.1), channel_id=1, source_target_pairs={{0,4},{1,5},{2,6},{3,7},{4,0},{5,1},{6,2},{7,3},{8,12},{9,13},{10,... | collective-permute-start | bytes 380936 | tf_op jit(solution)/shard_map/ppermute | solution.py:415
  78.7 11.3 %collective-permute-start.6 = (f32[336,128]{1,0:T(8,128)S(1)}, f32[336,128]{1,0:T(8,128)S(1)}, u32[]{:S(2)}, u32[]{:S(2)}) collective-permute-start(f32[336,128]{1,0:T(8,128)S(1)} %multiply_add_fusion), channel_id=1, source_target_pairs={{0,4},{1,5},{2,6},{3,7},{4,0},{5,1},{6,2},{7,3},{8,12},{9,13},{10,... | collective-permute-start | bytes 516104 | tf_op jit(solution)/shard_map/ppermute | solution.py:415
  88.2 6.3 %collective-permute-start.15 = (f32[496,128]{1,0:T(8,128)S(1)}, f32[496,128]{1,0:T(8,128)S(1)}, u32[]{:S(2)}, u32[]{:S(2)}) collective-permute-start(f32[496,128]{1,0:T(8,128)S(1)} %maximum_select_fusion.3), channel_id=1, source_target_pairs={{0,2},{1,3},{2,0},{3,1},{4,6},{5,7},{6,4},{7,5},{8,10},{9,11},{10,... | collective-permute-start | bytes 761864 | tf_op jit(solution)/shard_map/ppermute | solution.py:415
  90.1 11.1 %collective-permute-start.7 = (f32[672,128]{1,0:T(8,128)S(1)}, f32[672,128]{1,0:T(8,128)S(1)}, u32[]{:S(2)}, u32[]{:S(2)}) collective-permute-start(f32[672,128]{1,0:T(8,128)S(1)} %maximum_select_fusion.2), channel_id=1, source_target_pairs={{0,1},{1,0},{2,3},{3,2},{4,5},{5,4},{6,7},{7,6},{8,9},{9,8},{10,11... | collective-permute-start | bytes 1032200 | tf_op jit(solution)/shard_map/ppermute | solution.py:415
  94.6 14.2 %collective-permute-start.16 = (f32[992,128]{1,0:T(8,128)S(1)}, f32[992,128]{1,0:T(8,128)S(1)}, u32[]{:S(2)}, u32[]{:S(2)}) collective-permute-start(f32[992,128]{1,0:T(8,128)S(1)} %maximum_select_fusion.1.own_ref), channel_id=1, source_target_pairs={{0,1},{1,0},{2,3},{3,2},{4,5},{5,4},{6,7},{7,6},{8,9},{9,8},{10,11... | collective-permute-start | bytes 1523720 | tf_op jit(solution)/shard_map/ppermute | solution.py:415
  101.2 17.0 %collective-permute-start.8 = (f32[1344,128]{1,0:T(8,128)S(1)}, f32[1344,128]{1,0:T(8,128)S(1)}, u32[]{:S(2)}, u32[]{:S(2)}) collective-permute-start(f32[1344,128]{1,0:T(8,128)S(1)} %maximum_select_fusion.own_ref), channel_id=1, source_target_pairs={{0,2},{1,3},{2,0},{3,1},{4,6},{5,7},{6,4},{7,5},{8,10},{9,11},{10,... | collective-permute-start | bytes 2064392 | tf_op jit(solution)/shard_map/ppermute | solution.py:415

commit v5 on v4

--- a/solution.py
+++ b/solution.py
@@ -282,15 +282,16 @@
     row = row_of(lo)
     for k in range(hi - lo):
         at, end = k * width, (k + 1) * width
+        if lo + k + 1 < hi:
+            following = row_of(lo + k + 1)
+            if k:
+                following = following - dot_tn(r_ref[0:at, end : end + width], r_ref[0:at, end:])
         upper, inverse = diag_factor(row[:, :width])
         t_ref[at:end, :] = inverse
         r_ref[at:end, at:end] = upper
         if lo + k + 1 < hi:
             near = dot_nn(inverse, row[:, width : 2 * width])
             r_ref[at:end, end : end + width] = near
-            following = row_of(lo + k + 1)
-            if k:
-                following = following - dot_tn(r_ref[0:at, end : end + width], r_ref[0:at, end:])
             block = following[:, :width] - dot_tn(near, near)
             far = dot_nn(inverse, row[:, 2 * width :])
             r_ref[at:end, end + width :] = far

time: 142 us -> 142 us (level)
  no operation moved by 1% of the time
where the time goes in v5:
time: 142 us
  Pallas kernels  60.2 us (42%)
  waiting for transfers between devices  52.1 us (37%)
  starting transfers between devices  25.8 us (18%)
  other arithmetic  1.67 us (1%)
    ppermute x12, waiting for transfers between devices, exchange(): lax.ppermute(x, axis, [(i, i ^ mask) for i in range(lax.axis_size(axis))])  49.5 us
    pallas_call x2, Pallas kernels, factor_stage(): pl.pallas_call(functools.partial(stage_kernel, count, lo, hi), in_specs=[...  33.3 us
    pallas_call x2, Pallas kernels, local_gram(): pl.pallas_call(functools.partial(gram_kernel, count, spans, number), grid...  23.5 us
    ppermute x12, starting transfers between devices, exchange(): lax.ppermute(x, axis, [(i, i ^ mask) for i in range(lax.axis_size(axis))])  13 us
    ppermute x5, starting transfers between devices, earlier(): return lax.ppermute(x, 'tm', [(i, i + by) for i in range(steps - by)])  12.8 us
    pallas_call x2, Pallas kernels, decay_pieces(): pl.pallas_call(functools.partial(decay_kernel, count, spans), in_specs=[p...  3.35 us
  transfers between devices with their start and end apart: 17, of which 12 were waited for; matrix products, arithmetic and copies ran while one was open for 1% of the time, Pallas kernels for 18%

profile of v5, /device:TPU:0, one launch (start us, length us, event | category | flops | bytes accessed | tf_op | source)
XLA Modules:
  0.0 142.1 jit_solution(18059464633634084960)
XLA Ops:
  0.7 0.7 stack.31.place_ref
  1.3 10.7 %gram.2 = (f32[992,128]{1,0:T(8,128)}, f32[992,128]{1,0:T(8,128)}) custom-call(s32[6]{0:T(128)} %stack.31.place_ref, bf16[8192,256]{1,0:T(8,128)(2,1)} %v_ref.3, s32[2,8192]{1,0:T(2,128)} %bitcast.9, f32[1,8192]{1,0:T(1,128)} %n_ref.3, f32[1,8192]{1,0:T(1,128)} %r_ref.3, s32[1,8192]{1,0:T(1,128)} %a_ref.3, f32[1024,1024]{1,0:T(8,128)} %p_ref.3, ...), custom_call_target="tpu_custom_call" | custom-call | flops 4160749568 | bytes 4194304 | tf_op jit(solution)/shard_map/gram/pallas_call | solution.py:154
  12.0 3.0 %collective-permute-start.9 = (f32[992,128]{1,0:T(8,128)}, f32[992,128]{1,0:T(8,128)S(1)}, u32[]{:S(2)}, u32[]{:S(2)}) collective-permute-start(f32[992,128]{1,0:T(8,128)} %get-tuple-element.26), channel_id=1, source_target_pairs={{0,1},{1,0},{2,3},{3,2},{4,5},{5,4},{6,7},{7,6},{8,9},{9,8},{10,11... | collective-permute-start | bytes 1523720 | tf_op jit(solution)/shard_map/ppermute | solution.py:416
  15.1 12.8 %gram.3 = (f32[1344,128]{1,0:T(8,128)}, f32[1344,128]{1,0:T(8,128)}) custom-call(s32[6]{0:T(128)} %stack.31.place_ref, bf16[8192,256]{1,0:T(8,128)(2,1)} %v_ref.3, s32[2,8192]{1,0:T(2,128)} %bitcast.10, f32[1,8192]{1,0:T(1,128)} %n_ref.3, f32[1,8192]{1,0:T(1,128)} %r_ref.3, s32[1,8192]{1,0:T(1,128)} %a_ref.3, f32[1024,1024]{1,0:T(8,128)} %p_ref.3, ...), custom_call_target="tpu_custom_call" | custom-call | flops 5637144576 | bytes 4194304 | tf_op jit(solution)/shard_map/gram/pallas_call | solution.py:154
  27.9 1.6 %collective-permute-start = (f32[1344,128]{1,0:T(8,128)}, f32[1344,128]{1,0:T(8,128)S(1)}, u32[]{:S(2)}, u32[]{:S(2)}) collective-permute-start(f32[1344,128]{1,0:T(8,128)} %get-tuple-element.21), channel_id=1, source_target_pairs={{0,2},{1,3},{2,0},{3,1},{4,6},{5,7},{6,4},{7,5},{8,10},{9,11},{10,... | collective-permute-start | bytes 2064392 | tf_op jit(solution)/shard_map/ppermute | solution.py:416
  29.5 0.0 collective-permute-done.9
  29.5 0.0 copy-done.2
  29.5 0.1 add.69
  29.6 0.5 collective-permute-start.10
  30.1 1.3 collective-permute-start.5
  31.4 1.7 %decays.2 = (f32[248,128]{1,0:T(8,128)}, f32[336,128]{1,0:T(8,128)}) custom-call(s32[6]{0:T(128)} %stack.31.place_ref, f32[1,1024]{1,0:T(1,128)} %f_ref.1), custom_call_target="tpu_custom_call" | custom-call | flops 598016 | bytes 598016 | tf_op jit(solution)/shard_map/decays/pallas_call | solution.py:207
  33.1 0.0 collective-permute-done.5.f_ref
  33.1 0.0 copy-start.7
  33.1 0.6 copy-done.7
  33.7 1.7 %decays.3 = (f32[248,128]{1,0:T(8,128)}, f32[336,128]{1,0:T(8,128)}) custom-call(s32[6]{0:T(128)} %stack.31.place_ref, f32[1,1024]{1,0:T(1,128)} %copy-done.7), custom_call_target="tpu_custom_call" | custom-call | flops 598016 | bytes 598016 | tf_op jit(solution)/shard_map/decays/pallas_call | solution.py:207
  35.4 11.1 %collective-permute-done = f32[1344,128]{1,0:T(8,128)S(1)} collective-permute-done((f32[1344,128]{1,0:T(8,128)}, f32[1344,128]{1,0:T(8,128)S(1)}, u32[]{:S(2)}, u32[]{:S(2)}) %collective-permute-start) | collective-permute-done | bytes 688160 | tf_op jit(solution)/shard_map/ppermute | solution.py:416
  46.5 1.2 add.62
  47.7 0.2 collective-permute-start.1
  47.9 2.5 %collective-permute-done.10 = f32[496,128]{1,0:T(8,128)S(1)} collective-permute-done((f32[496,128]{1,0:T(8,128)S(1)}, f32[496,128]{1,0:T(8,128)S(1)}, u32[]{:S(2)}, u32[]{:S(2)}) %collective-permute-start.10) | collective-permute-done | bytes 253984 | tf_op jit(solution)/shard_map/ppermute | solution.py:416
  50.5 2.7 %collective-permute-start.11 = (f32[248,128]{1,0:T(8,128)S(1)}, f32[248,128]{1,0:T(8,128)S(1)}, u32[]{:S(2)}, u32[]{:S(2)}) collective-permute-start(f32[248,128]{1,0:T(8,128)S(1)} %constant_dynamic-slice_fusion), channel_id=1, source_target_pairs={{0,4},{1,5},{2,6},{3,7},{4,0},{5,1},{6,2},{7,3},{8,12},{9,13},{10,... | collective-permute-start | bytes 380936 | tf_op jit(solution)/shard_map/ppermute | solution.py:416
  53.2 1.9 %collective-permute-done.1 = f32[672,128]{1,0:T(8,128)S(1)} collective-permute-done((f32[672,128]{1,0:T(8,128)S(1)}, f32[672,128]{1,0:T(8,128)S(1)}, u32[]{:S(2)}, u32[]{:S(2)}) %collective-permute-start.1) | collective-permute-done | bytes 344096 | tf_op jit(solution)/shard_map/ppermute | solution.py:416
  55.1 0.0 copy-start
  55.1 2.7 %collective-permute-start.2 = (f32[336,128]{1,0:T(8,128)S(1)}, f32[336,128]{1,0:T(8,128)S(1)}, u32[]{:S(2)}, u32[]{:S(2)}) collective-permute-start(f32[336,128]{1,0:T(8,128)S(1)} %constant_dynamic-slice_fusion.2), channel_id=1, source_target_pairs={{0,4},{1,5},{2,6},{3,7},{4,0},{5,1},{6,2},{7,3},{8,12},{9,13},{10,... | collective-permute-start | bytes 516104 | tf_op jit(solution)/shard_map/ppermute | solution.py:416
  57.8 5.3 %collective-permute-done.11 = f32[248,128]{1,0:T(8,128)S(1)} collective-permute-done((f32[248,128]{1,0:T(8,128)S(1)}, f32[248,128]{1,0:T(8,128)S(1)}, u32[]{:S(2)}, u32[]{:S(2)}) %collective-permute-start.11) | collective-permute-done | bytes 127008 | tf_op jit(solution)/shard_map/ppermute | solution.py:416
  63.1 1.3 collective-permute-start.12
  64.4 1.1 collective-permute-done.2
  65.6 3.0 %collective-permute-start.3 = (f32[336,128]{1,0:T(8,128)S(1)}, f32[336,128]{1,0:T(8,128)S(1)}, u32[]{:S(2)}, u32[]{:S(2)}) collective-permute-start(f32[336,128]{1,0:T(8,128)S(1)} %fusion.1), channel_id=1, source_target_pairs={{0,8},{8,16},{16,24},{1,9},{9,17},{17,25},{2,10},{10,18},{18,26},{... | collective-permute-start | bytes 516104 | tf_op jit(solution)/shard_map/ppermute | solution.py:453
  68.6 0.0 collective-permute-done.12
  68.6 4.1 %collective-permute-start.13 = (f32[248,128]{1,0:T(8,128)S(1)}, f32[248,128]{1,0:T(8,128)S(1)}, u32[]{:S(2)}, u32[]{:S(2)}) collective-permute-start(f32[248,128]{1,0:T(8,128)S(1)} %get-tuple-element.34), channel_id=1, source_target_pairs={{0,16},{8,24},{1,17},{9,25},{2,18},{10,26},{3,19},{11,27},{4,20},{... | collective-permute-start | bytes 380936 | tf_op jit(solution)/shard_map/ppermute | solution.py:453
  72.7 0.0 collective-permute-done.3
  72.8 0.1 fusion.6
  72.8 3.1 %collective-permute-start.4 = (f32[336,128]{1,0:T(8,128)S(1)}, f32[336,128]{1,0:T(8,128)S(1)}, u32[]{:S(2)}, u32[]{:S(2)}) collective-permute-start(f32[336,128]{1,0:T(8,128)S(1)} %get-tuple-element.36), channel_id=1, source_target_pairs={{0,16},{8,24},{1,17},{9,25},{2,18},{10,26},{3,19},{11,27},{4,20},{... | collective-permute-start | bytes 516104 | tf_op jit(solution)/shard_map/ppermute | solution.py:453
  75.9 0.4 collective-permute-done.13
  76.4 0.1 collective-permute-start.14
  76.5 2.2 %collective-permute-done.4 = f32[336,128]{1,0:T(8,128)S(1)} collective-permute-done((f32[336,128]{1,0:T(8,128)S(1)}, f32[336,128]{1,0:T(8,128)S(1)}, u32[]{:S(2)}, u32[]{:S(2)}) %collective-permute-start.4) | collective-permute-done | bytes 172064 | tf_op jit(solution)/shard_map/ppermute | solution.py:453
  78.7 0.8 collective-permute-start.6
  79.5 8.7 %collective-permute-done.14 = f32[248,128]{1,0:T(8,128)S(1)} collective-permute-done((f32[248,128]{1,0:T(8,128)S(1)}, f32[248,128]{1,0:T(8,128)S(1)}, u32[]{:S(2)}, u32[]{:S(2)}) %collective-permute-start.14) | collective-permute-done | bytes 127008 | tf_op jit(solution)/shard_map/ppermute | solution.py:416
  88.2 0.1 collective-permute-start.15
  88.3 1.7 %collective-permute-done.6 = f32[336,128]{1,0:T(8,128)S(1)} collective-permute-done((f32[336,128]{1,0:T(8,128)S(1)}, f32[336,128]{1,0:T(8,128)S(1)}, u32[]{:S(2)}, u32[]{:S(2)}) %collective-permute-start.6) | collective-permute-done | bytes 172064 | tf_op jit(solution)/shard_map/ppermute | solution.py:416
  90.1 0.6 collective-permute-start.7
  90.6 3.9 %collective-permute-done.15 = f32[496,128]{1,0:T(8,128)S(1)} collective-permute-done((f32[496,128]{1,0:T(8,128)S(1)}, f32[496,128]{1,0:T(8,128)S(1)}, u32[]{:S(2)}, u32[]{:S(2)}) %collective-permute-start.15) | collective-permute-done | bytes 253984 | tf_op jit(solution)/shard_map/ppermute | solution.py:416
  94.6 0.6 collective-permute-start.16
  95.2 5.9 %collective-permute-done.7 = f32[672,128]{1,0:T(8,128)S(1)} collective-permute-done((f32[672,128]{1,0:T(8,128)S(1)}, f32[672,128]{1,0:T(8,128)S(1)}, u32[]{:S(2)}, u32[]{:S(2)}) %collective-permute-start.7) | collective-permute-done | bytes 344096 | tf_op jit(solution)/shard_map/ppermute | solution.py:416
  101.2 0.3 collective-permute-start.8
  101.5 7.2 %collective-permute-done.16.other_ref = f32[992,128]{1,0:T(8,128)S(1)} collective-permute-done((f32[992,128]{1,0:T(8,128)S(1)}, f32[992,128]{1,0:T(8,128)S(1)}, u32[]{:S(2)}, u32[]{:S(2)}) %collective-permute-start.16) | collective-permute-done | bytes 507936 | tf_op jit(solution)/shard_map/ppermute | solution.py:416
  108.8 9.4 %factor.2 = (f32[256,1152]{1,0:T(8,128)S(1)}, f32[256,128]{1,0:T(8,128)S(1)}, f32[768,896]{1,0:T(8,128)S(1)}) custom-call(s32[6]{0:T(128)S(1)} %copy-done, f32[992,128]{1,0:T(8,128)S(1)} %maximum_select_fusion.1.own_ref, f32[992,128]{1,0:T(8,128)S(1)} %collective-permute-done.16.other_ref), custom_call_target="tpu_custom_call" | custom-call | flops 10000000000 | bytes 1015808 | tf_op jit(solution)/shard_map/factor/pallas_call | solution.py:401
  118.2 0.0 collective-permute-done.8.other_ref
  118.2 23.9 %factor.3 = (f32[128,1024]{1,0:T(8,128)}, f32[1,1024]{1,0:T(1,128)}) custom-call(s32[6]{0:T(128)S(1)} %copy-done, f32[1344,128]{1,0:T(8,128)S(1)} %maximum_select_fusion.own_ref, f32[1344,128]{1,0:T(8,128)S(1)} %collective-permute-done.8.other_ref, f32[768,896]{1,0:T(8,128)S(1)} %get-tuple-element.29.refs_0_, f32[256,1152]{1,0:T(8,128)S(1)} %get-tuple-element.30.refs_1_, ...), custom_call_target="tpu_custom_call" | custom-call | flops 30000001024 | bytes 1376256 | tf_op jit(solution)/shard_map/factor/pallas_call | solution.py:401
  (27 shorter events, 0.5 us)
Async XLA Ops:
  12.0 17.5 %copy-start.2 = (f32[992,128]{1,0:T(8,128)S(1)}, f32[992,128]{1,0:T(8,128)}, u32[]{:S(2)}) copy-start(f32[992,128]{1,0:T(8,128)} %get-tuple-element.25) | copy-start | bytes 1523716
  12.0 18.1 %copy-start.6 = (f32[1,1024]{1,0:T(1,128)S(1)}, f32[1,1024]{1,0:T(1,128)}, u32[]{:S(2)}) copy-start(f32[1,1024]{1,0:T(1,128)} %f_ref.1) | copy-start | bytes 12292
  12.0 17.4 %collective-permute-start.9 = (f32[992,128]{1,0:T(8,128)}, f32[992,128]{1,0:T(8,128)S(1)}, u32[]{:S(2)}, u32[]{:S(2)}) collective-permute-start(f32[992,128]{1,0:T(8,128)} %get-tuple-element.26), channel_id=1, source_target_pairs={{0,1},{1,0},{2,3},{3,2},{4,5},{5,4},{6,7},{7,6},{8,9},{9,8},{10,11... | collective-permute-start | bytes 1523720 | tf_op jit(solution)/shard_map/ppermute | solution.py:416
  27.9 18.6 %collective-permute-start = (f32[1344,128]{1,0:T(8,128)}, f32[1344,128]{1,0:T(8,128)S(1)}, u32[]{:S(2)}, u32[]{:S(2)}) collective-permute-start(f32[1344,128]{1,0:T(8,128)} %get-tuple-element.21), channel_id=1, source_target_pairs={{0,2},{1,3},{2,0},{3,1},{4,6},{5,7},{6,4},{7,5},{8,10},{9,11},{10,... | collective-permute-start | bytes 2064392 | tf_op jit(solution)/shard_map/ppermute | solution.py:416
  29.6 20.9 %collective-permute-start.10 = (f32[496,128]{1,0:T(8,128)S(1)}, f32[496,128]{1,0:T(8,128)S(1)}, u32[]{:S(2)}, u32[]{:S(2)}) collective-permute-start(f32[496,128]{1,0:T(8,128)S(1)} %constant_dynamic-slice_fusion.1), channel_id=1, source_target_pairs={{0,2},{1,3},{2,0},{3,1},{4,6},{5,7},{6,4},{7,5},{8,10},{9,11},{10,... | collective-permute-start | bytes 761864 | tf_op jit(solution)/shard_map/ppermute | solution.py:416
  30.1 3.0 %collective-permute-start.5 = (f32[1,1024]{1,0:T(1,128)S(1)}, f32[1,1024]{1,0:T(1,128)S(1)}, u32[]{:S(2)}, u32[]{:S(2)}) collective-permute-start(f32[1,1024]{1,0:T(1,128)S(1)} %copy-done.6), channel_id=1, source_target_pairs={{0,8},{8,16},{16,24},{1,9},{9,17},{17,25},{2,10},{10,18},{18,26},{... | collective-permute-start | bytes 12296 | tf_op jit(solution)/shard_map/ppermute | solution.py:453
  33.1 30.0 %copy-start.3 = (f32[248,128]{1,0:T(8,128)S(1)}, f32[248,128]{1,0:T(8,128)}, u32[]{:S(2)}) copy-start(f32[248,128]{1,0:T(8,128)} %get-tuple-element.27) | copy-start | bytes 380932
  33.1 32.5 %copy-start.1 = (f32[336,128]{1,0:T(8,128)S(1)}, f32[336,128]{1,0:T(8,128)}, u32[]{:S(2)}) copy-start(f32[336,128]{1,0:T(8,128)} %get-tuple-element.22) | copy-start | bytes 516100
  33.1 0.6 copy-start.7
  35.4 41.0 %copy-start.5 = (f32[248,128]{1,0:T(8,128)S(1)}, f32[248,128]{1,0:T(8,128)}, u32[]{:S(2)}) copy-start(f32[248,128]{1,0:T(8,128)} %get-tuple-element.28) | copy-start | bytes 380932
  46.5 32.2 %copy-start.4 = (f32[336,128]{1,0:T(8,128)S(1)}, f32[336,128]{1,0:T(8,128)}, u32[]{:S(2)}) copy-start(f32[336,128]{1,0:T(8,128)} %get-tuple-element.24) | copy-start | bytes 516100
  47.7 7.3 %collective-permute-start.1 = (f32[672,128]{1,0:T(8,128)S(1)}, f32[672,128]{1,0:T(8,128)S(1)}, u32[]{:S(2)}, u32[]{:S(2)}) collective-permute-start(f32[672,128]{1,0:T(8,128)S(1)} %constant_dynamic-slice_fusion.3), channel_id=1, source_target_pairs={{0,1},{1,0},{2,3},{3,2},{4,5},{5,4},{6,7},{7,6},{8,9},{9,8},{10,11... | collective-permute-start | bytes 1032200 | tf_op jit(solution)/shard_map/ppermute | solution.py:416
  50.5 12.6 %collective-permute-start.11 = (f32[248,128]{1,0:T(8,128)S(1)}, f32[248,128]{1,0:T(8,128)S(1)}, u32[]{:S(2)}, u32[]{:S(2)}) collective-permute-start(f32[248,128]{1,0:T(8,128)S(1)} %constant_dynamic-slice_fusion), channel_id=1, source_target_pairs={{0,4},{1,5},{2,6},{3,7},{4,0},{5,1},{6,2},{7,3},{8,12},{9,13},{10,... | collective-permute-start | bytes 380936 | tf_op jit(solution)/shard_map/ppermute | solution.py:416
  55.1 53.7 %copy-start = (s32[6]{0:T(128)S(1)}, s32[6]{0:T(128)}, u32[]{:S(2)}) copy-start(s32[6]{0:T(128)} %stack.31.place_ref) | copy-start | bytes 76
  55.1 10.4 %collective-permute-start.2 = (f32[336,128]{1,0:T(8,128)S(1)}, f32[336,128]{1,0:T(8,128)S(1)}, u32[]{:S(2)}, u32[]{:S(2)}) collective-permute-start(f32[336,128]{1,0:T(8,128)S(1)} %constant_dynamic-slice_fusion.2), channel_id=1, source_target_pairs={{0,4},{1,5},{2,6},{3,7},{4,0},{5,1},{6,2},{7,3},{8,12},{9,13},{10,... | collective-permute-start | bytes 516104 | tf_op jit(solution)/shard_map/ppermute | solution.py:416
  63.1 5.4 %collective-permute-start.12 = (f32[248,128]{1,0:T(8,128)S(1)}, f32[248,128]{1,0:T(8,128)S(1)}, u32[]{:S(2)}, u32[]{:S(2)}) collective-permute-start(f32[248,128]{1,0:T(8,128)S(1)} %fusion.3), channel_id=1, source_target_pairs={{0,8},{8,16},{16,24},{1,9},{9,17},{17,25},{2,10},{10,18},{18,26},{... | collective-permute-start | bytes 380936 | tf_op jit(solution)/shard_map/ppermute | solution.py:453
  65.6 7.2 %collective-permute-start.3 = (f32[336,128]{1,0:T(8,128)S(1)}, f32[336,128]{1,0:T(8,128)S(1)}, u32[]{:S(2)}, u32[]{:S(2)}) collective-permute-start(f32[336,128]{1,0:T(8,128)S(1)} %fusion.1), channel_id=1, source_target_pairs={{0,8},{8,16},{16,24},{1,9},{9,17},{17,25},{2,10},{10,18},{18,26},{... | collective-permute-start | bytes 516104 | tf_op jit(solution)/shard_map/ppermute | solution.py:453
  68.6 7.7 %collective-permute-start.13 = (f32[248,128]{1,0:T(8,128)S(1)}, f32[248,128]{1,0:T(8,128)S(1)}, u32[]{:S(2)}, u32[]{:S(2)}) collective-permute-start(f32[248,128]{1,0:T(8,128)S(1)} %get-tuple-element.34), channel_id=1, source_target_pairs={{0,16},{8,24},{1,17},{9,25},{2,18},{10,26},{3,19},{11,27},{4,20},{... | collective-permute-start | bytes 380936 | tf_op jit(solution)/shard_map/ppermute | solution.py:453
  72.8 5.8 %collective-permute-start.4 = (f32[336,128]{1,0:T(8,128)S(1)}, f32[336,128]{1,0:T(8,128)S(1)}, u32[]{:S(2)}, u32[]{:S(2)}) collective-permute-start(f32[336,128]{1,0:T(8,128)S(1)} %get-tuple-element.36), channel_id=1, source_target_pairs={{0,16},{8,24},{1,17},{9,25},{2,18},{10,26},{3,19},{11,27},{4,20},{... | collective-permute-start | bytes 516104 | tf_op jit(solution)/shard_map/ppermute | solution.py:453
  76.4 11.8 %collective-permute-start.14 = (f32[248,128]{1,0:T(8,128)S(1)}, f32[248,128]{1,0:T(8,128)S(1)}, u32[]{:S(2)}, u32[]{:S(2)}) collective-permute-start(f32[248,128]{1,0:T(8,128)S(1)} %multiply_add_fusion.1), channel_id=1, source_target_pairs={{0,4},{1,5},{2,6},{3,7},{4,0},{5,1},{6,2},{7,3},{8,12},{9,13},{10,... | collective-permute-start | bytes 380936 | tf_op jit(solution)/shard_map/ppermute | solution.py:416
  78.7 11.3 %collective-permute-start.6 = (f32[336,128]{1,0:T(8,128)S(1)}, f32[336,128]{1,0:T(8,128)S(1)}, u32[]{:S(2)}, u32[]{:S(2)}) collective-permute-start(f32[336,128]{1,0:T(8,128)S(1)} %multiply_add_fusion), channel_id=1, source_target_pairs={{0,4},{1,5},{2,6},{3,7},{4,0},{5,1},{6,2},{7,3},{8,12},{9,13},{10,... | collective-permute-start | bytes 516104 | tf_op jit(solution)/shard_map/ppermute | solution.py:416
  88.2 6.3 %collective-permute-start.15 = (f32[496,128]{1,0:T(8,128)S(1)}, f32[496,128]{1,0:T(8,128)S(1)}, u32[]{:S(2)}, u32[]{:S(2)}) collective-permute-start(f32[496,128]{1,0:T(8,128)S(1)} %maximum_select_fusion.3), channel_id=1, source_target_pairs={{0,2},{1,3},{2,0},{3,1},{4,6},{5,7},{6,4},{7,5},{8,10},{9,11},{10,... | collective-permute-start | bytes 761864 | tf_op jit(solution)/shard_map/ppermute | solution.py:416
  90.1 11.1 %collective-permute-start.7 = (f32[672,128]{1,0:T(8,128)S(1)}, f32[672,128]{1,0:T(8,128)S(1)}, u32[]{:S(2)}, u32[]{:S(2)}) collective-permute-start(f32[672,128]{1,0:T(8,128)S(1)} %maximum_select_fusion.2), channel_id=1, source_target_pairs={{0,1},{1,0},{2,3},{3,2},{4,5},{5,4},{6,7},{7,6},{8,9},{9,8},{10,11... | collective-permute-start | bytes 1032200 | tf_op jit(solution)/shard_map/ppermute | solution.py:416
  94.6 14.2 %collective-permute-start.16 = (f32[992,128]{1,0:T(8,128)S(1)}, f32[992,128]{1,0:T(8,128)S(1)}, u32[]{:S(2)}, u32[]{:S(2)}) collective-permute-start(f32[992,128]{1,0:T(8,128)S(1)} %maximum_select_fusion.1.own_ref), channel_id=1, source_target_pairs={{0,1},{1,0},{2,3},{3,2},{4,5},{5,4},{6,7},{7,6},{8,9},{9,8},{10,11... | collective-permute-start | bytes 1523720 | tf_op jit(solution)/shard_map/ppermute | solution.py:416
  101.2 17.0 %collective-permute-start.8 = (f32[1344,128]{1,0:T(8,128)S(1)}, f32[1344,128]{1,0:T(8,128)S(1)}, u32[]{:S(2)}, u32[]{:S(2)}) collective-permute-start(f32[1344,128]{1,0:T(8,128)S(1)} %maximum_select_fusion.own_ref), channel_id=1, source_target_pairs={{0,2},{1,3},{2,0},{3,1},{4,6},{5,7},{6,4},{7,5},{8,10},{9,11},{10,... | collective-permute-start | bytes 2064392 | tf_op jit(solution)/shard_map/ppermute | solution.py:416
